TPU v7x, 32 devices: a whole 2x2x4 slice. The times are simulated.
32 devices in a mesh: dp: 8 (over y, x, core), fsdp: 4 (over z).
Axes of the slice: x: 2, y: 2, z: 4, core: 2. Of those that a mesh axis runs over, the one named last changes fastest.
Arguments:
- hidden_in: bfloat16 [32768, 768], P(('dp', 'fsdp')), may hold values from -6 to 6
- cotangent: bfloat16 [32768, 768], P(('dp', 'fsdp')), may hold values from -6 to 6
- seq_lengths: int32 [32, 4], P(('dp', 'fsdp')), may hold values from 0 to 1024, as said below
- in_weight: float32 [2, 768, 3352], P(None, ('dp', 'fsdp')), may hold values from -0.21875 to 0.21875
- out_weight: float32 [2, 1536, 768], P(None, ('dp', 'fsdp')), may hold values from -0.15625 to 0.15625
- vector_weight: float32 [2, 11264], P(None, ('dp', 'fsdp'))
- head_weight: float32 [2, 3, 24], replicated
- in_row_moment: float32 [2, 768], P(None, ('dp', 'fsdp')), may hold values from 819 to 8192
- in_col_moment: float32 [2, 3352], replicated, may hold values from 163 to 1638
- out_row_moment: float32 [2, 1536], P(None, ('dp', 'fsdp')), may hold values from 16384 to 65536
- out_col_moment: float32 [2, 768], replicated, may hold values from 16384 to 65536
- vector_moment: float32 [2, 11264], P(None, ('dp', 'fsdp')), may hold values from 16384 to 65536
- head_moment: float32 [2, 3, 24], replicated, may hold values from 163 to 1638
Outputs:
- layer_out: bfloat16 [32768, 768], P(('dp', 'fsdp'))
- input_grad: float32 [32768, 768], P(('dp', 'fsdp'))
- in_grad: float32 [2, 768, 3352], P(None, ('dp', 'fsdp'))
- out_grad: float32 [2, 1536, 768], P(None, ('dp', 'fsdp'))
- vector_grad: float32 [2, 11264], P(None, ('dp', 'fsdp'))
- head_grad: float32 [2, 3, 24], replicated
- new_in_weight: float32 [2, 768, 3352], P(None, ('dp', 'fsdp'))
- new_out_weight: float32 [2, 1536, 768], P(None, ('dp', 'fsdp'))
- new_vector_weight: float32 [2, 11264], P(None, ('dp', 'fsdp'))
- new_head_weight: float32 [2, 3, 24], replicated
- in_copy: bfloat16 [2, 768, 3352], P(None, ('dp', 'fsdp'))
- out_copy: bfloat16 [2, 1536, 768], P(None, ('dp', 'fsdp'))
- vector_copy: bfloat16 [2, 11264], P(None, ('dp', 'fsdp'))
- head_copy: bfloat16 [2, 3, 24], replicated
- new_in_row: float32 [2, 768], P(None, ('dp', 'fsdp'))
- new_in_col: float32 [2, 3352], replicated
- new_out_row: float32 [2, 1536], P(None, ('dp', 'fsdp'))
- new_out_col: float32 [2, 768], replicated
- new_vector_moment: float32 [2, 11264], P(None, ('dp', 'fsdp'))
- new_head_moment: float32 [2, 3, 24], replicated
- update_rms: float32 [2, 4], replicated
Inputs may be any that keep to these rules, and one draw needn't show every extreme that they name: `seq_lengths`: each slot lists the lengths of its 1 to 3 sequences in its first entries and zeros after them; each length is at least 256, a slot's lengths add up to more than 512 and at most 1024; positions after them are padding.
All inputs are finite; a program needn't handle non-finite values.
Results may differ from a plain program's by a relative error of at most 0.0085.
The roundings to bfloat16 on the way count: a program that leaves them out, or rounds other values in their place, can miss the bound.
Values may be sent and summed in bfloat16 or wider, within the bound.
No kernel may reach another device: no remote copies, remote signals or barrier semaphores. Data moves between devices by JAX's collectives and lax.ppermute only.
A program may use at most 384 MiB of HBM per device.

v0:
```python
from functools import partial

import jax
import jax.numpy as jnp
from jax import lax
from jax.sharding import PartitionSpec as P

D = 768
NHEADS = 24
HEADDIM = 64
STATE = 128
SPAN = 256
LAYERS = 2
INNER = 1536
CH = 1792
P_SIZE = 3352
VEC = 11264


EPSILON = 1e-05
MOMENT_DECAY = 0.5
CLIP_LIMIT = 1.0
RELATIVE_STEP = 0.5
PRECISE = lax.Precision.HIGHEST


def segment_ids(lengths, token_count):
    ends_at = jnp.cumsum(lengths)
    position = jnp.arange(token_count, dtype=jnp.int32)
    segments = jnp.sum((position[:, None] >= ends_at[None, :]).astype(jnp.int32), axis=1)
    valid_mask = (position < ends_at[-1]).astype(jnp.float32)
    return (segments, valid_mask)


def rms_norm(values, scales):
    return values * lax.rsqrt(jnp.mean(values * values, axis=-1, keepdims=True) + EPSILON) * scales


def norm_part(stream, vector_w):
    return rms_norm(stream, vector_w[:D][None, :])


def causal_conv(inputs, segments, kernel, offset):
    channels = inputs.shape[1]
    result = offset[None, :] + kernel[3][None, :] * inputs
    for lag_rows in range(1, 4):
        earlier = jnp.concatenate(
            [jnp.zeros((lag_rows, channels), jnp.float32), inputs[:-lag_rows]], axis=0
        )
        earlier_seg = jnp.concatenate(
            [jnp.full((lag_rows,), -1, jnp.int32), segments[:-lag_rows]], axis=0
        )
        result = result + kernel[3 - lag_rows][None, :] * jnp.where(
            (earlier_seg == segments)[:, None], earlier, 0.0
        )
    return result


def span_terms(block_items):
    span_x, span_b, span_c, cumlog, span_dt, span_seg = block_items
    places = jnp.arange(span_seg.shape[0])
    allowed = (span_seg[:, None] == span_seg[None, :]) & (places[:, None] >= places[None, :])
    intersections = jnp.dot(span_c, span_b.T, precision=PRECISE)
    head_cum = cumlog.T
    log_gaps = jnp.where(allowed[None], head_cum[:, :, None] - head_cum[:, None, :], 0.0)
    mixing = (
        jnp.where(allowed[None], jnp.exp(log_gaps), 0.0)
        * intersections[None]
        * span_dt.T[:, None, :]
    )
    within = jnp.einsum("hij,jhp->ihp", mixing, span_x, precision=PRECISE)
    to_end = (
        jnp.where((span_seg == span_seg[-1])[:, None], jnp.exp(cumlog[-1][None, :] - cumlog), 0.0)
        * span_dt
    )
    local_state = jnp.einsum("js,jhp->hsp", span_b, span_x * to_end[:, :, None], precision=PRECISE)
    return (within, local_state)


def state_space(inputs_x, inputs_b, inputs_c, log_rate, steps_dt, segments):
    token_count, head_count, head_dim = inputs_x.shape
    blocks = token_count // SPAN
    span_x = inputs_x.reshape(blocks, SPAN, head_count, head_dim)
    span_b = inputs_b.reshape(blocks, SPAN, STATE)
    span_c = inputs_c.reshape(blocks, SPAN, STATE)
    span_rate = log_rate.reshape(blocks, SPAN, head_count)
    span_dt = steps_dt.reshape(blocks, SPAN, head_count)
    span_seg = segments.reshape(blocks, SPAN)
    cumlog = jnp.cumsum(span_rate, axis=1)
    within, local_state = lax.map(
        jax.checkpoint(span_terms), (span_x, span_b, span_c, cumlog, span_dt, span_seg)
    )
    last_seg = span_seg[:, -1]
    prior_seg = jnp.concatenate([jnp.full((1,), -1, jnp.int32), last_seg[:-1]], axis=0)
    linked = last_seg == prior_seg

    def advance(state_in, step_items):
        local_one, cum_last, link_one = step_items
        carried = jnp.where(link_one, jnp.exp(cum_last), 0.0)[:, None, None] * state_in
        return (carried + local_one, state_in)

    start_state = jnp.zeros((head_count, STATE, head_dim), jnp.float32)
    final_state, entering = lax.scan(advance, start_state, (local_state, cumlog[:, -1, :], linked))
    inflow = jnp.einsum("cis,chsp->cihp", span_c, entering, precision=PRECISE)
    reach_in = jnp.where((span_seg == prior_seg[:, None])[:, :, None], jnp.exp(cumlog), 0.0)
    result = within + inflow * reach_in[..., None]
    return result.reshape(token_count, head_count, head_dim)


def mixer(in_proj, vector_w, head_w, segments):
    token_count = in_proj.shape[0]
    gate_in = in_proj[:, :INNER]
    conv_in = in_proj[:, INNER : INNER + CH]
    rate_in = in_proj[:, INNER + CH :]
    kernel = vector_w[D + INNER : D + INNER + 4 * CH].reshape(4, CH)
    offset = vector_w[D + INNER + 4 * CH :]
    mixed_out = jax.nn.silu(causal_conv(conv_in, segments, kernel, offset))
    inputs_x = mixed_out[:, :INNER].reshape(token_count, NHEADS, HEADDIM)
    inputs_b = mixed_out[:, INNER : INNER + STATE]
    inputs_c = mixed_out[:, INNER + STATE :]
    steps_dt = jax.nn.softplus(rate_in + head_w[0][None, :])
    log_rate = -jnp.exp(head_w[1])[None, :] * steps_dt
    output = (
        state_space(inputs_x, inputs_b, inputs_c, log_rate, steps_dt, segments)
        + head_w[2][None, :, None] * inputs_x
    )
    gated_out = output.reshape(token_count, INNER) * jax.nn.silu(gate_in)
    return rms_norm(gated_out, vector_w[D : D + INNER][None, :])


def column_factors(
    grad_in, grad_out, row_in, row_out, column_in, column_out, totals, in_col_moment, out_col_moment
):
    col_in_new = MOMENT_DECAY * in_col_moment + (1.0 - MOMENT_DECAY) * column_in / D
    col_out_new = MOMENT_DECAY * out_col_moment + (1.0 - MOMENT_DECAY) * column_out / INNER
    mean_in = totals[:, 0] / D
    mean_out = totals[:, 1] / INNER
    update_in = grad_in * lax.rsqrt(
        row_in[:, :, None] * col_in_new[:, None, :] / mean_in[:, None, None]
    )
    update_out = grad_out * lax.rsqrt(
        row_out[:, :, None] * col_out_new[:, None, :] / mean_out[:, None, None]
    )
    return (col_in_new, col_out_new, mean_in, mean_out, update_in, update_out)


def on_device(
    hidden_in,
    cotangent,
    seq_lengths,
    in_weight,
    out_weight,
    vector_weight,
    head_weight,
    in_row_moment,
    in_col_moment,
    out_row_moment,
    out_col_moment,
    vector_moment,
    head_moment,
):
    token_count = hidden_in.shape[0]
    segments, valid_mask = segment_ids(seq_lengths[0], token_count)
    stream = hidden_in.astype(jnp.float32)
    stored = []
    for layer_idx in range(LAYERS):
        shards = (
            in_weight[layer_idx].astype(jnp.bfloat16),
            out_weight[layer_idx].astype(jnp.bfloat16),
            vector_weight[layer_idx].astype(jnp.bfloat16),
        )
        full_in, full_out, full_vector = (
            lax.all_gather(shards[0], ("dp", "fsdp"), axis=0, tiled=True),
            lax.all_gather(shards[1], ("dp", "fsdp"), axis=0, tiled=True),
            lax.all_gather(shards[2], ("dp", "fsdp"), axis=0, tiled=True),
        )
        vector_full = full_vector.astype(jnp.float32)
        normed, norm_pull = jax.vjp(norm_part, stream, vector_full)
        normed_low = normed.astype(jnp.bfloat16)
        in_proj = jnp.dot(normed_low, full_in, preferred_element_type=jnp.float32)
        mixed_out, mixer_pull = jax.vjp(
            jax.checkpoint(partial(mixer, segments=segments)),
            in_proj,
            vector_full,
            head_weight[layer_idx],
        )
        mixed_low = mixed_out.astype(jnp.bfloat16)
        stream = stream + jnp.dot(mixed_low, full_out, preferred_element_type=jnp.float32)
        stored.append((norm_pull, mixer_pull, normed_low, mixed_low, full_in, full_out))
    layer_out = stream.astype(jnp.bfloat16)
    flowing = cotangent.astype(jnp.float32) * valid_mask[:, None]
    in_parts = [None] * LAYERS
    out_parts = [None] * LAYERS
    vector_parts = [None] * LAYERS
    head_parts = [None] * LAYERS
    for layer_idx in reversed(range(LAYERS)):
        norm_pull, mixer_pull, normed_low, mixed_low, full_in, full_out = stored[layer_idx]
        full_in, full_out = (
            lax.all_gather(
                in_weight[layer_idx].astype(jnp.bfloat16), ("dp", "fsdp"), axis=0, tiled=True
            ),
            lax.all_gather(
                out_weight[layer_idx].astype(jnp.bfloat16), ("dp", "fsdp"), axis=0, tiled=True
            ),
        )
        flowing_low = flowing.astype(jnp.bfloat16)
        grad_out = jnp.einsum(
            "te,td->ed", mixed_low, flowing_low, preferred_element_type=jnp.float32
        )
        grad_mixed = jnp.einsum(
            "td,ed->te", flowing_low, full_out, preferred_element_type=jnp.float32
        )
        grad_proj, grad_vec_mix, grad_head = mixer_pull(grad_mixed)
        proj_low = grad_proj.astype(jnp.bfloat16)
        grad_in = jnp.einsum("td,tp->dp", normed_low, proj_low, preferred_element_type=jnp.float32)
        grad_normed = jnp.einsum("tp,dp->td", proj_low, full_in, preferred_element_type=jnp.float32)
        grad_stream, grad_vec_norm = norm_pull(grad_normed)
        flowing = flowing + grad_stream
        grad_vec_all = grad_vec_mix + grad_vec_norm
        share_in, share_out, share_vector = (
            lax.psum_scatter(grad_in, ("dp", "fsdp"), scatter_dimension=0, tiled=True),
            lax.psum_scatter(grad_out, ("dp", "fsdp"), scatter_dimension=0, tiled=True),
            lax.psum_scatter(grad_vec_all, ("dp", "fsdp"), scatter_dimension=0, tiled=True),
        )
        in_parts[layer_idx] = share_in
        out_parts[layer_idx] = share_out
        vector_parts[layer_idx] = share_vector
        head_parts[layer_idx] = grad_head
    grad_in = jnp.stack(in_parts)
    grad_out = jnp.stack(out_parts)
    grad_vector = jnp.stack(vector_parts)
    head_part = jnp.stack(head_parts)
    squares_in = grad_in * grad_in
    squares_out = grad_out * grad_out
    row_in = MOMENT_DECAY * in_row_moment + (1.0 - MOMENT_DECAY) * jnp.mean(squares_in, axis=2)
    row_out = MOMENT_DECAY * out_row_moment + (1.0 - MOMENT_DECAY) * jnp.mean(squares_out, axis=2)
    vector_new = MOMENT_DECAY * vector_moment + (1.0 - MOMENT_DECAY) * grad_vector * grad_vector
    vector_update = grad_vector * lax.rsqrt(vector_new)
    totals = jnp.stack(
        [
            jnp.sum(row_in, axis=1),
            jnp.sum(row_out, axis=1),
            jnp.sum(in_weight * in_weight, axis=(1, 2)),
            jnp.sum(out_weight * out_weight, axis=(1, 2)),
            jnp.sum(vector_weight * vector_weight, axis=1),
            jnp.sum(vector_update * vector_update, axis=1),
        ],
        axis=1,
    )
    column_in = jnp.sum(squares_in, axis=1)
    column_out = jnp.sum(squares_out, axis=1)
    column_in, column_out, head_total, totals = lax.psum(
        (column_in, column_out, head_part, totals), ("dp", "fsdp")
    )
    col_in_new, col_out_new, mean_in, mean_out, update_in, update_out = column_factors(
        grad_in,
        grad_out,
        row_in,
        row_out,
        column_in,
        column_out,
        totals,
        in_col_moment,
        out_col_moment,
    )
    update_squares = lax.psum(
        jnp.stack(
            [
                jnp.sum(update_in * update_in, axis=(1, 2)),
                jnp.sum(update_out * update_out, axis=(1, 2)),
            ],
            axis=1,
        ),
        ("dp", "fsdp"),
    )
    norm_in = jnp.sqrt(update_squares[:, 0] / (D * P_SIZE))
    norm_out = jnp.sqrt(update_squares[:, 1] / (INNER * D))
    step_in = (
        RELATIVE_STEP
        * jnp.sqrt(totals[:, 2] / (D * P_SIZE))
        / jnp.maximum(1.0, norm_in / CLIP_LIMIT)
    )
    step_out = (
        RELATIVE_STEP
        * jnp.sqrt(totals[:, 3] / (INNER * D))
        / jnp.maximum(1.0, norm_out / CLIP_LIMIT)
    )
    new_in = in_weight - step_in[:, None, None] * update_in
    new_out = out_weight - step_out[:, None, None] * update_out
    norm_vector = jnp.sqrt(totals[:, 5] / VEC)
    step_vector = (
        RELATIVE_STEP * jnp.sqrt(totals[:, 4] / VEC) / jnp.maximum(1.0, norm_vector / CLIP_LIMIT)
    )
    new_vector = vector_weight - step_vector[:, None] * vector_update
    head_new = MOMENT_DECAY * head_moment + (1.0 - MOMENT_DECAY) * head_total * head_total
    head_update = head_total * lax.rsqrt(head_new)
    norm_head = jnp.sqrt(jnp.mean(head_update * head_update, axis=(1, 2)))
    step_head = (
        RELATIVE_STEP
        * jnp.sqrt(jnp.mean(head_weight * head_weight, axis=(1, 2)))
        / jnp.maximum(1.0, norm_head / CLIP_LIMIT)
    )
    new_head = head_weight - step_head[:, None, None] * head_update
    update_rms = jnp.stack([norm_in, norm_out, norm_vector, norm_head], axis=1)
    return (
        layer_out,
        flowing,
        grad_in,
        grad_out,
        grad_vector,
        head_total,
        new_in,
        new_out,
        new_vector,
        new_head,
        new_in.astype(jnp.bfloat16),
        new_out.astype(jnp.bfloat16),
        new_vector.astype(jnp.bfloat16),
        new_head.astype(jnp.bfloat16),
        row_in,
        col_in_new,
        row_out,
        col_out_new,
        vector_new,
        head_new,
        update_rms,
    )


def solution(mesh):
    placed = (
        P(("dp", "fsdp"), None),
        P(("dp", "fsdp"), None),
        P(("dp", "fsdp"), None),
        P(None, ("dp", "fsdp"), None),
        P(None, ("dp", "fsdp"), None),
        P(None, ("dp", "fsdp")),
        P(),
        P(None, ("dp", "fsdp")),
        P(),
        P(None, ("dp", "fsdp")),
        P(),
        P(None, ("dp", "fsdp")),
        P(),
    )
    return jax.shard_map(
        on_device,
        mesh=mesh,
        in_specs=placed,
        out_specs=(
            P(("dp", "fsdp"), None),
            P(("dp", "fsdp"), None),
            P(None, ("dp", "fsdp"), None),
            P(None, ("dp", "fsdp"), None),
            P(None, ("dp", "fsdp")),
            P(),
            P(None, ("dp", "fsdp"), None),
            P(None, ("dp", "fsdp"), None),
            P(None, ("dp", "fsdp")),
            P(),
            P(None, ("dp", "fsdp"), None),
            P(None, ("dp", "fsdp"), None),
            P(None, ("dp", "fsdp")),
            P(),
            P(None, ("dp", "fsdp")),
            P(),
            P(None, ("dp", "fsdp")),
            P(),
            P(None, ("dp", "fsdp")),
            P(),
            P(),
        ),
        check_vma=False,
    )
```

profile of v0, /device:TPU:0, one launch (start us, length us, event | category | flops | bytes accessed | tf_op | source)
XLA Modules:
  0.0 2651.8 jit_solution(7313634433158586218)
XLA Ops:
  15.9 43.0 %all-reduce.71 = (bf16[11264]{0:T(1024)(128)(2,1)S(1)}, bf16[11264]{0:T(1024)(128)(2,1)S(1)}) all-reduce(bf16[11264]{0:T(1024)(128)(2,1)S(1)} %dynamic-update-slice, bf16[11264]{0:T(1024)(128)(2,1)S(1)} %dynamic-update-slice.1), channel_id=2, replica_groups=mesh['dp'=8,'fsdp'=4] {'dp','fsdp'}, use_global_device_ids=true, to_apply=%add.62 | all-reduce | flops 22528 | bytes 90112
  79.7 59.7 %all-gather.11.cloned.1.call-done = bf16[1,768,3352]{2,1,0:T(8,128)(2,1)} async-done(((bf16[1,24,3352]{2,1,0:T(8,128)(2,1)}), bf16[1,768,3352]{2,1,0:T(8,128)(2,1)}) %all-gather.11.cloned.1.call-update) | async-done | bytes 5148688 | tf_op jit(solution)/shard_map/all_gather | solution.py:173
  196.9 77.2 %while.204 = (s32[]{:T(128)}, f32[4,256,24,64]{1,3,2,0:T(8,128)}, f32[4,24,128,64]{2,3,1,0:T(8,128)}, f32[4,256,24,64]{1,0,3,2:T(4,128)}, f32[4,256,128]{2,1,0:T...) while((s32[]{:T(128)}, f32[4,256,24,64]{1,3,2,0:T(8,128)}, ...), condition=%wide.region_6.7_spmd, body=%wide.region_5.6_spmd.sunk | while | flops 1921075456 | bytes 13841333 | solution.py:90
  277.9 29.8 %while.210 = (s32[]{:T(128)}, f32[24,128,64]{2,1,0:T(8,128)}, f32[4,24,128,64]{2,3,1,0:T(8,128)}, pred[4]{0:T(512)(128)(4,1)}, f32[4,24]{1,0:T(4,128)S(1)}, /*in...) while((s32[]{:T(128)}, f32[24,128,64]{2,1,0:T(8,128)}, f32[4,24,128,64]{2,3,1,0:T(8,128)}, ...), condition=%wide.region_8.9_spmd.clone, body=%wide.region_7.8_spmd.clone.sunk | while | flops 589851 | bytes 9437594 | solution.py:103
  455.2 64.9 %while.208 = (s32[]{:T(128)}, f32[4,256,24,64]{1,3,2,0:T(8,128)}, f32[4,24,128,64]{2,3,1,0:T(8,128)}, f32[4,256,24,64]{1,3,2,0:T(8,128)}, s32[4,256]{1,0:T(4,128...) while((s32[]{:T(128)}, f32[4,256,24,64]{1,3,2,0:T(8,128)}, ...), condition=%wide.region_21.23_spmd.clone, body=%wide.region_20.22_spmd.clone.sunk | while | flops 1921075456 | bytes 6832781 | solution.py:90
  523.6 28.8 %while.212 = (s32[]{:T(128)}, f32[24,128,64]{2,1,0:T(8,128)S(1)}, f32[4,24,128,64]{3,2,1,0:T(8,128)}, f32[4,24]{1,0:T(4,128)S(1)}, f32[4,24,1,1]{1,3,2,0:T(1,128...) while((s32[]{:T(128)}, f32[24,128,64]{2,1,0:T(8,128)S(1)}, ...), condition=%wide.region_23.25_spmd.clone, body=%wide.region_22.24_spmd.clone.sunk | while | flops 786483 | bytes 7866480 | solution.py:103
  647.8 36.4 %while.213 = (s32[]{:T(128)}, f32[24,128,64]{2,1,0:T(8,128)}, f32[4,24,128,64]{2,3,1,0:T(8,128)}, f32[4,24]{1,0:T(4,128)S(1)}, f32[4,24,128,64]{2,3,1,0:T(8,128)...) while((s32[]{:T(128)}, f32[24,128,64]{2,1,0:T(8,128)}, ...), condition=%wide.region_28.30_spmd.clone, body=%wide.region_26.29_spmd.clone.sunk | while | flops 983068 | bytes 10224658 | solution.py:103
  691.2 275.0 %while.206 = (s32[]{:T(128)}, f32[4,256,24,64]{1,0,3,2:T(4,128)}, f32[4,256,128]{2,1,0:T(8,128)}, f32[4,256,128]{2,1,0:T(8,128)}, f32[4,256,24]{1,2,0:T(8,128)},...) while((s32[]{:T(128)}, f32[4,256,24,64]{1,0,3,2:T(4,128)}, ...), condition=%wide.region_36.38_spmd, body=%wide.region_29.37_spmd.sunk | while | flops 3959517440 | bytes 32503172 | solution.py:90
  718.2 34.7 %dynamic_update_slice.293 = f32[4,256,24,64]{1,0,3,2:T(4,128)} dynamic-update-slice(f32[4,256,24,64]{1,0,3,2:T(4,128)} %get-tuple-element.4155, f32[1,256,24,64]{1,0,3,2:T(1,128)} %copy.1192, s32[]{:T(128)S(6)} %sub.628, s32[]{:T(128)} %constant.478.clone.1..sunk, s32[]{:T(128)} %constant.478.clone.1..sunk, s32[]{:T(128)} %constant.478.clone.1..sunk) | dynamic-update-slice | bytes 3145732 | tf_op jit(solution)/shard_map/transpose(jvp(jvp()))/checkpoint/while/body/jit(dynamic_update_index_in_dim)/dynamic_update_slice | solution.py:90
  786.8 34.7 %dynamic_update_slice.293 = f32[4,256,24,64]{1,0,3,2:T(4,128)} dynamic-update-slice(f32[4,256,24,64]{1,0,3,2:T(4,128)} %get-tuple-element.4155, f32[1,256,24,64]{1,0,3,2:T(1,128)} %copy.1192, s32[]{:T(128)S(6)} %sub.628, s32[]{:T(128)} %constant.478.clone.1..sunk, s32[]{:T(128)} %constant.478.clone.1..sunk, s32[]{:T(128)} %constant.478.clone.1..sunk) | dynamic-update-slice | bytes 3145732 | tf_op jit(solution)/shard_map/transpose(jvp(jvp()))/checkpoint/while/body/jit(dynamic_update_index_in_dim)/dynamic_update_slice | solution.py:90
  855.4 34.7 %dynamic_update_slice.293 = f32[4,256,24,64]{1,0,3,2:T(4,128)} dynamic-update-slice(f32[4,256,24,64]{1,0,3,2:T(4,128)} %get-tuple-element.4155, f32[1,256,24,64]{1,0,3,2:T(1,128)} %copy.1192, s32[]{:T(128)S(6)} %sub.628, s32[]{:T(128)} %constant.478.clone.1..sunk, s32[]{:T(128)} %constant.478.clone.1..sunk, s32[]{:T(128)} %constant.478.clone.1..sunk) | dynamic-update-slice | bytes 3145732 | tf_op jit(solution)/shard_map/transpose(jvp(jvp()))/checkpoint/while/body/jit(dynamic_update_index_in_dim)/dynamic_update_slice | solution.py:90
  924.0 34.7 %dynamic_update_slice.293 = f32[4,256,24,64]{1,0,3,2:T(4,128)} dynamic-update-slice(f32[4,256,24,64]{1,0,3,2:T(4,128)} %get-tuple-element.4155, f32[1,256,24,64]{1,0,3,2:T(1,128)} %copy.1192, s32[]{:T(128)S(6)} %sub.628, s32[]{:T(128)} %constant.478.clone.1..sunk, s32[]{:T(128)} %constant.478.clone.1..sunk, s32[]{:T(128)} %constant.478.clone.1..sunk) | dynamic-update-slice | bytes 3145732 | tf_op jit(solution)/shard_map/transpose(jvp(jvp()))/checkpoint/while/body/jit(dynamic_update_index_in_dim)/dynamic_update_slice | solution.py:90
  977.4 22.5 fusion.323
  1000.2 19.9 fusion.377
  1140.1 77.0 %while.205 = (s32[]{:T(128)}, f32[4,256,24,64]{1,3,2,0:T(8,128)}, f32[4,24,128,64]{2,3,1,0:T(8,128)}, f32[4,256,24,64]{1,0,3,2:T(4,128)}, f32[4,256,128]{2,1,0:T...) while((s32[]{:T(128)}, f32[4,256,24,64]{1,3,2,0:T(8,128)}, ...), condition=%wide.region_14.15_spmd, body=%wide.region_13.14_spmd.sunk | while | flops 1921075456 | bytes 13841333 | solution.py:90
  1219.2 29.8 %while.211 = (s32[]{:T(128)}, f32[24,128,64]{2,1,0:T(8,128)}, f32[4,24,128,64]{2,3,1,0:T(8,128)}, pred[4]{0:T(512)(128)(4,1)}, f32[4,24]{1,0:T(4,128)S(1)}, /*in...) while((s32[]{:T(128)}, f32[24,128,64]{2,1,0:T(8,128)}, f32[4,24,128,64]{2,3,1,0:T(8,128)}, ...), condition=%wide.region_16.17_spmd.clone, body=%wide.region_15.16_spmd.clone.sunk | while | flops 589851 | bytes 9437594 | solution.py:103
  1302.7 64.9 %while.209 = (s32[]{:T(128)}, f32[4,256,24,64]{1,3,2,0:T(8,128)}, f32[4,24,128,64]{2,3,1,0:T(8,128)}, f32[4,256,24,64]{1,3,2,0:T(8,128)}, s32[4,256]{1,0:T(4,128...) while((s32[]{:T(128)}, f32[4,256,24,64]{1,3,2,0:T(8,128)}, ...), condition=%wide.region_44.46_spmd.clone, body=%wide.region_43.45_spmd.clone.sunk | while | flops 1921075456 | bytes 6832781 | solution.py:90
  1371.2 28.8 %while.214 = (s32[]{:T(128)}, f32[24,128,64]{2,1,0:T(8,128)S(1)}, f32[4,24,128,64]{3,2,1,0:T(8,128)}, f32[4,24]{1,0:T(4,128)S(1)}, f32[4,24,1,1]{1,3,2,0:T(1,128...) while((s32[]{:T(128)}, f32[24,128,64]{2,1,0:T(8,128)S(1)}, ...), condition=%wide.region_46.48_spmd.clone, body=%wide.region_45.47_spmd.clone.sunk | while | flops 786483 | bytes 7866480 | solution.py:103
  1495.3 31.1 %while.215 = (s32[]{:T(128)}, f32[24,128,64]{2,1,0:T(8,128)}, f32[4,24,128,64]{2,3,1,0:T(8,128)}, f32[4,24]{1,0:T(4,128)S(1)}, f32[4,24,128,64]{2,3,1,0:T(8,128)...) while((s32[]{:T(128)}, f32[24,128,64]{2,1,0:T(8,128)}, ...), condition=%wide.region_51.53_spmd.clone, body=%wide.region_49.52_spmd.clone.sunk | while | flops 983068 | bytes 10224658 | solution.py:103
  1533.5 274.9 %while.207 = (s32[]{:T(128)}, f32[4,256,24,64]{1,0,3,2:T(4,128)}, f32[4,256,128]{2,1,0:T(8,128)}, f32[4,256,128]{2,1,0:T(8,128)}, f32[4,256,24]{1,2,0:T(8,128)},...) while((s32[]{:T(128)}, f32[4,256,24,64]{1,0,3,2:T(4,128)}, ...), condition=%wide.region_59.61_spmd, body=%wide.region_52.60_spmd.sunk | while | flops 3959517440 | bytes 32503172 | solution.py:90
  1560.2 34.7 %dynamic_update_slice.298 = f32[4,256,24,64]{1,0,3,2:T(4,128)} dynamic-update-slice(f32[4,256,24,64]{1,0,3,2:T(4,128)} %get-tuple-element.4308, f32[1,256,24,64]{1,0,3,2:T(1,128)} %copy.1195, s32[]{:T(128)S(6)} %sub.635, s32[]{:T(128)} %constant.478.clone.1..sunk.1, s32[]{:T(128)} %constant.478.clone.1..sunk.1, s32[]{:T(128)} %constant.478.clone.1..sunk.1) | dynamic-update-slice | bytes 3145732 | tf_op jit(solution)/shard_map/transpose(jvp(jvp()))/checkpoint/while/body/jit(dynamic_update_index_in_dim)/dynamic_update_slice | solution.py:90
  1628.8 34.7 %dynamic_update_slice.298 = f32[4,256,24,64]{1,0,3,2:T(4,128)} dynamic-update-slice(f32[4,256,24,64]{1,0,3,2:T(4,128)} %get-tuple-element.4308, f32[1,256,24,64]{1,0,3,2:T(1,128)} %copy.1195, s32[]{:T(128)S(6)} %sub.635, s32[]{:T(128)} %constant.478.clone.1..sunk.1, s32[]{:T(128)} %constant.478.clone.1..sunk.1, s32[]{:T(128)} %constant.478.clone.1..sunk.1) | dynamic-update-slice | bytes 3145732 | tf_op jit(solution)/shard_map/transpose(jvp(jvp()))/checkpoint/while/body/jit(dynamic_update_index_in_dim)/dynamic_update_slice | solution.py:90
  1697.4 34.7 %dynamic_update_slice.298 = f32[4,256,24,64]{1,0,3,2:T(4,128)} dynamic-update-slice(f32[4,256,24,64]{1,0,3,2:T(4,128)} %get-tuple-element.4308, f32[1,256,24,64]{1,0,3,2:T(1,128)} %copy.1195, s32[]{:T(128)S(6)} %sub.635, s32[]{:T(128)} %constant.478.clone.1..sunk.1, s32[]{:T(128)} %constant.478.clone.1..sunk.1, s32[]{:T(128)} %constant.478.clone.1..sunk.1) | dynamic-update-slice | bytes 3145732 | tf_op jit(solution)/shard_map/transpose(jvp(jvp()))/checkpoint/while/body/jit(dynamic_update_index_in_dim)/dynamic_update_slice | solution.py:90
  1766.0 34.7 %dynamic_update_slice.298 = f32[4,256,24,64]{1,0,3,2:T(4,128)} dynamic-update-slice(f32[4,256,24,64]{1,0,3,2:T(4,128)} %get-tuple-element.4308, f32[1,256,24,64]{1,0,3,2:T(1,128)} %copy.1195, s32[]{:T(128)S(6)} %sub.635, s32[]{:T(128)} %constant.478.clone.1..sunk.1, s32[]{:T(128)} %constant.478.clone.1..sunk.1, s32[]{:T(128)} %constant.478.clone.1..sunk.1) | dynamic-update-slice | bytes 3145732 | tf_op jit(solution)/shard_map/transpose(jvp(jvp()))/checkpoint/while/body/jit(dynamic_update_index_in_dim)/dynamic_update_slice | solution.py:90
  1819.5 22.5 fusion.320
  1985.3 51.3 %all-reduce.74.cloned.1.call-done = (f32[11264]{0:T(1024)}, f32[11264]{0:T(1024)}) async-done(((f32[11264]{0:T(1024)}, f32[11264]{0:T(1024)}), (f32[11264]{0:T(1024)}, f32[11264]{0:T(1024)})) %all-reduce.74.cloned.1.call-update) | async-done | bytes 90128
  2038.4 112.2 %reduce-scatter.11.cloned.1.call-done = f32[48,768]{1,0:T(8,128)} async-done(((f32[1536,768]{1,0:T(8,128)}), f32[48,768]{1,0:T(8,128)}) %reduce-scatter.11.cloned.1.call-update) | async-done | bytes 147472 | tf_op jit(solution)/shard_map/reduce_scatter | solution.py:222
  2150.5 112.4 %reduce-scatter.9.cloned.1.call-done = f32[48,768]{1,0:T(8,128)} async-done(((f32[1536,768]{1,0:T(8,128)}), f32[48,768]{1,0:T(8,128)}) %reduce-scatter.9.cloned.1.call-update) | async-done | bytes 147472 | tf_op jit(solution)/shard_map/reduce_scatter | solution.py:222
  2264.2 145.7 %reduce-scatter.15.cloned.1.call-done = f32[24,3352]{1,0:T(8,128)} async-done(((f32[768,3352]{1,0:T(8,128)}), f32[24,3352]{1,0:T(8,128)}) %reduce-scatter.15.cloned.1.call-update) | async-done | bytes 321808
  2409.9 146.9 %reduce-scatter.13.cloned.1.call-done = f32[24,3352]{1,0:T(8,128)} async-done(((f32[768,3352]{1,0:T(8,128)}), f32[24,3352]{1,0:T(8,128)}) %reduce-scatter.13.cloned.1.call-update) | async-done | bytes 321808
  2558.3 40.6 %all-reduce.69 = (f32[2,6]{0,1:T(8,128)S(1)}, f32[2,768]{1,0:T(2,128)S(1)}, f32[2,3352]{1,0:T(2,128)S(1)}) all-reduce(f32[2,6]{0,1:T(8,128)S(1)} %stack.91, f32[2,768]{1,0:T(2,128)S(1)} %get-tuple-element.2677, f32[2,3352]{1,0:T(2,128)S(1)} %get-tuple-element.2675), channel_id=1, replica_groups=mesh['dp'=8,'fsdp'=4] {'dp','fsdp'}, use_global_device_ids=true, to_apply=%region_101.103 | all-reduce | flops 8252 | bytes 66016 | tf_op jit(solution)/shard_map/psum | solution.py:252
  2599.5 39.5 %all-reduce.68 = (f32[2,3,24]{2,1,0:T(4,128)S(1)}, f32[2,2]{0,1:T(2,128)S(1)}) all-reduce(f32[2,3,24]{2,1,0:T(4,128)S(1)} %pad_maximum_fusion.2, f32[2,2]{0,1:T(2,128)S(1)} %pad_maximum_fusion.5), channel_id=1, replica_groups=mesh['dp'=8,'fsdp'=4] {'dp','fsdp'}, use_global_device_ids=true, to_apply=%region_92.94 | all-reduce | flops 148 | bytes 1184 | tf_op jit(solution)/shard_map/psum | solution.py:252
  (1405 shorter events, 1537.3 us)
Async XLA Ops:
  7.2 65.8 %all-gather.17.cloned.1.call-start = ((), (), s32[]{:S(2)}) async-start(), calls=%async_computation.9 | async-start | bytes 2433024 | tf_op jit(solution)/shard_map/all_gather | solution.py:174
  9.7 129.7 %all-gather.11.cloned.1.call-start = ((), (), s32[]{:S(2)}) async-start(), calls=%async_computation.6 | async-start | bytes 5474304 | tf_op jit(solution)/shard_map/all_gather | solution.py:173
  12.5 321.4 %all-gather.13.cloned.1.call-start = ((), (), s32[]{:S(2)}) async-start(), calls=%async_computation.7 | async-start | bytes 2433024 | tf_op jit(solution)/shard_map/all_gather | solution.py:174
  13.2 328.9 %all-gather.15.cloned.1.call-start = ((), (), s32[]{:S(2)}) async-start(), calls=%async_computation.8 | async-start | bytes 5474304 | tf_op jit(solution)/shard_map/all_gather | solution.py:173
  13.8 2022.8 %all-reduce.74.cloned.1.call-start = ((), (), s32[]{:S(2)}) async-start(), calls=%async_computation.12 | async-start | bytes 180224
  61.0 281.2 %copy-start.127 = (f32[768]{0:T(1024)}, f32[768]{0:T(1024)S(1)}, u32[]{:S(2)}) copy-start(f32[768]{0:T(1024)S(1)} %slice_reduce_fusion.18) | copy-start | bytes 9220
  73.0 88.2 %copy-start.145 = (pred[1024]{0:T(1024)(128)(4,1)}, pred[1024]{0:T(1024)(128)(4,1)S(1)}, u32[]{:S(2)}) copy-start(pred[1024]{0:T(1024)(128)(4,1)S(1)} %get-tuple-element.3062) | copy-start | bytes 3076
  73.0 88.2 %copy-start.147 = (pred[1024]{0:T(1024)(128)(4,1)}, pred[1024]{0:T(1024)(128)(4,1)S(1)}, u32[]{:S(2)}) copy-start(pred[1024]{0:T(1024)(128)(4,1)S(1)} %get-tuple-element.3063) | copy-start | bytes 3076
  73.0 88.2 %copy-start.149 = (pred[1024]{0:T(1024)(128)(4,1)}, pred[1024]{0:T(1024)(128)(4,1)S(1)}, u32[]{:S(2)}) copy-start(pred[1024]{0:T(1024)(128)(4,1)S(1)} %get-tuple-element.3064) | copy-start | bytes 3076
  446.9 120.1 %copy-start.37 = (f32[4,24,2,128]{3,1,2,0:T(8,128)}, f32[4,24,2,128]{3,1,2,0:T(8,128)S(1)}, u32[]{:S(2)}) copy-start(f32[4,24,2,128]{3,1,2,0:T(8,128)S(1)} %reduce-window.51) | copy-start | bytes 294916
  447.1 119.8 %copy-start.91 = (f32[4,24,2]{1,2,0:T(2,128)}, f32[4,24,2]{1,2,0:T(2,128)S(1)}, u32[]{:S(2)}) copy-start(f32[4,24,2]{1,2,0:T(2,128)S(1)} %copy.789) | copy-start | bytes 2308
  1294.5 119.7 %copy-start.35 = (f32[4,24,2,128]{3,1,2,0:T(8,128)}, f32[4,24,2,128]{3,1,2,0:T(8,128)S(1)}, u32[]{:S(2)}) copy-start(f32[4,24,2,128]{3,1,2,0:T(8,128)S(1)} %reduce-window.59) | copy-start | bytes 294916
  1294.8 119.5 %copy-start.89 = (f32[4,24,2]{1,2,0:T(2,128)}, f32[4,24,2]{1,2,0:T(2,128)S(1)}, u32[]{:S(2)}) copy-start(f32[4,24,2]{1,2,0:T(2,128)S(1)} %copy.827) | copy-start | bytes 2308
  1917.3 233.2 %reduce-scatter.11.cloned.1.call-start = ((), (), s32[]{:S(2)}) async-start(), calls=%async_computation.5 | async-start | bytes 4866048 | tf_op jit(solution)/shard_map/reduce_scatter | solution.py:222
  1925.1 337.9 %reduce-scatter.9.cloned.1.call-start = ((), (), s32[]{:S(2)}) async-start(), calls=%async_computation.4 | async-start | bytes 4866048 | tf_op jit(solution)/shard_map/reduce_scatter | solution.py:222
  1933.9 476.0 %reduce-scatter.15.cloned.1.call-start = ((), (), s32[]{:S(2)}) async-start(), calls=%async_computation.11 | async-start | bytes 10948608
  1949.9 606.9 %reduce-scatter.13.cloned.1.call-start = ((), (), s32[]{:S(2)}) async-start(), calls=%async_computation.10 | async-start | bytes 10948608
  1974.5 289.5 %copy-start.192 = (f32[2,48]{1,0:T(2,128)S(1)}, f32[2,48]{1,0:T(2,128)}, u32[]{:S(2)}) copy-start(f32[2,48]{1,0:T(2,128)} %param.47) | copy-start | bytes 1156
  1979.8 578.3 %copy-start.193 = (f32[2,24]{1,0:T(2,128)S(1)}, f32[2,24]{1,0:T(2,128)}, u32[]{:S(2)}) copy-start(f32[2,24]{1,0:T(2,128)} %param.45) | copy-start | bytes 580
  1979.8 578.4 %copy-start.183 = (f32[2]{0:T(128)S(1)}, f32[2]{0:T(128)}, u32[]{:S(2)}) copy-start(f32[2]{0:T(128)} %get-tuple-element.3027) | copy-start | bytes 28
  1979.8 578.4 %copy-start.186 = (f32[2]{0:T(128)S(1)}, f32[2]{0:T(128)}, u32[]{:S(2)}) copy-start(f32[2]{0:T(128)} %get-tuple-element.3065) | copy-start | bytes 28
  1979.8 578.4 %copy-start.190 = (f32[2]{0:T(128)S(1)}, f32[2]{0:T(128)}, u32[]{:S(2)}) copy-start(f32[2]{0:T(128)} %get-tuple-element.3031) | copy-start | bytes 28
  1979.8 619.0 %copy-start.163 = (f32[2,768]{1,0:T(2,128)S(1)}, f32[2,768]{1,0:T(2,128)}, u32[]{:S(2)}) copy-start(f32[2,768]{1,0:T(2,128)} %param.48) | copy-start | bytes 18436
  1979.9 619.1 %copy-start.112 = (f32[2,3352]{1,0:T(2,128)S(1)}, f32[2,3352]{1,0:T(2,128)}, u32[]{:S(2)}) copy-start(f32[2,3352]{1,0:T(2,128)} %param.46) | copy-start | bytes 80452
  1979.9 659.8 %copy-start.33 = (f32[2,24,3352]{2,1,0:T(8,128)S(1)}, f32[2,24,3352]{2,1,0:T(8,128)}, u32[]{:S(2)}) copy-start(f32[2,24,3352]{2,1,0:T(8,128)} %param.41) | copy-start | bytes 1930756
  1979.9 661.0 %copy-start.47 = (f32[2,48,768]{2,1,0:T(8,128)S(1)}, f32[2,48,768]{2,1,0:T(8,128)}, u32[]{:S(2)}) copy-start(f32[2,48,768]{2,1,0:T(8,128)} %param.42) | copy-start | bytes 884740
  1979.9 661.9 %copy-start.143 = (f32[2,3,24]{2,0,1:T(2,128)S(1)}, f32[2,3,24]{2,0,1:T(2,128)}, u32[]{:S(2)}) copy-start(f32[2,3,24]{2,0,1:T(2,128)} %param.50) | copy-start | bytes 1732
  1979.9 664.4 %copy-start.140 = (f32[2,352]{1,0:T(2,128)S(1)}, f32[2,352]{1,0:T(2,128)}, u32[]{:S(2)}) copy-start(f32[2,352]{1,0:T(2,128)} %param.43) | copy-start | bytes 8452
  2038.3 606.7 %copy-start.141 = (f32[2,352]{1,0:T(2,128)}, f32[2,352]{1,0:T(2,128)S(1)}, u32[]{:S(2)}) copy-start(f32[2,352]{1,0:T(2,128)S(1)} %get-tuple-element.2937) | copy-start | bytes 8452
  2038.3 606.7 %copy-start.142 = (f32[2,352]{1,0:T(2,128)}, f32[2,352]{1,0:T(2,128)S(1)}, u32[]{:S(2)}) copy-start(f32[2,352]{1,0:T(2,128)S(1)} %get-tuple-element.2938) | copy-start | bytes 8452
  2264.1 380.9 %copy-start.34 = (f32[2,48,768]{2,1,0:T(8,128)}, f32[2,48,768]{2,1,0:T(8,128)S(1)}, u32[]{:S(2)}) copy-start(f32[2,48,768]{2,1,0:T(8,128)S(1)} %get-tuple-element.2941) | copy-start | bytes 884740
  2264.2 380.8 %copy-start.157 = (f32[2,48]{1,0:T(2,128)}, f32[2,48]{1,0:T(2,128)S(1)}, u32[]{:S(2)}) copy-start(f32[2,48]{1,0:T(2,128)S(1)} %get-tuple-element.2940) | copy-start | bytes 1156
  (193 other events, 2454.9 us)
Sparse Core Ops, SparseCore 0:
  11.4 60.1 all-gather.16
  75.0 64.4 all-gather.10
  142.8 56.1 all-gather.12
  202.3 64.5 all-gather.14
  1917.4 119.1 all-reduce.73
  2042.0 108.4 reduce-scatter.10
  2156.9 106.0 reduce-scatter.8
  2269.0 140.7 reduce-scatter.14
  2416.0 140.7 reduce-scatter.12
where the time goes:
time: 2670 us; the launch traced here: 2650 us
  local copies, waits for them, and re-layouts  828 us (31%)
  waiting for transfers between devices  630 us (24%)
  matrix products  595 us (22%)
  other arithmetic  455 us (17%)
  blocking collectives  123 us (5%)
    unnamed x12, waiting for transfers between devices  345 us
    dynamic_update_slice x32, local copies, waits for them, and re-layouts, state_space(): lax.map(jax.checkpoint(span_terms), (span_x, span_b, span_c, cumlog, span...  314 us
    dot_general x32, matrix products, span_terms(): within = jnp.einsum('hij,jhp->ihp', mixing, span_x, precision=PRECISE)  271 us
    reduce_scatter x2, waiting for transfers between devices, on_device(): lax.psum_scatter(grad_out, ('dp', 'fsdp'), scatter_dimension=0, tiled=True)  225 us
    dot_general x32, matrix products, span_terms(): jnp.einsum('js,jhp->hsp', span_b, span_x * to_end[:, :, None], precision=...  80.7 us
    psum x2, blocking collectives, on_device(): lax.psum((column_in, column_out, head_part, totals), ('dp', 'fsdp'))  80.1 us
    dynamic_slice x72, local copies, waits for them, and re-layouts, state_space(): lax.scan(advance, start_state, (local_state, cumlog[:, -1, :], linked))  75 us
    dot_general x4, matrix products, state_space(): inflow = jnp.einsum('cis,chsp->cihp', span_c, entering, precision=PRECISE)  60.4 us
  transfers between devices with their start and end apart: 9, of which 6 were waited for; matrix products, arithmetic and copies ran while one was open for 11% of the time, Pallas kernels for 0%

commit v1 on v0

v1 whole, which is shorter than its diff:
```python
from functools import partial

import jax
import jax.numpy as jnp
from jax import lax
from jax.experimental import pallas as pl
from jax.experimental.pallas import tpu as pltpu
from jax.sharding import PartitionSpec as P

D = 768
NHEADS = 24
HEADDIM = 64
STATE = 128
LAYERS = 2
INNER = 1536
CH = 1792
P_SIZE = 3352
VEC = 11264

EPSILON = 1e-05
MOMENT_DECAY = 0.5
CLIP_LIMIT = 1.0
RELATIVE_STEP = 0.5

SPAN = 128
GROUP = 256
GROUPS = INNER // GROUP
LANES = 128
LOG2E = 1.4426950408889634
VMEM_LIMIT = 60 * 1024 * 1024
F32 = jnp.float32
BF16 = jnp.bfloat16
NN = ((1,), (0,))
NT = ((1,), (1,))
TN = ((0,), (0,))

PASS_PAIR = 3
PASS_STATE = 3
PASS_RED = 2


def halves(v):
    high = v.astype(BF16)
    return high, (v - high.astype(F32)).astype(BF16)


def raw_dot(a, b, dims):
    return lax.dot_general(a, b, (dims, ((), ())), preferred_element_type=F32)


def mm(a, b, dims, passes):
    if passes == 1:
        return raw_dot(a.astype(BF16), b.astype(BF16), dims)
    a_hi, a_lo = halves(a)
    b_hi, b_lo = halves(b)
    return raw_dot(a_hi, b_hi, dims) + (raw_dot(a_lo, b_hi, dims) + raw_dot(a_hi, b_lo, dims))


def exact_left(a01, b):
    hi, lo = halves(b)
    rest = (b - hi.astype(F32) - lo.astype(F32)).astype(BF16)
    return raw_dot(a01, hi, NN) + (raw_dot(a01, lo, NN) + raw_dot(a01, rest, NN))


def reduce_right(a, b01, passes):
    if passes == 1:
        return raw_dot(a.astype(BF16), b01, NN)
    hi, lo = halves(a)
    return raw_dot(hi, b01, NN) + raw_dot(lo, b01, NN)


def sigmoid(v):
    return 0.5 * jnp.tanh(0.5 * v) + 0.5


def partial8(v):
    return jnp.sum(v.reshape(v.shape[0] // 8, 8, v.shape[1]), axis=0)


def segment_of(place, ends_ref):
    total = (place >= ends_ref[0]).astype(jnp.int32)
    for k in range(1, 4):
        total = total + (place >= ends_ref[k]).astype(jnp.int32)
    return total


def scalar_segment(place, ends_ref):
    total = jnp.int32(0)
    for k in range(4):
        total = total + jnp.where(place >= ends_ref[k], 1, 0).astype(jnp.int32)
    return total


def block_terms(base, ends_ref, hw_ref, rate_in):
    shape = (SPAN, LANES)
    place = base + lax.broadcasted_iota(jnp.int32, shape, 0)
    seg = segment_of(place, ends_ref)
    first_seg = jnp.where(base > 0, scalar_segment(base - 1, ends_ref), -1)
    last_seg = scalar_segment(base + SPAN - 1, ends_ref)
    pre = rate_in + hw_ref[0:1, :]
    head_ok = lax.broadcasted_iota(jnp.int32, shape, 1) < NHEADS
    steps = jnp.where(head_ok, jnp.maximum(pre, 0.0) + jnp.log1p(jnp.exp(-jnp.abs(pre))), 0.0)
    log_rate = hw_ref[1:2, :] * steps
    rows = lax.broadcasted_iota(jnp.int32, (SPAN, SPAN), 0)
    cols = lax.broadcasted_iota(jnp.int32, (SPAN, SPAN), 1)
    lower = jnp.where(rows >= cols, 1.0, 0.0)
    cum = exact_left(lower.astype(BF16), log_rate * LOG2E)
    reach = jnp.where(seg == first_seg, jnp.exp2(cum), 0.0)
    to_end = jnp.where(seg == last_seg, jnp.exp2(cum[SPAN - 1 : SPAN, :] - cum), 0.0)
    seg_row = segment_of(base + cols, ends_ref)
    seg_col = segment_of(base + rows, ends_ref)
    same = seg_row == seg_col
    return place, seg, pre, steps, log_rate, cum, reach, to_end, rows, cols, same


def lag_mask(place, seg, ends_ref, lag):
    other = place + lag
    ok = (segment_of(other, ends_ref) == seg) & (other >= 0)
    return jnp.where(ok, 1.0, 0.0)


def two_parts(v):
    hi, lo = halves(v)
    return jnp.concatenate([hi, lo], axis=1)


def lane_split(v):
    first = lax.broadcasted_iota(jnp.int32, v.shape, 1) < HEADDIM
    return jnp.concatenate([jnp.where(first, v, 0.0), jnp.where(first, 0.0, v)], axis=0)


def pair_columns(cum, head):
    one = jnp.broadcast_to(cum[:, head : head + 1], (SPAN, SPAN))
    two = jnp.broadcast_to(cum[:, head + 1 : head + 2], (SPAN, SPAN))
    return jnp.concatenate([one, two], axis=1)


def pair_rows(cum_t, head):
    return jnp.concatenate([cum_t[head : head + 1, :], cum_t[head + 1 : head + 2, :]], axis=1)


def forward_kernel(
    ends_ref, zx_ref, par_ref, gain_ref, hw_ref, spread_ref, gn_ref, ys_ref, st_ref, buf, act, pad, state, yg
):
    block = pl.program_id(0)
    base = block * SPAN

    @pl.when(block == 0)
    def _():
        buf[0:8, :] = jnp.zeros((8, CH), F32)
        state[...] = jnp.zeros_like(state)
        pad[...] = jnp.zeros_like(pad)

    pad[:, 0:NHEADS] = zx_ref[:, INNER + CH : P_SIZE]
    place, seg, pre, steps, log_rate, cum, reach, to_end, rows, cols, same = block_terms(
        base, ends_ref, hw_ref, pad[...]
    )
    masks = [lag_mask(place, seg, ends_ref, -k) for k in range(1, 4)]
    for c in range(CH // LANES):
        cs = slice(LANES * c, LANES * (c + 1))
        now = zx_ref[:, INNER + LANES * c : INNER + LANES * (c + 1)]
        buf[8 : 8 + SPAN, cs] = now
        conv = par_ref[4:5, cs] + par_ref[3:4, cs] * now
        for k in range(1, 4):
            conv = conv + par_ref[3 - k : 4 - k, cs] * (masks[k - 1] * buf[8 - k : 8 - k + SPAN, cs])
        buf[0:8, cs] = now[SPAN - 8 : SPAN, :]
        act[:, cs] = conv * sigmoid(conv)
    bm = act[:, INNER : INNER + STATE]
    cm = act[:, INNER + STATE : CH]
    gram = mm(cm, bm, NT, 3)
    gram2 = jnp.concatenate([gram, gram], axis=1)
    bias = jnp.where(same & (rows >= cols), 0.0, -1e30)
    bias2 = jnp.concatenate([bias, bias], axis=1)
    cum_t = cum.T
    bm_t = bm.T
    steps2, reach2, to_end2 = two_parts(steps), two_parts(reach), two_parts(to_end)
    st_ref[0] = state[...]
    squares = jnp.zeros((SPAN, LANES), F32)
    for g in range(GROUPS):
        gs = slice(GROUP * g, GROUP * (g + 1))
        spread = spread_ref[:, gs]
        x = act[:, gs]
        xd = x * raw_dot(steps2, spread, NN)
        within = []
        for q in range(2):
            head = 4 * g + 2 * q
            mix = jnp.exp2(pair_columns(cum, head) - pair_rows(cum_t, head) + bias2) * gram2
            within.append(mm(mix, lane_split(xd[:, LANES * q : LANES * (q + 1)]), NN, PASS_PAIR))
        reach_g = raw_dot(reach2, spread, NN)
        before = state[:, gs]
        scan = jnp.concatenate(within, axis=1) + mm(cm, before, NN, PASS_STATE) * reach_g
        ys_ref[:, gs] = scan
        state[:, gs] = before * reach_g[SPAN - 1 : SPAN, :] + mm(
            bm_t, xd * raw_dot(to_end2, spread, NN), NN, PASS_STATE
        )
        z = zx_ref[:, gs]
        gated = (scan + gain_ref[1:2, gs] * x) * (z * sigmoid(z))
        yg[:, gs] = gated
        gated = gated * gated
        squares = squares + gated[:, :LANES] + gated[:, LANES:]
    scale = lax.rsqrt(jnp.sum(squares, axis=1, keepdims=True) / INNER + EPSILON)
    for g in range(GROUPS):
        gs = slice(GROUP * g, GROUP * (g + 1))
        gn_ref[:, gs] = (yg[:, gs] * scale * gain_ref[0:1, gs]).astype(BF16)


def backward_kernel(
    ends_ref, zx_ref, halo_ref, dgn_ref, ys_ref, st_ref, par_ref, gain_ref, hw_ref, spread_ref, gather_ref,
    dzx_ref, dpar_ref, dgain_ref, dhw_ref,
    buf, act, slope, dact, dcv, pad, rgrad, yg, dgram,
):
    step = pl.program_id(0)
    block = pl.num_programs(0) - 1 - step
    base = block * SPAN

    @pl.when(step == 0)
    def _():
        dcv[0:8, :] = jnp.zeros((8, CH), F32)
        rgrad[...] = jnp.zeros_like(rgrad)
        pad[...] = jnp.zeros_like(pad)
        dpar_ref[...] = jnp.zeros_like(dpar_ref)
        dgain_ref[...] = jnp.zeros_like(dgain_ref)
        dhw_ref[...] = jnp.zeros_like(dhw_ref)

    pad[:, 0:NHEADS] = zx_ref[:, INNER + CH : P_SIZE]
    place, seg, pre, steps, log_rate, cum, reach, to_end, rows, cols, same = block_terms(
        base, ends_ref, hw_ref, pad[...]
    )
    back_masks = [lag_mask(place, seg, ends_ref, -k) for k in range(1, 4)]
    fore_masks = [lag_mask(place, seg, ends_ref, k) for k in range(1, 4)]
    for c in range(CH // LANES):
        cs = slice(LANES * c, LANES * (c + 1))
        zs = slice(INNER + LANES * c, INNER + LANES * (c + 1))
        now = zx_ref[:, zs]
        buf[0:8, cs] = halo_ref[:, zs]
        buf[8 : 8 + SPAN, cs] = now
        conv = par_ref[4:5, cs] + par_ref[3:4, cs] * now
        for k in range(1, 4):
            conv = conv + par_ref[3 - k : 4 - k, cs] * (back_masks[k - 1] * buf[8 - k : 8 - k + SPAN, cs])
        gate = sigmoid(conv)
        act[:, cs] = conv * gate
        slope[:, cs] = gate * (1.0 + conv * (1.0 - gate))
        dcv[SPAN : SPAN + 8, cs] = dcv[0:8, cs]
    bm = act[:, INNER : INNER + STATE]
    cm = act[:, INNER + STATE : CH]
    gram_t = mm(cm, bm, NT, 3).T
    gram2 = jnp.concatenate([gram_t, gram_t], axis=1)
    bias = jnp.where(same & (rows <= cols), 0.0, -1e30)
    bias2 = jnp.concatenate([bias, bias], axis=1)
    cum_t = cum.T
    cm_t = cm.T
    steps2, reach2, to_end2 = two_parts(steps), two_parts(reach), two_parts(to_end)

    squares = jnp.zeros((SPAN, LANES), F32)
    overlap = jnp.zeros((SPAN, LANES), F32)
    for g in range(GROUPS):
        gs = slice(GROUP * g, GROUP * (g + 1))
        z = zx_ref[:, gs]
        gated = (ys_ref[:, gs] + gain_ref[1:2, gs] * act[:, gs]) * (z * sigmoid(z))
        yg[:, gs] = gated
        shared = gated * (dgn_ref[:, gs] * gain_ref[0:1, gs])
        gated = gated * gated
        squares = squares + gated[:, :LANES] + gated[:, LANES:]
        overlap = overlap + shared[:, :LANES] + shared[:, LANES:]
    scale = lax.rsqrt(jnp.sum(squares, axis=1, keepdims=True) / INNER + EPSILON)
    pull = jnp.sum(overlap, axis=1, keepdims=True) * (scale * scale * scale) / INNER

    dgram[...] = jnp.zeros_like(dgram)
    dbm = jnp.zeros((SPAN, STATE), F32)
    dcm = jnp.zeros((SPAN, STATE), F32)
    red_rate = jnp.zeros((SPAN, LANES), F32)
    red_tail = jnp.zeros((SPAN, LANES), F32)
    red_step = jnp.zeros((SPAN, LANES), F32)
    red_through = jnp.zeros((8, LANES), F32)
    for g in range(GROUPS):
        gs = slice(GROUP * g, GROUP * (g + 1))
        spread = spread_ref[:, gs]
        gather = gather_ref[gs, :]
        x = act[:, gs]
        z = zx_ref[:, gs]
        gate = sigmoid(z)
        soft = z * gate
        scan = ys_ref[:, gs]
        skip = gain_ref[1:2, gs]
        y = scan + skip * x
        gated = yg[:, gs]
        dgn = dgn_ref[:, gs]
        dgated = scale * (dgn * gain_ref[0:1, gs]) - gated * pull
        dgain_ref[0:8, gs] += partial8(dgn * (gated * scale))
        dy = dgated * soft
        dzx_ref[:, gs] = (dgated * y * (gate * (1.0 + z * (1.0 - gate)))).astype(BF16)
        dgain_ref[8:16, gs] += partial8(dy * x)
        steps_g = raw_dot(steps2, spread, NN)
        reach_g = raw_dot(reach2, spread, NN)
        to_end_g = raw_dot(to_end2, spread, NN)
        xd = x * steps_g
        dxd_in = []
        for q in range(2):
            head = 4 * g + 2 * q
            qs = slice(LANES * q, LANES * (q + 1))
            decay = jnp.exp2(pair_rows(cum_t, head) - pair_columns(cum, head) + bias2)
            dy_two = lane_split(dy[:, qs])
            dxd_in.append(mm(decay * gram2, dy_two, NN, PASS_PAIR))
            dgram[...] += decay * mm(xd[:, qs], dy_two, NT, PASS_PAIR)
        dxd_in = jnp.concatenate(dxd_in, axis=1)
        later = rgrad[:, gs]
        before = st_ref[0, :, gs]
        dxd_out = mm(bm, later, NN, PASS_STATE) * to_end_g
        dbm = dbm + mm(xd * to_end_g, later, NT, PASS_STATE)
        dy_reach = dy * reach_g
        dcm = dcm + mm(dy_reach, before, NT, PASS_STATE)
        fade = reach_g[SPAN - 1 : SPAN, :]
        red_through = red_through + reduce_right(partial8(before * later) * fade, gather, 2)
        rgrad[:, gs] = later * fade + mm(cm_t, dy_reach, NN, PASS_STATE)
        if PASS_PAIR == 1:
            dy_seen, xd_seen = dy.astype(BF16).astype(F32), xd.astype(BF16).astype(F32)
        else:
            dy_seen, xd_seen = dy, xd
        dxd = dxd_in + dxd_out
        red_rate = red_rate + reduce_right(dy_seen * scan - xd_seen * dxd_in, gather, 2)
        red_tail = red_tail + reduce_right(x * dxd_out, gather, PASS_RED)
        red_step = red_step + reduce_right(x * dxd, gather, PASS_RED)
        dact[:, gs] = skip * dy + steps_g * dxd
    dgram_t = dgram[:, :SPAN] + dgram[:, SPAN:]
    dact[:, INNER : INNER + STATE] = dbm + mm(dgram_t, cm, NN, 3)
    dact[:, INNER + STATE : CH] = dcm + mm(dgram_t.T, bm, NN, 3)

    upper = jnp.where(rows <= cols, 1.0, 0.0).astype(BF16)
    strict = jnp.where(rows > cols, 1.0, 0.0).astype(BF16)
    through = jnp.sum(red_through, axis=0, keepdims=True)
    drate = exact_left(upper, red_rate) + exact_left(strict, steps * red_tail) + through
    dsteps = red_step + drate * hw_ref[1:2, :]
    dpre = dsteps * sigmoid(pre)
    dhw_ref[0:8, :] += partial8(dpre)
    dhw_ref[8:16, :] += partial8(drate * log_rate)
    dzx_ref[:, INNER + CH : P_SIZE] = dpre[:, :NHEADS].astype(BF16)

    for c in range(CH // LANES):
        cs = slice(LANES * c, LANES * (c + 1))
        dconv = dact[:, cs] * slope[:, cs]
        dcv[0:SPAN, cs] = dconv
        dxbc = par_ref[3:4, cs] * dconv
        dpar_ref[24:32, cs] += partial8(dconv * buf[8 : 8 + SPAN, cs])
        dpar_ref[32:40, cs] += partial8(dconv)
        for k in range(1, 4):
            dxbc = dxbc + par_ref[3 - k : 4 - k, cs] * (fore_masks[k - 1] * dcv[k : k + SPAN, cs])
            dpar_ref[24 - 8 * k : 32 - 8 * k, cs] += partial8(
                dconv * (back_masks[k - 1] * buf[8 - k : 8 - k + SPAN, cs])
            )
        dzx_ref[:, INNER + LANES * c : INNER + LANES * (c + 1)] = dxbc.astype(BF16)


def spread_matrices():
    heads = lax.broadcasted_iota(jnp.int32, (LANES, INNER), 0)
    lanes = lax.broadcasted_iota(jnp.int32, (LANES, INNER), 1) // HEADDIM
    one = (heads == lanes).astype(BF16)
    return jnp.concatenate([one, one], axis=0), one.T


def kernel_params(vector, head):
    taps = vector[D + INNER :].reshape(5, CH)
    par = jnp.concatenate([taps, jnp.zeros((3, CH), F32)], axis=0)
    gain = jnp.stack([vector[D : D + INNER], jnp.repeat(head[2], HEADDIM)])
    gain = jnp.concatenate([gain, jnp.zeros((6, INNER), F32)], axis=0)
    hw = jnp.stack([head[0], -jnp.exp(head[1])])
    hw = jnp.pad(hw, ((0, 6), (0, LANES - NHEADS)))
    return par, gain, hw


def whole(shape):
    return pl.BlockSpec(shape, lambda i: (0,) * len(shape))


SMEM = pl.BlockSpec(memory_space=pltpu.SMEM)


def mixer_forward(ends, zx, par, gain, hw, spread):
    tokens = zx.shape[0]
    blocks = tokens // SPAN
    rows = lambda width: pl.BlockSpec((SPAN, width), lambda i: (i, 0))
    return pl.pallas_call(
        forward_kernel,
        grid=(blocks,),
        in_specs=[SMEM, rows(P_SIZE), whole((8, CH)), whole((8, INNER)), whole((8, LANES)), whole((256, INNER))],
        out_specs=[rows(INNER), rows(INNER), pl.BlockSpec((1, STATE, INNER), lambda i: (i, 0, 0))],
        out_shape=[
            jax.ShapeDtypeStruct((tokens, INNER), BF16),
            jax.ShapeDtypeStruct((tokens, INNER), F32),
            jax.ShapeDtypeStruct((blocks, STATE, INNER), F32),
        ],
        scratch_shapes=[
            pltpu.VMEM((SPAN + 8, CH), F32),
            pltpu.VMEM((SPAN, CH), F32),
            pltpu.VMEM((SPAN, LANES), F32),
            pltpu.VMEM((STATE, INNER), F32),
            pltpu.VMEM((SPAN, INNER), F32),
        ],
        compiler_params=pltpu.CompilerParams(vmem_limit_bytes=VMEM_LIMIT),
        cost_estimate=pl.CostEstimate(flops=20_000_000_000, bytes_accessed=30_000_000, transcendentals=6_000_000),
        name="mixer_forward",
    )(ends, zx, par, gain, hw, spread)


def mixer_backward(ends, zx, dgn, ys, st, par, gain, hw, spread, gather):
    tokens = zx.shape[0]
    blocks = tokens // SPAN
    back = lambda width: pl.BlockSpec((SPAN, width), lambda i: (blocks - 1 - i, 0))
    halo = pl.BlockSpec((8, P_SIZE), lambda i: (jnp.maximum((blocks - 1 - i) * (SPAN // 8) - 1, 0), 0))
    return pl.pallas_call(
        backward_kernel,
        grid=(blocks,),
        in_specs=[
            SMEM,
            back(P_SIZE),
            halo,
            back(INNER),
            back(INNER),
            pl.BlockSpec((1, STATE, INNER), lambda i: (blocks - 1 - i, 0, 0)),
            whole((8, CH)),
            whole((8, INNER)),
            whole((8, LANES)),
            whole((256, INNER)),
            whole((INNER, LANES)),
        ],
        out_specs=[back(P_SIZE), whole((40, CH)), whole((16, INNER)), whole((16, LANES))],
        out_shape=[
            jax.ShapeDtypeStruct((tokens, P_SIZE), BF16),
            jax.ShapeDtypeStruct((40, CH), F32),
            jax.ShapeDtypeStruct((16, INNER), F32),
            jax.ShapeDtypeStruct((16, LANES), F32),
        ],
        scratch_shapes=[
            pltpu.VMEM((SPAN + 8, CH), F32),
            pltpu.VMEM((SPAN, CH), F32),
            pltpu.VMEM((SPAN, CH), F32),
            pltpu.VMEM((SPAN, CH), F32),
            pltpu.VMEM((SPAN + 8, CH), F32),
            pltpu.VMEM((SPAN, LANES), F32),
            pltpu.VMEM((STATE, INNER), F32),
            pltpu.VMEM((SPAN, INNER), F32),
            pltpu.VMEM((SPAN, 2 * SPAN), F32),
        ],
        compiler_params=pltpu.CompilerParams(vmem_limit_bytes=VMEM_LIMIT),
        cost_estimate=pl.CostEstimate(flops=60_000_000_000, bytes_accessed=60_000_000, transcendentals=9_000_000),
        name="mixer_backward",
    )(ends, zx, zx, dgn, ys, st, par, gain, hw, spread, gather)


def finish_params(dpar, dgain, dhw):
    dtaps = jnp.sum(dpar.reshape(5, 8, CH), axis=1).reshape(5 * CH)
    dgate = jnp.sum(dgain[0:8], axis=0)
    dskip = jnp.sum(dgain[8:16].reshape(8, NHEADS, HEADDIM), axis=(0, 2))
    dh = jnp.sum(dhw.reshape(2, 8, LANES), axis=1)[:, :NHEADS]
    return jnp.concatenate([dgate, dtaps]), jnp.concatenate([dh, dskip[None]], axis=0)


AXES = ("dp", "fsdp")


def rms_norm(values, scales):
    return values * lax.rsqrt(jnp.mean(values * values, axis=-1, keepdims=True) + EPSILON) * scales


def norm_part(stream, gain):
    return rms_norm(stream, gain[None, :])


def on_device(
    hidden_in,
    cotangent,
    seq_lengths,
    in_weight,
    out_weight,
    vector_weight,
    head_weight,
    in_row_moment,
    in_col_moment,
    out_row_moment,
    out_col_moment,
    vector_moment,
    head_moment,
):
    token_count = hidden_in.shape[0]
    lengths = seq_lengths[0]
    e0 = lengths[0]
    e1 = e0 + lengths[1]
    e2 = e1 + lengths[2]
    e3 = e2 + lengths[3]
    ends = jnp.stack([e0, e1, e2, e3])
    valid = (jnp.arange(token_count, dtype=jnp.int32) < e3).astype(F32)
    spread, gather = spread_matrices()
    vector_full = lax.all_gather(vector_weight.astype(BF16), AXES, axis=1, tiled=True).astype(F32)
    stream = hidden_in.astype(F32)
    stored = []
    for l in range(LAYERS):
        full_in = lax.all_gather(in_weight[l].astype(BF16), AXES, axis=0, tiled=True)
        full_out = lax.all_gather(out_weight[l].astype(BF16), AXES, axis=0, tiled=True)
        tables = kernel_params(vector_full[l], head_weight[l])
        normed, norm_pull = jax.vjp(norm_part, stream, vector_full[l, :D])
        normed = normed.astype(BF16)
        zx = jnp.dot(normed, full_in, preferred_element_type=F32)
        gn, ys, st = mixer_forward(ends, zx, *tables, spread)
        stream = stream + jnp.dot(gn, full_out, preferred_element_type=F32)
        stored.append((norm_pull, normed, zx, gn, ys, st, tables, full_in, full_out))
    layer_out = stream.astype(BF16)
    flowing = cotangent.astype(F32) * valid[:, None]
    in_parts = [None] * LAYERS
    out_parts = [None] * LAYERS
    vector_parts = [None] * LAYERS
    head_parts = [None] * LAYERS
    for l in reversed(range(LAYERS)):
        norm_pull, normed, zx, gn, ys, st, tables, full_in, full_out = stored[l]
        gb = flowing.astype(BF16)
        grad_out = jnp.einsum("te,td->ed", gn, gb, preferred_element_type=F32)
        dgn = jnp.einsum("td,ed->te", gb, full_out, preferred_element_type=F32)
        dzx, dpar, dgain, dhw = mixer_backward(ends, zx, dgn, ys, st, *tables, spread, gather)
        grad_in = jnp.einsum("td,tp->dp", normed, dzx, preferred_element_type=F32)
        dxn = jnp.einsum("tp,dp->td", dzx, full_in, preferred_element_type=F32)
        grad_stream, dnorm = norm_pull(dxn)
        flowing = flowing + grad_stream
        dvec, head_parts[l] = finish_params(dpar, dgain, dhw)
        vector_parts[l] = jnp.concatenate([dnorm, dvec])
        in_parts[l] = lax.psum_scatter(grad_in, AXES, scatter_dimension=0, tiled=True)
        out_parts[l] = lax.psum_scatter(grad_out, AXES, scatter_dimension=0, tiled=True)
    grad_in = jnp.stack(in_parts)
    grad_out = jnp.stack(out_parts)
    grad_vector = lax.psum_scatter(jnp.stack(vector_parts), AXES, scatter_dimension=1, tiled=True)
    head_part = jnp.stack(head_parts)
    squares_in = grad_in * grad_in
    squares_out = grad_out * grad_out
    row_in = MOMENT_DECAY * in_row_moment + (1.0 - MOMENT_DECAY) * jnp.mean(squares_in, axis=2)
    row_out = MOMENT_DECAY * out_row_moment + (1.0 - MOMENT_DECAY) * jnp.mean(squares_out, axis=2)
    vector_new = MOMENT_DECAY * vector_moment + (1.0 - MOMENT_DECAY) * grad_vector * grad_vector
    vector_update = grad_vector * lax.rsqrt(vector_new)
    totals = jnp.stack(
        [
            jnp.sum(row_in, axis=1),
            jnp.sum(row_out, axis=1),
            jnp.sum(in_weight * in_weight, axis=(1, 2)),
            jnp.sum(out_weight * out_weight, axis=(1, 2)),
            jnp.sum(vector_weight * vector_weight, axis=1),
            jnp.sum(vector_update * vector_update, axis=1),
        ],
        axis=1,
    )
    local = (
        jnp.sum(squares_in, axis=1),
        jnp.sum(squares_out, axis=1),
        jnp.sum(squares_in / row_in[:, :, None], axis=1),
        jnp.sum(squares_out / row_out[:, :, None], axis=1),
        head_part.reshape(LAYERS, 3 * NHEADS),
        totals,
    )
    widths = [v.shape[1] for v in local]
    summed = lax.psum(jnp.concatenate(local, axis=1), AXES)
    column_in, column_out, scaled_in, scaled_out, head_total, totals = jnp.split(
        summed, [sum(widths[: i + 1]) for i in range(5)], axis=1
    )
    head_total = head_total.reshape(LAYERS, 3, NHEADS)
    col_in = MOMENT_DECAY * in_col_moment + (1.0 - MOMENT_DECAY) * column_in / D
    col_out = MOMENT_DECAY * out_col_moment + (1.0 - MOMENT_DECAY) * column_out / INNER
    mean_in = totals[:, 0] / D
    mean_out = totals[:, 1] / INNER
    norm_in = jnp.sqrt(mean_in * jnp.sum(scaled_in / col_in, axis=1) / (D * P_SIZE))
    norm_out = jnp.sqrt(mean_out * jnp.sum(scaled_out / col_out, axis=1) / (INNER * D))
    norm_vector = jnp.sqrt(totals[:, 5] / VEC)
    head_new = MOMENT_DECAY * head_moment + (1.0 - MOMENT_DECAY) * head_total * head_total
    head_update = head_total * lax.rsqrt(head_new)
    norm_head = jnp.sqrt(jnp.mean(head_update * head_update, axis=(1, 2)))

    def step_of(square_mean, norm):
        return RELATIVE_STEP * jnp.sqrt(square_mean) / jnp.maximum(1.0, norm / CLIP_LIMIT)

    step_in = step_of(totals[:, 2] / (D * P_SIZE), norm_in)
    step_out = step_of(totals[:, 3] / (INNER * D), norm_out)
    step_vector = step_of(totals[:, 4] / VEC, norm_vector)
    step_head = step_of(jnp.mean(head_weight * head_weight, axis=(1, 2)), norm_head)
    update_in = grad_in * lax.rsqrt(row_in[:, :, None] * col_in[:, None, :] / mean_in[:, None, None])
    update_out = grad_out * lax.rsqrt(row_out[:, :, None] * col_out[:, None, :] / mean_out[:, None, None])
    new_in = in_weight - step_in[:, None, None] * update_in
    new_out = out_weight - step_out[:, None, None] * update_out
    new_vector = vector_weight - step_vector[:, None] * vector_update
    new_head = head_weight - step_head[:, None, None] * head_update
    update_rms = jnp.stack([norm_in, norm_out, norm_vector, norm_head], axis=1)
    return (
        layer_out,
        flowing,
        grad_in,
        grad_out,
        grad_vector,
        head_total,
        new_in,
        new_out,
        new_vector,
        new_head,
        new_in.astype(BF16),
        new_out.astype(BF16),
        new_vector.astype(BF16),
        new_head.astype(BF16),
        row_in,
        col_in,
        row_out,
        col_out,
        vector_new,
        head_new,
        update_rms,
    )


def solution(mesh):
    rows = P(AXES, None)
    mat = P(None, AXES, None)
    vec = P(None, AXES)
    one = P()
    return jax.shard_map(
        on_device,
        mesh=mesh,
        in_specs=(rows, rows, rows, mat, mat, vec, one, vec, one, vec, one, vec, one),
        out_specs=(
            rows, rows, mat, mat, vec, one, mat, mat, vec, one, mat, mat, vec, one, vec, one, vec, one, vec, one, one,
        ),
        check_vma=False,
    )
```

time: 2670 us -> 1290 us (0.48)
  local copies, waits for them, and re-layouts: 828 us -> 22.7 us
  matrix products: 595 us -> 110 us
  other arithmetic: 455 us -> 34.4 us
  waiting for transfers between devices: 630 us -> 842 us
  Pallas kernels: 0 us -> 183 us
  blocking collectives: 123 us -> 70.6 us
    dot_general x120 -> x12, matrix products: 564 us -> 110 us  [the longest x2 24.1 us: on_device(): zx = jnp.dot(normed, full_in, preferred_element_type=F32)]
    dynamic_update_slice x80 -> x0, local copies, waits for them, and re-layouts: 337 us -> none  [the longest x32 314 us: state_space(): lax.map(jax.checkpoint(span_terms), (span_x, span_b, span_c, cumlog, span...]
    pallas_call x0 -> x4, Pallas kernels: none -> 183 us  [the longest x2 119 us: mixer_backward(): pl.pallas_call(backward_kernel, grid=(blocks,), in_specs=[SMEM, back(P_SI...]
    reduce_sum x33 -> x14, other arithmetic: 130 us -> 6.8 us  [the longest x1 1.21 us: on_device(): jnp.mean(squares_in, axis=2)]
    dynamic_slice x128 -> x0, local copies, waits for them, and re-layouts: 119 us -> none  [the longest x72 75 us: state_space(): lax.scan(advance, start_state, (local_state, cumlog[:, -1, :], linked))]
    psum x0 -> x1, waiting for transfers between devices: none -> 110 us  [on_device(): summed = lax.psum(jnp.concatenate(local, axis=1), AXES)]
    slice x85 -> x6, local copies, waits for them, and re-layouts: 97.1 us -> 2.33 us  [the longest x1 0.74 us: on_device(): in_weight[l].astype(BF16)]
    psum x2 -> x0, blocking collectives: 80.1 us -> none  [on_device(): lax.psum((column_in, column_out, head_part, totals), ('dp', 'fsdp'))]
  transfers between devices with their start and end apart: 9 -> 10, of which waited for: 6 -> 9; matrix products, arithmetic and copies ran while one was open for 11% -> 8% of each run, Pallas kernels for 0% -> 3%
where the time goes in v1:
time: 1290 us; the launch traced here: 1280 us
  waiting for transfers between devices  842 us (65%)
  Pallas kernels  183 us (14%)
  matrix products  110 us (9%)
  blocking collectives  70.6 us (5%)
  other arithmetic  34.4 us (3%)
  local copies, waits for them, and re-layouts  22.7 us (2%)
  between operations  17.8 us (1%)
    unnamed x13, waiting for transfers between devices  401 us
    reduce_scatter x2, waiting for transfers between devices, on_device(): lax.psum_scatter(grad_out, AXES, scatter_dimension=0, tiled=True)  222 us
    pallas_call x2, Pallas kernels, mixer_backward(): pl.pallas_call(backward_kernel, grid=(blocks,), in_specs=[SMEM, back(P_SI...  119 us
    psum x1, waiting for transfers between devices, on_device(): summed = lax.psum(jnp.concatenate(local, axis=1), AXES)  110 us
    all_gather x2, waiting for transfers between devices, on_device(): lax.all_gather(in_weight[l].astype(BF16), AXES, axis=0, tiled=True)  93.8 us
    all_gather x1, blocking collectives, on_device(): lax.all_gather(vector_weight.astype(BF16), AXES, axis=1, tiled=True)  70.6 us
    pallas_call x2, Pallas kernels, mixer_forward(): pl.pallas_call(forward_kernel, grid=(blocks,), in_specs=[SMEM, rows(P_SIZ...  64.4 us
  transfers between devices with their start and end apart: 10, of which 9 were waited for; matrix products, arithmetic and copies ran while one was open for 8% of the time, Pallas kernels for 3%

profile of v1, /device:TPU:0, one launch (start us, length us, event | category | flops | bytes accessed | tf_op | source)
XLA Modules:
  0.0 1281.7 jit_solution(9209142346767352447)
XLA Ops:
  15.5 70.6 %all-gather.4 = bf16[32,352,2]{1,2,0:T(2,128)(2,1)S(1)} all-gather(bf16[1,352,2]{1,2,0:T(2,128)(2,1)S(1)} %get-tuple-element.217), channel_id=1, replica_groups=mesh['dp'=8,'fsdp'=4] {'dp','fsdp'}, dimensions={0}, use_global_device_ids=true | all-gather | bytes 46464 | tf_op jit(solution)/shard_map/all_gather | solution.py:492
  100.0 6.3 fusion.17.dgn_ref
  106.3 33.2 %all-gather.10.cloned.1.call-done = bf16[1,768,3352]{2,1,0:T(8,128)(2,1)} async-done(((bf16[1,24,3352]{2,1,0:T(8,128)(2,1)}), bf16[1,768,3352]{2,1,0:T(8,128)(2,1)}) %all-gather.10.cloned.1.call-update) | async-done | bytes 5148688 | tf_op jit(solution)/shard_map/all_gather | solution.py:496
  139.5 11.8 fusion.6.zx_ref.halo_ref
  151.3 32.3 %mixer_forward.2 = (bf16[1024,1536]{1,0:T(8,128)(2,1)}, f32[1024,1536]{1,0:T(8,128)}, f32[8,128,1536]{2,1,0:T(8,128)}) custom-call(s32[4]{0:T(128)} %pad_add_fusion.ends_ref, f32[1024,3352]{1,0:T(8,128)} %fusion.6.zx_ref.halo_ref, f32[8,1792]{1,0:T(8,128)} %concatenate.33.par_ref, f32[8,1536]{1,0:T(8,128)} %get-tuple-element.227.gain_ref, ...), custom_call_target="tpu_custom_call" | custom-call | flops 20000000000 | bytes 30000000 | tf_op jit(solution)/shard_map/mixer_forward/pallas_call | solution.py:381
  183.6 15.6 %all-gather.12.cloned.1.call-done = bf16[1,1536,768]{2,1,0:T(8,128)(2,1)} async-done(((bf16[1,48,768]{2,1,0:T(8,128)(2,1)}), bf16[1,1536,768]{2,1,0:T(8,128)(2,1)}) %all-gather.12.cloned.1.call-update) | async-done | bytes 2359312 | tf_op jit(solution)/shard_map/all_gather | solution.py:497
  199.1 7.2 multiply_reduce_fusion.2
  206.3 60.6 %all-gather.14.cloned.1.call-done = bf16[1,768,3352]{2,1,0:T(8,128)(2,1)} async-done(((bf16[1,24,3352]{2,1,0:T(8,128)(2,1)}), bf16[1,768,3352]{2,1,0:T(8,128)(2,1)}) %all-gather.14.cloned.1.call-update) | async-done | bytes 5148688 | tf_op jit(solution)/shard_map/all_gather | solution.py:496
  267.0 12.3 fusion.2.zx_ref.halo_ref
  279.2 32.1 %mixer_forward.3 = (bf16[1024,1536]{1,0:T(8,128)(2,1)}, f32[1024,1536]{1,0:T(8,128)}, f32[8,128,1536]{2,1,0:T(8,128)}) custom-call(s32[4]{0:T(128)} %pad_add_fusion.ends_ref, f32[1024,3352]{1,0:T(8,128)} %fusion.2.zx_ref.halo_ref, f32[8,1792]{1,0:T(8,128)} %concatenate.37.par_ref, f32[8,1536]{1,0:T(8,128)} %get-tuple-element.226.gain_ref, ...), custom_call_target="tpu_custom_call" | custom-call | flops 20000000000 | bytes 30000000 | tf_op jit(solution)/shard_map/mixer_forward/pallas_call | solution.py:381
  311.4 59.5 %mixer_backward.2 = (bf16[1024,3352]{1,0:T(8,128)(2,1)}, f32[40,1792]{1,0:T(8,128)}, f32[16,1536]{1,0:T(8,128)}, f32[16,128]{1,0:T(8,128)}) custom-call(s32[4]{0:T(128)} %pad_add_fusion.ends_ref, f32[1024,3352]{1,0:T(8,128)} %fusion.2.zx_ref.halo_ref, f32[1024,3352]{1,0:T(8,128)} %fusion.2.zx_ref.halo_ref, f32[1024,1536]{1,0:T(8,128)} %fusion.17.dgn_ref, ...), custom_call_target="tpu_custom_call" | custom-call | flops 60000002048 | bytes 60000000 | tf_op jit(solution)/shard_map/mixer_backward/pallas_call | solution.py:409
  370.8 11.3 multiply_reduce_fusion
  382.3 3.4 fusion.12
  385.7 4.7 fusion.21.dgn_ref
  390.4 59.1 %mixer_backward.3 = (bf16[1024,3352]{1,0:T(8,128)(2,1)}, f32[40,1792]{1,0:T(8,128)}, f32[16,1536]{1,0:T(8,128)}, f32[16,128]{1,0:T(8,128)}) custom-call(s32[4]{0:T(128)} %pad_add_fusion.ends_ref, f32[1024,3352]{1,0:T(8,128)} %fusion.6.zx_ref.halo_ref, f32[1024,3352]{1,0:T(8,128)} %fusion.6.zx_ref.halo_ref, f32[1024,1536]{1,0:T(8,128)} %fusion.21.dgn_ref, ...), custom_call_target="tpu_custom_call" | custom-call | flops 60000002048 | bytes 60000000 | tf_op jit(solution)/shard_map/mixer_backward/pallas_call | solution.py:409
  451.5 11.4 fusion.11
  463.0 3.3 copy.196
  467.7 6.7 fusion.29
  474.5 7.6 fusion.32
  482.2 12.2 fusion.65
  494.4 11.6 fusion.36
  507.8 7.5 add_convert_fusion
  515.3 107.1 %reduce-scatter.16.cloned.1.call-done = f32[352,2]{1,0:T(8,128)} async-done(((f32[11264,2]{1,0:T(8,128)}), f32[352,2]{1,0:T(8,128)}) %reduce-scatter.16.cloned.1.call-update) | async-done | bytes 2832
  623.7 109.4 %reduce-scatter.14.cloned.1.call-done = f32[48,768]{1,0:T(8,128)} async-done(((f32[1536,768]{1,0:T(8,128)}), f32[48,768]{1,0:T(8,128)}) %reduce-scatter.14.cloned.1.call-update) | async-done | bytes 147472 | tf_op jit(solution)/shard_map/reduce_scatter | solution.py:524
  733.0 112.5 %reduce-scatter.12.cloned.1.call-done = f32[48,768]{1,0:T(8,128)} async-done(((f32[1536,768]{1,0:T(8,128)}), f32[48,768]{1,0:T(8,128)}) %reduce-scatter.12.cloned.1.call-update) | async-done | bytes 147472 | tf_op jit(solution)/shard_map/reduce_scatter | solution.py:524
  847.0 145.6 %reduce-scatter.20.cloned.1.call-done = f32[24,3352]{1,0:T(8,128)} async-done(((f32[768,3352]{1,0:T(8,128)}), f32[24,3352]{1,0:T(8,128)}) %reduce-scatter.20.cloned.1.call-update) | async-done | bytes 321808
  992.6 146.9 %reduce-scatter.18.cloned.1.call-done = f32[24,3352]{1,0:T(8,128)} async-done(((f32[768,3352]{1,0:T(8,128)}), f32[24,3352]{1,0:T(8,128)}) %reduce-scatter.18.cloned.1.call-update) | async-done | bytes 321808
  1142.0 5.3 fusion.13
  1147.3 2.7 copy.185
  1150.1 2.4 copy.186
  1152.4 109.6 %all-reduce.8.cloned.1.call-done = f32[2,8318]{1,0:T(2,128)} async-done(((f32[2,8318]{1,0:T(2,128)}), f32[2,8318]{1,0:T(2,128)}) %all-reduce.8.cloned.1.call-update) | async-done | bytes 66560 | tf_op jit(solution)/shard_map/psum | solution.py:555
  1268.7 2.5 fusion.69
  (198 shorter events, 39.7 us)
Async XLA Ops:
  7.2 92.8 %all-gather.16.cloned.1.call-start = ((), (), s32[]{:S(2)}) async-start(), calls=%async_computation.11 | async-start | bytes 2433024 | tf_op jit(solution)/shard_map/all_gather | solution.py:497
  9.1 77.4 %copy-start.20 = (f32[2,3,24]{2,0,1:T(2,128)S(1)}, f32[2,3,24]{2,0,1:T(2,128)}, u32[]{:S(2)}) copy-start(f32[2,3,24]{2,0,1:T(2,128)} %param.19) | copy-start | bytes 1732
  9.8 129.7 %all-gather.10.cloned.1.call-start = ((), (), s32[]{:S(2)}) async-start(), calls=%async_computation.8 | async-start | bytes 5474304 | tf_op jit(solution)/shard_map/all_gather | solution.py:496
  12.6 186.6 %all-gather.12.cloned.1.call-start = ((), (), s32[]{:S(2)}) async-start(), calls=%async_computation.9 | async-start | bytes 2433024 | tf_op jit(solution)/shard_map/all_gather | solution.py:497
  13.3 253.7 %all-gather.14.cloned.1.call-start = ((), (), s32[]{:S(2)}) async-start(), calls=%async_computation.10 | async-start | bytes 5474304 | tf_op jit(solution)/shard_map/all_gather | solution.py:496
  13.9 75.9 %copy-start.32 = (s32[1,4]{1,0:T(1,128)S(1)}, s32[1,4]{1,0:T(1,128)}, u32[]{:S(2)}) copy-start(s32[1,4]{1,0:T(1,128)} %param.15) | copy-start | bytes 52
  13.9 608.5 %reduce-scatter.16.cloned.1.call-start = ((), (), s32[]{:S(2)}) async-start(), calls=%async_computation.12 | async-start | bytes 5947392
  14.7 184.4 %copy-start = (bf16[1024,768]{0,1:T(8,128)(2,1)}, bf16[1024,768]{0,1:T(8,128)(2,1)S(1)}, u32[]{:S(2)}) copy-start(bf16[1024,768]{0,1:T(8,128)(2,1)S(1)} %copy.160) | copy-start | bytes 4718596
  89.8 16.5 %copy-start.5 = (bf16[1024,768]{0,1:T(8,128)(2,1)}, bf16[1024,768]{0,1:T(8,128)(2,1)S(1)}, u32[]{:S(2)}) copy-start(bf16[1024,768]{0,1:T(8,128)(2,1)S(1)} %copy.165) | copy-start | bytes 4718596
  95.7 43.8 %copy-start.10 = (f32[768]{0:T(1024)}, f32[768]{0:T(1024)S(1)}, u32[]{:S(2)}) copy-start(f32[768]{0:T(1024)S(1)} %get-tuple-element.169) | copy-start | bytes 9220
  96.1 43.4 %copy-start.12 = (f32[1024]{0:T(1024)}, f32[1024]{0:T(1024)S(1)}, u32[]{:S(2)}) copy-start(f32[1024]{0:T(1024)S(1)} %fusion.48) | copy-start | bytes 12292
  311.4 59.5 %copy-start.4 = (f32[1024,768]{0,1:T(8,128)S(1)}, f32[1024,768]{0,1:T(8,128)}, u32[]{:S(2)}) copy-start(f32[1024,768]{0,1:T(8,128)} %get-tuple-element.233) | copy-start | bytes 9437188
  390.4 61.1 %copy-start.1 = (bf16[1024,768]{0,1:T(8,128)(2,1)S(1)}, bf16[1024,768]{0,1:T(8,128)(2,1)}, u32[]{:S(2)}) copy-start(bf16[1024,768]{0,1:T(8,128)(2,1)} %copy-done) | copy-start | bytes 4718596
  390.4 61.1 %copy-start.11 = (f32[768]{0:T(1024)S(1)}, f32[768]{0:T(1024)}, u32[]{:S(2)}) copy-start(f32[768]{0:T(1024)} %copy-done.10) | copy-start | bytes 9220
  390.4 61.1 %copy-start.13 = (f32[1024]{0:T(1024)S(1)}, f32[1024]{0:T(1024)}, u32[]{:S(2)}) copy-start(f32[1024]{0:T(1024)} %copy-done.12) | copy-start | bytes 12292
  466.3 266.7 %reduce-scatter.14.cloned.1.call-start = ((), (), s32[]{:S(2)}) async-start(), calls=%async_computation.6 | async-start | bytes 4866048 | tf_op jit(solution)/shard_map/reduce_scatter | solution.py:524
  474.4 371.1 %reduce-scatter.12.cloned.1.call-start = ((), (), s32[]{:S(2)}) async-start(), calls=%async_computation.5 | async-start | bytes 4866048 | tf_op jit(solution)/shard_map/reduce_scatter | solution.py:524
  482.1 510.5 %reduce-scatter.20.cloned.1.call-start = ((), (), s32[]{:S(2)}) async-start(), calls=%async_computation.14 | async-start | bytes 10948608
  494.4 645.2 %reduce-scatter.18.cloned.1.call-start = ((), (), s32[]{:S(2)}) async-start(), calls=%async_computation.13 | async-start | bytes 10948608
  506.1 755.9 %all-reduce.8.cloned.1.call-start = ((), (), s32[]{:S(2)}) async-start(), calls=%async_computation.7 | async-start | bytes 133120 | tf_op jit(solution)/shard_map/psum | solution.py:555
  507.7 115.7 %copy-start.34 = (f32[2,352]{1,0:T(2,128)S(1)}, f32[2,352]{1,0:T(2,128)}, u32[]{:S(2)}) copy-start(f32[2,352]{1,0:T(2,128)} %param.24) | copy-start | bytes 8452
  507.7 338.9 %copy-start.35 = (f32[2,48]{1,0:T(2,128)S(1)}, f32[2,48]{1,0:T(2,128)}, u32[]{:S(2)}) copy-start(f32[2,48]{1,0:T(2,128)} %param.22) | copy-start | bytes 1156
  507.8 633.0 %copy-start.36 = (f32[2,24]{1,0:T(2,128)S(1)}, f32[2,24]{1,0:T(2,128)}, u32[]{:S(2)}) copy-start(f32[2,24]{1,0:T(2,128)} %param.20) | copy-start | bytes 580
  623.4 649.7 %copy-start.22 = (f32[2,352]{1,0:T(2,128)}, f32[2,352]{1,0:T(2,128)S(1)}, u32[]{:S(2)}) copy-start(f32[2,352]{1,0:T(2,128)S(1)} %copy.197) | copy-start | bytes 8452
  623.5 649.5 %copy-start.24 = (f32[2,352]{1,0:T(2,128)}, f32[2,352]{1,0:T(2,128)S(1)}, u32[]{:S(2)}) copy-start(f32[2,352]{1,0:T(2,128)S(1)} %get-tuple-element.188) | copy-start | bytes 8452
  846.6 424.6 %copy-start.8 = (f32[2,48,768]{2,1,0:T(8,128)}, f32[2,48,768]{2,1,0:T(8,128)S(1)}, u32[]{:S(2)}) copy-start(f32[2,48,768]{2,1,0:T(8,128)S(1)} %get-tuple-element.194) | copy-start | bytes 884740
  846.7 424.5 %copy-start.29 = (f32[2,48]{1,0:T(2,128)}, f32[2,48]{1,0:T(2,128)S(1)}, u32[]{:S(2)}) copy-start(f32[2,48]{1,0:T(2,128)S(1)} %get-tuple-element.190) | copy-start | bytes 1156
  1140.9 127.9 %copy-start.28 = (f32[2,24]{1,0:T(2,128)}, f32[2,24]{1,0:T(2,128)S(1)}, u32[]{:S(2)}) copy-start(f32[2,24]{1,0:T(2,128)S(1)} %get-tuple-element.192) | copy-start | bytes 580
  1150.0 113.4 %copy-start.19 = (f32[2,3352]{1,0:T(2,128)S(1)}, f32[2,3352]{1,0:T(2,128)}, u32[]{:S(2)}) copy-start(f32[2,3352]{1,0:T(2,128)} %param.21) | copy-start | bytes 80452
  1150.0 114.4 %copy-start.33 = (f32[2,768]{1,0:T(2,128)S(1)}, f32[2,768]{1,0:T(2,128)}, u32[]{:S(2)}) copy-start(f32[2,768]{1,0:T(2,128)} %param.23) | copy-start | bytes 18436
  1150.0 115.5 %copy-start.27 = (f32[2,3,24]{2,0,1:T(2,128)S(1)}, f32[2,3,24]{2,0,1:T(2,128)}, u32[]{:S(2)}) copy-start(f32[2,3,24]{2,0,1:T(2,128)} %param.25) | copy-start | bytes 1732
  1152.4 120.7 %copy-start.26 = (f32[2,352]{1,0:T(2,128)S(1)}, f32[2,352]{1,0:T(2,128)}, u32[]{:S(2)}) copy-start(f32[2,352]{1,0:T(2,128)} %param.18) | copy-start | bytes 8452
  (19 other events, 78.2 us)
Sparse Core Ops, SparseCore 0:
  11.4 60.0 all-gather.15
  75.0 64.4 all-gather.9
  142.9 56.1 all-gather.11
  202.4 64.5 all-gather.13
  466.5 155.8 reduce-scatter.15
  627.7 105.2 reduce-scatter.13
  739.4 106.0 reduce-scatter.11
  851.6 140.9 reduce-scatter.19
  998.7 140.7 reduce-scatter.17
  1145.5 116.4 all-reduce.7

commit v2 on v1

--- a/solution.py
+++ b/solution.py
@@ -15,6 +15,7 @@
 INNER = 1536
 CH = 1792
 P_SIZE = 3352
+XR = 1920
 VEC = 11264
 
 EPSILON = 1e-05
@@ -140,7 +141,7 @@
 
 
 def forward_kernel(
-    ends_ref, zx_ref, par_ref, gain_ref, hw_ref, spread_ref, gn_ref, ys_ref, st_ref, buf, act, pad, state, yg
+    ends_ref, z_ref, xr_ref, par_ref, gain_ref, hw_ref, spread_ref, gn_ref, ys_ref, st_ref, buf, act, state, yg
 ):
     block = pl.program_id(0)
     base = block * SPAN
@@ -149,16 +150,14 @@
     def _():
         buf[0:8, :] = jnp.zeros((8, CH), F32)
         state[...] = jnp.zeros_like(state)
-        pad[...] = jnp.zeros_like(pad)
-
-    pad[:, 0:NHEADS] = zx_ref[:, INNER + CH : P_SIZE]
+
     place, seg, pre, steps, log_rate, cum, reach, to_end, rows, cols, same = block_terms(
-        base, ends_ref, hw_ref, pad[...]
+        base, ends_ref, hw_ref, xr_ref[:, CH:XR]
     )
     masks = [lag_mask(place, seg, ends_ref, -k) for k in range(1, 4)]
     for c in range(CH // LANES):
         cs = slice(LANES * c, LANES * (c + 1))
-        now = zx_ref[:, INNER + LANES * c : INNER + LANES * (c + 1)]
+        now = xr_ref[:, cs]
         buf[8 : 8 + SPAN, cs] = now
         conv = par_ref[4:5, cs] + par_ref[3:4, cs] * now
         for k in range(1, 4):
@@ -193,7 +192,7 @@
         state[:, gs] = before * reach_g[SPAN - 1 : SPAN, :] + mm(
             bm_t, xd * raw_dot(to_end2, spread, NN), NN, PASS_STATE
         )
-        z = zx_ref[:, gs]
+        z = z_ref[:, gs]
         gated = (scan + gain_ref[1:2, gs] * x) * (z * sigmoid(z))
         yg[:, gs] = gated
         gated = gated * gated
@@ -205,34 +204,34 @@
 
 
 def backward_kernel(
-    ends_ref, zx_ref, halo_ref, dgn_ref, ys_ref, st_ref, par_ref, gain_ref, hw_ref, spread_ref, gather_ref,
-    dzx_ref, dpar_ref, dgain_ref, dhw_ref,
-    buf, act, slope, dact, dcv, pad, rgrad, yg, dgram,
+    top, ends_ref, z_ref, xr_ref, halo_ref, dgn_ref, ys_ref, st_ref, par_ref, gain_ref, hw_ref, spread_ref, gather_ref,
+    *refs,
 ):
+    (
+        rgrad_in, dcv_in, dz_ref, dxr_ref, dpar_ref, dgain_ref, dhw_ref, rgrad, dcv_out,
+        buf, act, slope, dact, dcv, yg, dgram,
+    ) = refs[-16:]
     step = pl.program_id(0)
-    block = pl.num_programs(0) - 1 - step
+    block = top - step
     base = block * SPAN
 
     @pl.when(step == 0)
     def _():
-        dcv[0:8, :] = jnp.zeros((8, CH), F32)
-        rgrad[...] = jnp.zeros_like(rgrad)
-        pad[...] = jnp.zeros_like(pad)
+        dcv[0:8, :] = dcv_in[...]
+        rgrad[...] = rgrad_in[...]
         dpar_ref[...] = jnp.zeros_like(dpar_ref)
         dgain_ref[...] = jnp.zeros_like(dgain_ref)
         dhw_ref[...] = jnp.zeros_like(dhw_ref)
 
-    pad[:, 0:NHEADS] = zx_ref[:, INNER + CH : P_SIZE]
     place, seg, pre, steps, log_rate, cum, reach, to_end, rows, cols, same = block_terms(
-        base, ends_ref, hw_ref, pad[...]
+        base, ends_ref, hw_ref, xr_ref[:, CH:XR]
     )
     back_masks = [lag_mask(place, seg, ends_ref, -k) for k in range(1, 4)]
     fore_masks = [lag_mask(place, seg, ends_ref, k) for k in range(1, 4)]
     for c in range(CH // LANES):
         cs = slice(LANES * c, LANES * (c + 1))
-        zs = slice(INNER + LANES * c, INNER + LANES * (c + 1))
-        now = zx_ref[:, zs]
-        buf[0:8, cs] = halo_ref[:, zs]
+        now = xr_ref[:, cs]
+        buf[0:8, cs] = halo_ref[:, cs]
         buf[8 : 8 + SPAN, cs] = now
         conv = par_ref[4:5, cs] + par_ref[3:4, cs] * now
         for k in range(1, 4):
@@ -255,7 +254,7 @@
     overlap = jnp.zeros((SPAN, LANES), F32)
     for g in range(GROUPS):
         gs = slice(GROUP * g, GROUP * (g + 1))
-        z = zx_ref[:, gs]
+        z = z_ref[:, gs]
         gated = (ys_ref[:, gs] + gain_ref[1:2, gs] * act[:, gs]) * (z * sigmoid(z))
         yg[:, gs] = gated
         shared = gated * (dgn_ref[:, gs] * gain_ref[0:1, gs])
@@ -277,7 +276,7 @@
         spread = spread_ref[:, gs]
         gather = gather_ref[gs, :]
         x = act[:, gs]
-        z = zx_ref[:, gs]
+        z = z_ref[:, gs]
         gate = sigmoid(z)
         soft = z * gate
         scan = ys_ref[:, gs]
@@ -288,7 +287,7 @@
         dgated = scale * (dgn * gain_ref[0:1, gs]) - gated * pull
         dgain_ref[0:8, gs] += partial8(dgn * (gated * scale))
         dy = dgated * soft
-        dzx_ref[:, gs] = (dgated * y * (gate * (1.0 + z * (1.0 - gate)))).astype(BF16)
+        dz_ref[:, gs] = (dgated * y * (gate * (1.0 + z * (1.0 - gate)))).astype(BF16)
         dgain_ref[8:16, gs] += partial8(dy * x)
         steps_g = raw_dot(steps2, spread, NN)
         reach_g = raw_dot(reach2, spread, NN)
@@ -333,7 +332,7 @@
     dpre = dsteps * sigmoid(pre)
     dhw_ref[0:8, :] += partial8(dpre)
     dhw_ref[8:16, :] += partial8(drate * log_rate)
-    dzx_ref[:, INNER + CH : P_SIZE] = dpre[:, :NHEADS].astype(BF16)
+    dxr_ref[:, CH:XR] = dpre.astype(BF16)
 
     for c in range(CH // LANES):
         cs = slice(LANES * c, LANES * (c + 1))
@@ -347,7 +346,8 @@
             dpar_ref[24 - 8 * k : 32 - 8 * k, cs] += partial8(
                 dconv * (back_masks[k - 1] * buf[8 - k : 8 - k + SPAN, cs])
             )
-        dzx_ref[:, INNER + LANES * c : INNER + LANES * (c + 1)] = dxbc.astype(BF16)
+        dxr_ref[:, cs] = dxbc.astype(BF16)
+    dcv_out[...] = dcv[0:8, :]
 
 
 def spread_matrices():
@@ -374,14 +374,14 @@
 SMEM = pl.BlockSpec(memory_space=pltpu.SMEM)
 
 
-def mixer_forward(ends, zx, par, gain, hw, spread):
-    tokens = zx.shape[0]
+def mixer_forward(ends, z, xr, par, gain, hw, spread):
+    tokens = z.shape[0]
     blocks = tokens // SPAN
     rows = lambda width: pl.BlockSpec((SPAN, width), lambda i: (i, 0))
     return pl.pallas_call(
         forward_kernel,
         grid=(blocks,),
-        in_specs=[SMEM, rows(P_SIZE), whole((8, CH)), whole((8, INNER)), whole((8, LANES)), whole((256, INNER))],
+        in_specs=[SMEM, rows(INNER), rows(XR), whole((8, CH)), whole((8, INNER)), whole((8, LANES)), whole((256, INNER))],
         out_specs=[rows(INNER), rows(INNER), pl.BlockSpec((1, STATE, INNER), lambda i: (i, 0, 0))],
         out_shape=[
             jax.ShapeDtypeStruct((tokens, INNER), BF16),
@@ -391,59 +391,77 @@
         scratch_shapes=[
             pltpu.VMEM((SPAN + 8, CH), F32),
             pltpu.VMEM((SPAN, CH), F32),
-            pltpu.VMEM((SPAN, LANES), F32),
             pltpu.VMEM((STATE, INNER), F32),
             pltpu.VMEM((SPAN, INNER), F32),
         ],
         compiler_params=pltpu.CompilerParams(vmem_limit_bytes=VMEM_LIMIT),
         cost_estimate=pl.CostEstimate(flops=20_000_000_000, bytes_accessed=30_000_000, transcendentals=6_000_000),
         name="mixer_forward",
-    )(ends, zx, par, gain, hw, spread)
-
-
-def mixer_backward(ends, zx, dgn, ys, st, par, gain, hw, spread, gather):
-    tokens = zx.shape[0]
-    blocks = tokens // SPAN
-    back = lambda width: pl.BlockSpec((SPAN, width), lambda i: (blocks - 1 - i, 0))
-    halo = pl.BlockSpec((8, P_SIZE), lambda i: (jnp.maximum((blocks - 1 - i) * (SPAN // 8) - 1, 0), 0))
+    )(ends, z, xr, par, gain, hw, spread)
+
+
+def mixer_backward(ends, z, xr, dgn, ys, st, par, gain, hw, spread, gather, first, last, earlier=None):
+    tokens = z.shape[0]
+    top = last - 1
+    back = lambda width: pl.BlockSpec((SPAN, width), lambda i: (top - i, 0))
+    halo = pl.BlockSpec((8, XR), lambda i: (jnp.maximum((top - i) * (SPAN // 8) - 1, 0), 0))
+    if earlier is None:
+        held, carried = [], [jnp.zeros((STATE, INNER), F32), jnp.zeros((8, CH), F32)]
+    else:
+        held, carried = list(earlier[:2]), list(earlier[5:])
     return pl.pallas_call(
-        backward_kernel,
-        grid=(blocks,),
+        partial(backward_kernel, top),
+        grid=(last - first,),
         in_specs=[
             SMEM,
-            back(P_SIZE),
+            back(INNER),
+            back(XR),
             halo,
             back(INNER),
             back(INNER),
-            pl.BlockSpec((1, STATE, INNER), lambda i: (blocks - 1 - i, 0, 0)),
+            pl.BlockSpec((1, STATE, INNER), lambda i: (top - i, 0, 0)),
             whole((8, CH)),
             whole((8, INNER)),
             whole((8, LANES)),
             whole((256, INNER)),
             whole((INNER, LANES)),
+        ]
+        + [pl.BlockSpec(memory_space=pl.ANY)] * len(held)
+        + [whole((STATE, INNER)), whole((8, CH))],
+        out_specs=[
+            back(INNER),
+            back(XR),
+            whole((40, CH)),
+            whole((16, INNER)),
+            whole((16, LANES)),
+            whole((STATE, INNER)),
+            whole((8, CH)),
         ],
-        out_specs=[back(P_SIZE), whole((40, CH)), whole((16, INNER)), whole((16, LANES))],
         out_shape=[
-            jax.ShapeDtypeStruct((tokens, P_SIZE), BF16),
+            jax.ShapeDtypeStruct((tokens, INNER), BF16),
+            jax.ShapeDtypeStruct((tokens, XR), BF16),
             jax.ShapeDtypeStruct((40, CH), F32),
             jax.ShapeDtypeStruct((16, INNER), F32),
             jax.ShapeDtypeStruct((16, LANES), F32),
+            jax.ShapeDtypeStruct((STATE, INNER), F32),
+            jax.ShapeDtypeStruct((8, CH), F32),
         ],
+        input_output_aliases={12 + k: k for k in range(len(held))},
         scratch_shapes=[
             pltpu.VMEM((SPAN + 8, CH), F32),
             pltpu.VMEM((SPAN, CH), F32),
             pltpu.VMEM((SPAN, CH), F32),
             pltpu.VMEM((SPAN, CH), F32),
             pltpu.VMEM((SPAN + 8, CH), F32),
-            pltpu.VMEM((SPAN, LANES), F32),
-            pltpu.VMEM((STATE, INNER), F32),
             pltpu.VMEM((SPAN, INNER), F32),
             pltpu.VMEM((SPAN, 2 * SPAN), F32),
         ],
         compiler_params=pltpu.CompilerParams(vmem_limit_bytes=VMEM_LIMIT),
-        cost_estimate=pl.CostEstimate(flops=60_000_000_000, bytes_accessed=60_000_000, transcendentals=9_000_000),
+        cost_estimate=pl.CostEstimate(
+            flops=7_500_000_000 * (last - first), bytes_accessed=6_000_000 * (last - first), transcendentals=0
+        ),
         name="mixer_backward",
-    )(ends, zx, zx, dgn, ys, st, par, gain, hw, spread, gather)
+    )(ends, z, xr, xr, dgn, ys, st, par, gain, hw, spread, gather, *held, *carried)
 
 
 def finish_params(dpar, dgain, dhw):
@@ -454,6 +472,91 @@
     return jnp.concatenate([dgate, dtaps]), jnp.concatenate([dh, dskip[None]], axis=0)
 
 
+class Net:
+    def __init__(self, mesh):
+        side = round((mesh.shape["dp"] // 2) ** 0.5)
+        self.sizes = {"y": mesh.shape["dp"] // (2 * side), "x": side, "core": 2, "z": mesh.shape["fsdp"]}
+        self.order = ("y", "x", "core", "z")
+
+    def coordinates(self):
+        at = lax.axis_index("dp")
+        return {
+            "y": at // (2 * self.sizes["x"]),
+            "x": (at // 2) % self.sizes["x"],
+            "core": at % 2,
+            "z": lax.axis_index("fsdp"),
+        }
+
+    def shift(self, value, axis, by):
+        n = self.sizes[axis]
+        if axis == "z":
+            return lax.ppermute(value, "fsdp", [(i, (i + by) % n) for i in range(n)])
+        inner = {"y": 2 * self.sizes["x"], "x": 2, "core": 1}[axis]
+        pairs = []
+        for i in range(2 * self.sizes["y"] * self.sizes["x"]):
+            at = (i // inner) % n
+            pairs.append((i, i + ((at + by) % n - at) * inner))
+        return lax.ppermute(value, "dp", pairs)
+
+    def gather_axis(self, value, axis, at):
+        n, dim = self.sizes[axis], self.order.index(axis)
+        pieces = [value] + [self.shift(value, axis, d) for d in range(1, n)]
+        rows = []
+        for j in range(n):
+            row = pieces[-j % n]
+            for i in range(1, n):
+                row = jnp.where(at == i, pieces[(i - j) % n], row)
+            rows.append(row)
+        return jnp.concatenate(rows, axis=dim)
+
+    def gather(self, shard, axes):
+        at = self.coordinates()
+        value = shard[None, None, None, None]
+        for axis in axes:
+            value = self.gather_axis(value, axis, at[axis])
+        return value.reshape(-1, shard.shape[1])
+
+    def shift_xy(self, value, dy, dx):
+        ny, nx = self.sizes["y"], self.sizes["x"]
+        pairs = []
+        for y in range(ny):
+            for x in range(nx):
+                for c in range(2):
+                    pairs.append(((y * nx + x) * 2 + c, ((y + dy) % ny * nx + (x + dx) % nx) * 2 + c))
+        return lax.ppermute(value, "dp", pairs)
+
+    def steps_xy(self):
+        return [(dy, dx) for dy in range(self.sizes["y"]) for dx in range(self.sizes["x"]) if dy or dx]
+
+    def scatter_axis(self, value, axis, at, wire=F32):
+        if axis == "xy":
+            ny, nx = self.sizes["y"], self.sizes["x"]
+
+            def block(dy, dx):
+                row = lax.dynamic_index_in_dim(value, (at["y"] + dy) % ny, 0)
+                return lax.dynamic_index_in_dim(row, (at["x"] + dx) % nx, 1)
+
+            total = block(0, 0)
+            for dy, dx in self.steps_xy():
+                total = total + self.shift_xy(block(dy, dx).astype(wire), dy, dx).astype(F32)
+            return total
+        n, dim = self.sizes[axis], self.order.index(axis)
+        total = lax.dynamic_index_in_dim(value, at[axis], dim)
+        for d in range(1, n):
+            part = lax.dynamic_index_in_dim(value, (at[axis] + d) % n, dim)
+            total = total + self.shift(part.astype(wire), axis, d).astype(F32)
+        return total
+
+    def blocks(self, whole):
+        s = self.sizes
+        return whole.reshape(s["y"], s["x"], s["core"], s["z"], -1, whole.shape[1])
+
+    def total(self, value):
+        value = value + self.shift(value, "core", 1)
+        value = value + sum(self.shift_xy(value, dy, dx) for dy, dx in self.steps_xy())
+        return value + sum(self.shift(value, "z", d) for d in range(1, self.sizes["z"]))
+
+
 AXES = ("dp", "fsdp")
 
 
@@ -461,11 +564,17 @@
     return values * lax.rsqrt(jnp.mean(values * values, axis=-1, keepdims=True) + EPSILON) * scales
 
 
+def side_by_side(value):
+    r = value.shape[-2] // 2
+    return jnp.concatenate([value[..., :r, :], value[..., r:, :]], axis=-1)
+
+
 def norm_part(stream, gain):
     return rms_norm(stream, gain[None, :])
 
 
 def on_device(
+    net,
     hidden_in,
     cotangent,
     seq_lengths,
@@ -489,43 +598,98 @@
     ends = jnp.stack([e0, e1, e2, e3])
     valid = (jnp.arange(token_count, dtype=jnp.int32) < e3).astype(F32)
     spread, gather = spread_matrices()
-    vector_full = lax.all_gather(vector_weight.astype(BF16), AXES, axis=1, tiled=True).astype(F32)
+    shard_rows = in_weight.shape[1]
+    in_low = jnp.pad(in_weight.astype(BF16), ((0, 0), (0, 0), (0, INNER + XR - P_SIZE)))
+    out_low = out_weight.astype(BF16).reshape(LAYERS, 2, shard_rows, D)
+    vec_low = vector_weight.astype(BF16).reshape(-1)
+    vec_low = jnp.pad(vec_low, (0, shard_rows * LANES - vec_low.shape[0])).reshape(shard_rows, LANES)
+    first = net.gather(jnp.concatenate([in_low[0, :, INNER:], vec_low], axis=1), ("z", "x", "y", "core"))
+    first_z = net.gather(in_low[0, :, :INNER], ("z", "y", "x", "core"))
+    rest = lax.all_gather(
+        jnp.concatenate([out_low[0, 0], out_low[0, 1], in_low[1], out_low[1, 0], out_low[1, 1]], axis=1),
+        AXES,
+        axis=0,
+        tiled=True,
+    )
+    devices = rest.shape[0] // shard_rows
+
+    def out_rows(columns):
+        return columns.reshape(devices, shard_rows, 2, D).swapaxes(1, 2).reshape(INNER, D)
+
+    in_from = 2 * D
+    out_from = in_from + INNER + XR
+    ins = [
+        (first_z, first[:, :XR]),
+        (rest[:, in_from : in_from + INNER], rest[:, in_from + INNER : out_from]),
+    ]
+    outs = [out_rows(rest[:, :in_from]), out_rows(rest[:, out_from:])]
+    vector_full = first[:, XR:].reshape(devices, -1)[:, : LAYERS * VEC // devices]
+    vector_full = vector_full.reshape(devices, LAYERS, -1).swapaxes(0, 1).reshape(LAYERS, VEC).astype(F32)
     stream = hidden_in.astype(F32)
     stored = []
     for l in range(LAYERS):
-        full_in = lax.all_gather(in_weight[l].astype(BF16), AXES, axis=0, tiled=True)
-        full_out = lax.all_gather(out_weight[l].astype(BF16), AXES, axis=0, tiled=True)
         tables = kernel_params(vector_full[l], head_weight[l])
         normed, norm_pull = jax.vjp(norm_part, stream, vector_full[l, :D])
         normed = normed.astype(BF16)
-        zx = jnp.dot(normed, full_in, preferred_element_type=F32)
-        gn, ys, st = mixer_forward(ends, zx, *tables, spread)
-        stream = stream + jnp.dot(gn, full_out, preferred_element_type=F32)
-        stored.append((norm_pull, normed, zx, gn, ys, st, tables, full_in, full_out))
+        z = jnp.dot(normed, ins[l][0], preferred_element_type=F32)
+        xr = jnp.dot(normed, ins[l][1], preferred_element_type=F32)
+        gn, ys, st = mixer_forward(ends, z, xr, *tables, spread)
+        stream = stream + jnp.dot(gn, outs[l], preferred_element_type=F32)
+        stored.append((norm_pull, normed, z, xr, gn, ys, st, tables))
     layer_out = stream.astype(BF16)
     flowing = cotangent.astype(F32) * valid[:, None]
-    in_parts = [None] * LAYERS
-    out_parts = [None] * LAYERS
-    vector_parts = [None] * LAYERS
-    head_parts = [None] * LAYERS
+    arrived = [None] * LAYERS
+    small_parts = [None] * LAYERS
+    travelling = []
+    at = net.coordinates()
+    blocks = token_count // SPAN
     for l in reversed(range(LAYERS)):
-        norm_pull, normed, zx, gn, ys, st, tables, full_in, full_out = stored[l]
+        norm_pull, normed, z, xr, gn, ys, st, tables = stored[l]
         gb = flowing.astype(BF16)
         grad_out = jnp.einsum("te,td->ed", gn, gb, preferred_element_type=F32)
-        dgn = jnp.einsum("td,ed->te", gb, full_out, preferred_element_type=F32)
-        dzx, dpar, dgain, dhw = mixer_backward(ends, zx, dgn, ys, st, *tables, spread, gather)
-        grad_in = jnp.einsum("td,tp->dp", normed, dzx, preferred_element_type=F32)
-        dxn = jnp.einsum("tp,dp->td", dzx, full_in, preferred_element_type=F32)
+        gb, grad_out = lax.optimization_barrier((gb, grad_out))
+        out_sum = side_by_side(net.scatter_axis(net.blocks(grad_out), "core", at))
+        travelling = jnp.concatenate(travelling + [out_sum], axis=-1)
+        dgn = jnp.einsum("td,ed->te", gb, outs[l], preferred_element_type=F32)
+        dgn, travelling = lax.optimization_barrier((dgn, travelling))
+        travelling = net.scatter_axis(travelling, "xy", at, BF16)
+        dz, dxr, *sums = mixer_backward(ends, z, xr, dgn, ys, st, *tables, spread, gather, 0, blocks)[:5]
+        dz, dxr, travelling = lax.optimization_barrier((dz, dxr, travelling))
+        arrived[l] = net.scatter_axis(travelling, "z", at, BF16)
+        grad_x = jnp.einsum("td,tp->dp", normed, dxr, preferred_element_type=F32)
+        dz, dxr, grad_x = lax.optimization_barrier((dz, dxr, grad_x))
+        grad_z = jnp.einsum("td,tp->dp", normed, dz, preferred_element_type=F32)
+        dz, dxr, grad_z = lax.optimization_barrier((dz, dxr, grad_z))
+        travelling = [net.scatter_axis(net.blocks(g), "core", at) for g in (grad_x, grad_z)]
+        dxn = jnp.einsum("tp,dp->td", dz, ins[l][0], preferred_element_type=F32) + jnp.einsum(
+            "tp,dp->td", dxr, ins[l][1], preferred_element_type=F32
+        )
         grad_stream, dnorm = norm_pull(dxn)
         flowing = flowing + grad_stream
-        dvec, head_parts[l] = finish_params(dpar, dgain, dhw)
-        vector_parts[l] = jnp.concatenate([dnorm, dvec])
-        in_parts[l] = lax.psum_scatter(grad_in, AXES, scatter_dimension=0, tiled=True)
-        out_parts[l] = lax.psum_scatter(grad_out, AXES, scatter_dimension=0, tiled=True)
+        dvec, dhead = finish_params(*sums)
+        small_parts[l] = jnp.concatenate([dnorm, dvec, dhead.reshape(-1)])
+    travelling_late = travelling
+    for axis in ("xy", "z"):
+        travelling = [net.scatter_axis(v, axis, at, BF16) for v in travelling]
+    flat = [v.reshape(-1, v.shape[-1]) for v in (arrived[1], arrived[0], *travelling)]
+    in_parts = [
+        jnp.concatenate([flat[3], flat[2]], axis=1)[:, :P_SIZE],
+        jnp.concatenate([flat[1][:, XR : XR + INNER], flat[1][:, :XR]], axis=1)[:, :P_SIZE],
+    ]
+    out_parts = [
+        jnp.concatenate([v[:, -2 * D : -D], v[:, -D:]], axis=0) for v in (flat[1], flat[0])
+    ]
+    late, _ = lax.optimization_barrier(((in_weight, out_weight, vector_weight), travelling_late))
+    weight_squares = [jnp.sum(w * w, axis=tuple(range(1, w.ndim))) for w in late]
+    small = jnp.stack(small_parts)
+    small = net.total(jnp.pad(small, ((0, 0), (0, -small.shape[1] % LANES))).reshape(-1, LANES))
+    small = small.reshape(LAYERS, -1)
+    head_total = small[:, VEC : VEC + 3 * NHEADS].reshape(LAYERS, 3, NHEADS)
+    share = VEC // devices
+    mine = lax.axis_index("dp") * lax.axis_size("fsdp") + lax.axis_index("fsdp")
+    grad_vector = lax.dynamic_slice(small, (0, mine * share), (LAYERS, share))
     grad_in = jnp.stack(in_parts)
     grad_out = jnp.stack(out_parts)
-    grad_vector = lax.psum_scatter(jnp.stack(vector_parts), AXES, scatter_dimension=1, tiled=True)
-    head_part = jnp.stack(head_parts)
     squares_in = grad_in * grad_in
     squares_out = grad_out * grad_out
     row_in = MOMENT_DECAY * in_row_moment + (1.0 - MOMENT_DECAY) * jnp.mean(squares_in, axis=2)
@@ -536,9 +700,7 @@
         [
             jnp.sum(row_in, axis=1),
             jnp.sum(row_out, axis=1),
-            jnp.sum(in_weight * in_weight, axis=(1, 2)),
-            jnp.sum(out_weight * out_weight, axis=(1, 2)),
-            jnp.sum(vector_weight * vector_weight, axis=1),
+            *weight_squares,
             jnp.sum(vector_update * vector_update, axis=1),
         ],
         axis=1,
@@ -548,15 +710,17 @@
         jnp.sum(squares_out, axis=1),
         jnp.sum(squares_in / row_in[:, :, None], axis=1),
         jnp.sum(squares_out / row_out[:, :, None], axis=1),
-        head_part.reshape(LAYERS, 3 * NHEADS),
         totals,
     )
-    widths = [v.shape[1] for v in local]
-    summed = lax.psum(jnp.concatenate(local, axis=1), AXES)
-    column_in, column_out, scaled_in, scaled_out, head_total, totals = jnp.split(
-        summed, [sum(widths[: i + 1]) for i in range(5)], axis=1
-    )
-    head_total = head_total.reshape(LAYERS, 3, NHEADS)
+    edges = [0]
+    for v in local:
+        edges.append(edges[-1] + v.shape[1])
+    summed = jnp.concatenate(local, axis=1)
+    summed = jnp.pad(summed, ((0, 0), (0, -edges[-1] % LANES))).reshape(-1, LANES)
+    summed = net.total(summed).reshape(LAYERS, -1)
+    column_in, column_out, scaled_in, scaled_out, totals = [
+        summed[:, a:b] for a, b in zip(edges[:-1], edges[1:])
+    ]
     col_in = MOMENT_DECAY * in_col_moment + (1.0 - MOMENT_DECAY) * column_in / D
     col_out = MOMENT_DECAY * out_col_moment + (1.0 - MOMENT_DECAY) * column_out / INNER
     mean_in = totals[:, 0] / D
@@ -613,7 +777,7 @@
     vec = P(None, AXES)
     one = P()
     return jax.shard_map(
-        on_device,
+        partial(on_device, Net(mesh)),
         mesh=mesh,
         in_specs=(rows, rows, rows, mat, mat, vec, one, vec, one, vec, one, vec, one),
         out_specs=(

time: 1290 us -> 574 us (0.44)
  waiting for transfers between devices: 842 us -> 73.4 us
  blocking collectives: 70.6 us -> 0 us
  starting transfers between devices: 0.87 us -> 65.4 us
  local copies, waits for them, and re-layouts: 22.7 us -> 72.6 us
  other arithmetic: 34.4 us -> 69.8 us
  matrix products: 110 us -> 86.2 us
    unnamed x13 -> x1, waiting for transfers between devices: 401 us -> 0.02 us
    reduce_scatter x2 -> x0, waiting for transfers between devices: 222 us -> none  [on_device(): lax.psum_scatter(grad_out, AXES, scatter_dimension=0, tiled=True)]
    psum x1 -> x0, waiting for transfers between devices: 110 us -> none  [on_device(): summed = lax.psum(jnp.concatenate(local, axis=1), AXES)]
    all_gather x4 -> x1, waiting for transfers between devices: 109 us -> 0.02 us  [on_device(): lax.all_gather(jnp.concatenate([out_low[0, 0], out_low[0, 1], in_low[1],...]
    ppermute x0 -> x56, waiting for transfers between devices: none -> 73.3 us  [the longest x18 26.2 us: shift_xy(): return lax.ppermute(value, 'dp', pairs)]
    all_gather x1 -> x0, blocking collectives: 70.6 us -> none  [on_device(): lax.all_gather(vector_weight.astype(BF16), AXES, axis=1, tiled=True)]
    ppermute x0 -> x56, starting transfers between devices: none -> 65.3 us  [the longest x24 35.7 us: shift(): return lax.ppermute(value, 'fsdp', [(i, (i + by) % n) for i in range(n)])]
    dot_general x10 -> x16, matrix products: 96.1 us -> 78.5 us  [the longest x2 12.1 us: on_device(): dgn = jnp.einsum('td,ed->te', gb, outs[l], preferred_element_type=F32)]
  transfers between devices with their start and end apart: 10 -> 57, of which waited for: 9 -> 18; matrix products, arithmetic and copies ran while one was open for 8% -> 20% of each run, Pallas kernels for 3% -> 27%
where the time goes in v2:
time: 574 us; the launch traced here: 569 us
  Pallas kernels  183 us (32%)
  matrix products  86.2 us (15%)
  waiting for transfers between devices  73.4 us (13%)
  local copies, waits for them, and re-layouts  72.6 us (13%)
  other arithmetic  69.8 us (12%)
  starting transfers between devices  65.4 us (11%)
  between operations  18.4 us (3%)
    pallas_call x2, Pallas kernels, mixer_backward(): pl.pallas_call(partial(backward_kernel, top), grid=(last - first,), in_sp...  119 us
    pallas_call x2, Pallas kernels, mixer_forward(): pl.pallas_call(forward_kernel, grid=(blocks,), in_specs=[SMEM, rows(INNER...  64.4 us
    ppermute x24, starting transfers between devices, shift(): return lax.ppermute(value, 'fsdp', [(i, (i + by) % n) for i in range(n)])  35.7 us
    unnamed x174, local copies, waits for them, and re-layouts  30.2 us
    ppermute x18, waiting for transfers between devices, shift_xy(): return lax.ppermute(value, 'dp', pairs)  26.2 us
    ppermute x14, waiting for transfers between devices, shift(): return lax.ppermute(value, 'dp', pairs)  26.1 us
    ppermute x18, starting transfers between devices, shift_xy(): return lax.ppermute(value, 'dp', pairs)  21.7 us
    ppermute x24, waiting for transfers between devices, shift(): return lax.ppermute(value, 'fsdp', [(i, (i + by) % n) for i in range(n)])  21 us
  transfers between devices with their start and end apart: 57, of which 18 were waited for; matrix products, arithmetic and copies ran while one was open for 20% of the time, Pallas kernels for 27%

profile of v2, /device:TPU:0, one launch (start us, length us, event | category | flops | bytes accessed | tf_op | source)
XLA Modules:
  0.0 569.2 jit_solution(15624407961024147585)
XLA Ops:
  10.3 5.1 collective-permute-start.6
  39.9 14.8 %collective-permute-done.3 = bf16[1,1,1,4,24,2048]{5,4,3,2,1,0:T(8,128)(2,1)S(1)} collective-permute-done((bf16[1,1,1,4,24,2048]{5,4,3,2,1,0:T(8,128)(2,1)S(1)}, bf16[1,1,1,4,24,2048]{5,4,3,2,1,0:T(8,128)(2,1)S(1)}, u32[]{:S(2)}, u32[]{:S(2)}) %collective-permute-start.3) | collective-permute-done | bytes 393248 | tf_op jit(solution)/shard_map/ppermute | solution.py:499
  57.2 9.6 %collective-permute-done.10 = bf16[2,1,1,4,24,1536]{5,4,3,2,1,0:T(8,128)(2,1)S(1)} collective-permute-done((bf16[2,1,1,4,24,1536]{5,4,3,2,1,0:T(8,128)(2,1)S(1)}, bf16[2,1,1,4,24,1536]{5,4,3,2,1,0:T(8,128)(2,1)S(1)}, u32[]{:S(2)}, u32[]{:S(2)}) %collective-permute-start.10) | collective-permute-done | bytes 589856 | tf_op jit(solution)/shard_map/ppermute | solution.py:499
  87.6 6.5 %fusion.66.z_ref = f32[1024,1536]{1,0:T(8,128)} fusion(bf16[768,1536]{1,0:T(8,128)(2,1)} %bitcast.158, bf16[1024,768]{0,1:T(8,128)(2,1)S(1)} %copy.110, f32[768]{0:T(1024)S(1)} %get-tuple-element.210, f32[1024]{0:T(1024)S(1)} %fusion.43), kind=kOutput, calls=%fused_computation.252 | convolution fusion | flops 2419064832 | bytes 10230784 | tf_op jit(solution)/shard_map/dot_general | solution.py:634
  94.2 5.8 %fusion.15.xr_ref.halo_ref = f32[1024,1920]{1,0:T(8,128)} fusion(bf16[768,2048]{1,0:T(8,128)(2,1)S(1)} %bitcast.156, bf16[1024,768]{0,1:T(8,128)(2,1)S(1)} %copy.110, f32[768]{0:T(1024)S(1)} %get-tuple-element.210, f32[1024]{0:T(1024)S(1)} %fusion.43), kind=kOutput, calls=%fused_computation.32 | convolution fusion | flops 3023044608 | bytes 12394496 | tf_op jit(solution)/shard_map/dot_general | solution.py:635
  100.0 32.1 %mixer_forward.2 = (bf16[1024,1536]{1,0:T(8,128)(2,1)}, f32[1024,1536]{1,0:T(8,128)}, f32[8,128,1536]{2,1,0:T(8,128)}) custom-call(s32[4]{0:T(128)} %pad_add_fusion.ends_ref, f32[1024,1536]{1,0:T(8,128)} %fusion.66.z_ref, f32[1024,1920]{1,0:T(8,128)} %fusion.15.xr_ref.halo_ref, f32[8,1792]{1,0:T(8,128)} %concatenate.89.par_ref, ...), custom_call_target="tpu_custom_call" | custom-call | flops 20000000000 | bytes 30000000 | tf_op jit(solution)/shard_map/mixer_forward/pallas_call | solution.py:381
  132.1 5.0 fusion.77
  137.1 5.1 reshape.357
  148.8 4.7 fusion.19.z_ref
  153.6 5.7 %fusion.11.xr_ref.halo_ref = f32[1024,1920]{1,0:T(8,128)} fusion(bf16[1024,768]{0,1:T(8,128)(2,1)S(1)} %multiply_convert_fusion, bf16[768,6528]{1,0:T(8,128)(2,1)S(1)} %bitcast.165), kind=kOutput, calls=%fused_computation.28 | convolution fusion | flops 3019898880 | bytes 12386304 | tf_op jit(solution)/shard_map/dot_general | solution.py:635
  159.3 32.3 %mixer_forward.3 = (bf16[1024,1536]{1,0:T(8,128)(2,1)}, f32[1024,1536]{1,0:T(8,128)}, f32[8,128,1536]{2,1,0:T(8,128)}) custom-call(s32[4]{0:T(128)} %pad_add_fusion.ends_ref, f32[1024,1536]{1,0:T(8,128)} %fusion.19.z_ref, f32[1024,1920]{1,0:T(8,128)} %fusion.11.xr_ref.halo_ref, f32[8,1792]{1,0:T(8,128)} %concatenate.94.par_ref, ...), custom_call_target="tpu_custom_call" | custom-call | flops 20000000000 | bytes 30000000 | tf_op jit(solution)/shard_map/mixer_forward/pallas_call | solution.py:381
  191.5 5.1 fusion.84
  203.5 6.0 %reshape.360 = bf16[32,24,2,768]{3,2,1,0:T(2,128)(2,1)} reshape(bf16[768,1536]{1,0:T(8,128)(2,1)} %get-tuple-element.239) | data formatting | bytes 4718592 | tf_op jit(solution)/shard_map/reshape | solution.py:617
  213.0 3.8 add_convert_fusion
  219.4 7.4 %fusion.85.dgn_ref = f32[1024,1536]{1,0:T(8,128)} fusion(bf16[1024,768]{0,1:T(8,128)(2,1)} %fusion.8, bf16[1536,768]{1,0:T(8,128)(2,1)} %bitcast.163), kind=kOutput, calls=%fused_computation.267 | convolution fusion | flops 2415919104 | bytes 10223616 | tf_op jit(solution)/shard_map/td,ed->te/dot_general | solution.py:653
  237.5 59.8 %mixer_backward.2 = (bf16[1024,1536]{1,0:T(8,128)(2,1)}, bf16[1024,1920]{1,0:T(8,128)(2,1)}, f32[40,1792]{1,0:T(8,128)}, f32[16,1536]{1,0:T(8,128)}, f32[16,128]...) custom-call(s32[4]{0:T(128)} %pad_add_fusion.ends_ref, f32[1024,1536]{1,0:T(8,128)} %fusion.19.z_ref, ...), custom_call_target="tpu_custom_call" | custom-call | flops 60000002048 | bytes 48000000 | tf_op jit(solution)/shard_map/mixer_backward/pallas_call | solution.py:412
  301.7 6.1 %fusion.86 = f32[768,1920]{1,0:T(8,128)S(1)} fusion(bf16[1024,768]{0,1:T(8,128)(2,1)} %copy-done.33, bf16[1024,1920]{1,0:T(8,128)(2,1)} %get-tuple-element.81), kind=kOutput, calls=%fused_computation.268 | convolution fusion | flops 3019898880 | bytes 11403264 | tf_op jit(solution)/shard_map/td,tp->dp/dot_general | solution.py:659
  310.6 5.1 fusion.9
  315.7 5.0 multiply_reduce_fusion
  328.3 6.1 %collective-permute-start.41 = (bf16[1,1,1,1,24,1536]{5,4,3,2,1,0:T(8,128)(2,1)S(1)}, bf16[1,1,1,1,24,1536]{5,4,3,2,1,0:T(8,128)(2,1)S(1)}, u32[]{:S(2)}, u32[]{:S(2)}) collective-permute-start(bf16[1,1,1,1,24,1536]{5,4,3,2,1,0:T(8,128)(2,1)S(1)} %get-tuple-element.274), channel_id=1, source_target_pairs={{0,3},{1,0},{2,1},{3,2},{4,7},{5,4},{6,5},{7,6},{8,11},{9,8},{10,9... | collective-permute-start | bytes 221192 | tf_op jit(solution)/shard_map/ppermute | solution.py:493
  334.3 4.7 fusion.89.dgn_ref
  340.6 5.3 collective-permute-done.40
  356.7 59.2 %mixer_backward.3 = (bf16[1024,1536]{1,0:T(8,128)(2,1)}, bf16[1024,1920]{1,0:T(8,128)(2,1)}, f32[40,1792]{1,0:T(8,128)}, f32[16,1536]{1,0:T(8,128)}, f32[16,128]...) custom-call(s32[4]{0:T(128)} %pad_add_fusion.ends_ref, f32[1024,1536]{1,0:T(8,128)} %fusion.66.z_ref, ...), custom_call_target="tpu_custom_call" | custom-call | flops 60000002048 | bytes 48000000 | tf_op jit(solution)/shard_map/mixer_backward/pallas_call | solution.py:412
  423.1 5.4 fusion.63
  428.5 4.5 fusion.61
  436.5 4.6 fusion.3
  446.0 5.9 %fusion.5 = f32[1024,768]{0,1:T(8,128)} fusion(bf16[1024,768]{0,1:T(8,128)(2,1)} %copy-done.3, f32[1024,768]{0,1:T(8,128)} %get-tuple-element.321, f32[1024]{0:T(1024)S(1)} %multiply_multiply_fusion.2, f32[768]{0:T(1024)S(1)} %copy-done.51, f32[1024]{0:T(1024)S(1)} %copy-done.53, f32[1024,768]{0,1:T(8,128)S(1)} %get-tuple-element.319, ...), kind=kLoop, calls=%fused_computation.13 | loop fusion | flops 11796480 | bytes 15755264 | tf_op jit(solution)/shard_map/add | solution.py:668
  482.6 4.9 collective-permute-done.25
  487.6 5.5 collective-permute-done.24
  507.5 6.9 %collective-permute-done.32 = bf16[1,1,1,4,24,1920]{5,4,3,2,1,0:T(8,128)(2,1)} collective-permute-done((bf16[1,1,1,4,24,1920]{5,4,3,2,1,0:T(8,128)(2,1)}, bf16[1,1,1,4,24,1920]{5,4,3,2,1,0:T(8,128)(2,1)}, u32[]{:S(2)}, u32[]{:S(2)}) %collective-permute-start.32) | collective-permute-done | bytes 368672 | tf_op jit(solution)/shard_map/ppermute | solution.py:526
  514.5 6.0 %collective-permute-done.31 = bf16[1,1,1,4,24,1920]{5,4,3,2,1,0:T(8,128)(2,1)} collective-permute-done((bf16[1,1,1,4,24,1920]{5,4,3,2,1,0:T(8,128)(2,1)}, bf16[1,1,1,4,24,1920]{5,4,3,2,1,0:T(8,128)(2,1)}, u32[]{:S(2)}, u32[]{:S(2)}) %collective-permute-start.31) | collective-permute-done | bytes 368672 | tf_op jit(solution)/shard_map/ppermute | solution.py:526
  529.1 5.7 %collective-permute-done.34 = bf16[1,1,1,1,24,1920]{5,4,3,2,1,0:T(8,128)(2,1)S(1)} collective-permute-done((bf16[1,1,1,1,24,1920]{5,4,3,2,1,0:T(8,128)(2,1)S(1)}, bf16[1,1,1,1,24,1920]{5,4,3,2,1,0:T(8,128)(2,1)S(1)}, u32[]{:S(2)}, u32[]{:S(2)}) %collective-permute-start.34) | collective-permute-done | bytes 92192 | tf_op jit(solution)/shard_map/ppermute | solution.py:493
  (461 shorter events, 200.9 us)
Async XLA Ops:
  7.2 124.9 %all-gather.2.cloned.1.call-start = ((), (), s32[]{:S(2)}) async-start(), calls=%async_computation | async-start | bytes 10340352 | tf_op jit(solution)/shard_map/all_gather | solution.py:608
  10.3 18.0 %collective-permute-start.6 = (bf16[1,1,1,1,24,1536]{5,4,3,2,1,0:T(8,128)(2,1)S(1)}, bf16[1,1,1,1,24,1536]{5,4,3,2,1,0:T(8,128)(2,1)}, u32[]{:S(2)}, u32[]{:S(2)}) collective-permute-start(bf16[1,1,1,1,24,1536]{5,4,3,2,1,0:T(8,128)(2,1)S(1)} %slice_bitcast_fusion), channel_id=1, source_target_pairs={{0,3},{1,0},{2,1},{3,2},{4,7},{5,4},{6,5},{7,6},{8,11},{9,8},{10,9... | collective-permute-start | bytes 221192 | tf_op jit(solution)/shard_map/ppermute | solution.py:493
  15.4 12.9 %collective-permute-start.7 = (bf16[1,1,1,1,24,1536]{5,4,3,2,1,0:T(8,128)(2,1)S(1)}, bf16[1,1,1,1,24,1536]{5,4,3,2,1,0:T(8,128)(2,1)}, u32[]{:S(2)}, u32[]{:S(2)}) collective-permute-start(bf16[1,1,1,1,24,1536]{5,4,3,2,1,0:T(8,128)(2,1)S(1)} %slice_bitcast_fusion), channel_id=1, source_target_pairs={{0,2},{1,3},{2,0},{3,1},{4,6},{5,7},{6,4},{7,5},{8,10},{9,11},{10,... | collective-permute-start | bytes 221192 | tf_op jit(solution)/shard_map/ppermute | solution.py:493
  15.4 12.9 %collective-permute-start.8 = (bf16[1,1,1,1,24,1536]{5,4,3,2,1,0:T(8,128)(2,1)S(1)}, bf16[1,1,1,1,24,1536]{5,4,3,2,1,0:T(8,128)(2,1)}, u32[]{:S(2)}, u32[]{:S(2)}) collective-permute-start(bf16[1,1,1,1,24,1536]{5,4,3,2,1,0:T(8,128)(2,1)S(1)} %slice_bitcast_fusion), channel_id=1, source_target_pairs={{0,1},{1,2},{2,3},{3,0},{4,5},{5,6},{6,7},{7,4},{8,9},{9,10},{10,1... | collective-permute-start | bytes 221192 | tf_op jit(solution)/shard_map/ppermute | solution.py:493
  18.5 12.5 %collective-permute-start = (bf16[1,1,1,1,24,2048]{5,4,3,2,1,0:T(8,128)(2,1)}, bf16[1,1,1,1,24,2048]{5,4,3,2,1,0:T(8,128)(2,1)}, u32[]{:S(2)}, u32[]{:S(2)}) collective-permute-start(bf16[1,1,1,1,24,2048]{5,4,3,2,1,0:T(8,128)(2,1)} %maximum_bitcast_fusion.2), channel_id=1, source_target_pairs={{0,3},{1,0},{2,1},{3,2},{4,7},{5,4},{6,5},{7,6},{8,11},{9,8},{10,9... | collective-permute-start | bytes 294920 | tf_op jit(solution)/shard_map/ppermute | solution.py:493
  21.3 12.7 %collective-permute-start.1 = (bf16[1,1,1,1,24,2048]{5,4,3,2,1,0:T(8,128)(2,1)}, bf16[1,1,1,1,24,2048]{5,4,3,2,1,0:T(8,128)(2,1)}, u32[]{:S(2)}, u32[]{:S(2)}) collective-permute-start(bf16[1,1,1,1,24,2048]{5,4,3,2,1,0:T(8,128)(2,1)} %maximum_bitcast_fusion.2), channel_id=1, source_target_pairs={{0,2},{1,3},{2,0},{3,1},{4,6},{5,7},{6,4},{7,5},{8,10},{9,11},{10,... | collective-permute-start | bytes 294920 | tf_op jit(solution)/shard_map/ppermute | solution.py:493
  37.6 17.1 %collective-permute-start.3 = (bf16[1,1,1,4,24,2048]{5,4,3,2,1,0:T(8,128)(2,1)S(1)}, bf16[1,1,1,4,24,2048]{5,4,3,2,1,0:T(8,128)(2,1)S(1)}, u32[]{:S(2)}, u32[]{:S(2)}) collective-permute-start(bf16[1,1,1,4,24,2048]{5,4,3,2,1,0:T(8,128)(2,1)S(1)} %pad_maximum_fusion.9), channel_id=1, source_target_pairs={{0,8},{4,12},{8,0},{12,4},{16,24},{20,28},{24,16},{28,20},{1,9},{5... | collective-permute-start | bytes 1179656 | tf_op jit(solution)/shard_map/ppermute | solution.py:499
  39.7 27.0 %collective-permute-start.10 = (bf16[2,1,1,4,24,1536]{5,4,3,2,1,0:T(8,128)(2,1)S(1)}, bf16[2,1,1,4,24,1536]{5,4,3,2,1,0:T(8,128)(2,1)S(1)}, u32[]{:S(2)}, u32[]{:S(2)}) collective-permute-start(bf16[2,1,1,4,24,1536]{5,4,3,2,1,0:T(8,128)(2,1)S(1)} %pad_maximum_fusion.8), channel_id=1, source_target_pairs={{0,8},{4,12},{8,0},{12,4},{16,24},{20,28},{24,16},{28,20},{1,9},{5... | collective-permute-start | bytes 1769480 | tf_op jit(solution)/shard_map/ppermute | solution.py:499
  54.9 13.2 %collective-permute-start.4 = (bf16[1,2,1,4,24,2048]{5,4,3,2,1,0:T(8,128)(2,1)S(1)}, bf16[1,2,1,4,24,2048]{5,4,3,2,1,0:T(8,128)(2,1)S(1)}, u32[]{:S(2)}, u32[]{:S(2)}) collective-permute-start(bf16[1,2,1,4,24,2048]{5,4,3,2,1,0:T(8,128)(2,1)S(1)} %pad_maximum_fusion.6), channel_id=1, source_target_pairs={{0,16},{4,20},{8,24},{12,28},{16,0},{20,4},{24,8},{28,12},{1,17},{... | collective-permute-start | bytes 2359304 | tf_op jit(solution)/shard_map/ppermute | solution.py:499
  200.4 26.4 %collective-permute-start.12 = (f32[2,2,1,4,48,768]{5,4,3,2,1,0:T(8,128)}, f32[2,2,1,4,48,768]{5,4,3,2,1,0:T(8,128)}, u32[]{:S(2)}, u32[]{:S(2)}) collective-permute-start(f32[2,2,1,4,48,768]{5,4,3,2,1,0:T(8,128)} %constant_dynamic-slice_fusion.6), channel_id=1, source_target_pairs={{0,4},{4,0},{8,12},{12,8},{16,20},{20,16},{24,28},{28,24},{1,5},{5... | collective-permute-start | bytes 7077896 | tf_op jit(solution)/shard_map/ppermute | solution.py:499
  232.4 67.9 %collective-permute-start.15 = (bf16[1,1,1,4,24,1536]{5,4,3,2,1,0:T(8,128)(2,1)}, bf16[1,1,1,4,24,1536]{5,4,3,2,1,0:T(8,128)(2,1)S(1)}, u32[]{:S(2)}, u32[]{:S(2)}) collective-permute-start(bf16[1,1,1,4,24,1536]{5,4,3,2,1,0:T(8,128)(2,1)} %get-tuple-element.255), channel_id=1, source_target_pairs={{0,24},{4,28},{8,16},{12,20},{16,8},{20,12},{24,0},{28,4},{1,25},{... | collective-permute-start | bytes 884744 | tf_op jit(solution)/shard_map/ppermute | solution.py:526
  234.6 65.7 %collective-permute-start.14 = (bf16[1,1,1,4,24,1536]{5,4,3,2,1,0:T(8,128)(2,1)}, bf16[1,1,1,4,24,1536]{5,4,3,2,1,0:T(8,128)(2,1)}, u32[]{:S(2)}, u32[]{:S(2)}) collective-permute-start(bf16[1,1,1,4,24,1536]{5,4,3,2,1,0:T(8,128)(2,1)} %get-tuple-element.256), channel_id=1, source_target_pairs={{0,16},{4,20},{8,24},{12,28},{16,0},{20,4},{24,8},{28,12},{1,17},{... | collective-permute-start | bytes 884744 | tf_op jit(solution)/shard_map/ppermute | solution.py:526
  235.4 64.9 %collective-permute-start.13 = (bf16[1,1,1,4,24,1536]{5,4,3,2,1,0:T(8,128)(2,1)}, bf16[1,1,1,4,24,1536]{5,4,3,2,1,0:T(8,128)(2,1)}, u32[]{:S(2)}, u32[]{:S(2)}) collective-permute-start(bf16[1,1,1,4,24,1536]{5,4,3,2,1,0:T(8,128)(2,1)} %get-tuple-element.254), channel_id=1, source_target_pairs={{0,8},{4,12},{8,0},{12,4},{16,24},{20,28},{24,16},{28,20},{1,9},{5... | collective-permute-start | bytes 884744 | tf_op jit(solution)/shard_map/ppermute | solution.py:526
  326.7 20.0 %collective-permute-start.18 = (f32[2,2,1,4,48,768]{5,4,3,2,1,0:T(8,128)S(1)}, f32[2,2,1,4,48,768]{5,4,3,2,1,0:T(8,128)S(1)}, u32[]{:S(2)}, u32[]{:S(2)}) collective-permute-start(f32[2,2,1,4,48,768]{5,4,3,2,1,0:T(8,128)S(1)} %constant_dynamic-slice_fusion.3), channel_id=1, source_target_pairs={{0,4},{4,0},{8,12},{12,8},{16,20},{20,16},{24,28},{28,24},{1,5},{5... | collective-permute-start | bytes 7077896 | tf_op jit(solution)/shard_map/ppermute | solution.py:499
  327.0 20.2 %collective-permute-start.17 = (f32[2,2,1,4,24,1536]{5,4,3,2,1,0:T(8,128)S(1)}, f32[2,2,1,4,24,1536]{5,4,3,2,1,0:T(8,128)S(1)}, u32[]{:S(2)}, u32[]{:S(2)}) collective-permute-start(f32[2,2,1,4,24,1536]{5,4,3,2,1,0:T(8,128)S(1)} %constant_dynamic-slice_fusion.4), channel_id=1, source_target_pairs={{0,4},{4,0},{8,12},{12,8},{16,20},{20,16},{24,28},{28,24},{1,5},{5... | collective-permute-start | bytes 7077896 | tf_op jit(solution)/shard_map/ppermute | solution.py:499
  327.7 19.8 %collective-permute-start.16 = (f32[2,2,1,4,24,1920]{5,4,3,2,1,0:T(8,128)S(1)}, f32[2,2,1,4,24,1920]{5,4,3,2,1,0:T(8,128)S(1)}, u32[]{:S(2)}, u32[]{:S(2)}) collective-permute-start(f32[2,2,1,4,24,1920]{5,4,3,2,1,0:T(8,128)S(1)} %constant_dynamic-slice_fusion.5), channel_id=1, source_target_pairs={{0,4},{4,0},{8,12},{12,8},{16,20},{20,16},{24,28},{28,24},{1,5},{5... | collective-permute-start | bytes 8847368 | tf_op jit(solution)/shard_map/ppermute | solution.py:499
  328.3 11.2 %collective-permute-start.41 = (bf16[1,1,1,1,24,1536]{5,4,3,2,1,0:T(8,128)(2,1)S(1)}, bf16[1,1,1,1,24,1536]{5,4,3,2,1,0:T(8,128)(2,1)S(1)}, u32[]{:S(2)}, u32[]{:S(2)}) collective-permute-start(bf16[1,1,1,1,24,1536]{5,4,3,2,1,0:T(8,128)(2,1)S(1)} %get-tuple-element.274), channel_id=1, source_target_pairs={{0,3},{1,0},{2,1},{3,2},{4,7},{5,4},{6,5},{7,6},{8,11},{9,8},{10,9... | collective-permute-start | bytes 221192 | tf_op jit(solution)/shard_map/ppermute | solution.py:493
  353.2 65.7 %collective-permute-start.21 = (bf16[1,1,1,4,24,4992]{5,4,3,2,1,0:T(8,128)(2,1)}, bf16[1,1,1,4,24,4992]{5,4,3,2,1,0:T(8,128)(2,1)}, u32[]{:S(2)}, u32[]{:S(2)}) collective-permute-start(bf16[1,1,1,4,24,4992]{5,4,3,2,1,0:T(8,128)(2,1)} %get-tuple-element.242), channel_id=1, source_target_pairs={{0,24},{4,28},{8,16},{12,20},{16,8},{20,12},{24,0},{28,4},{1,25},{... | collective-permute-start | bytes 2875400 | tf_op jit(solution)/shard_map/ppermute | solution.py:526
  356.0 62.9 %collective-permute-start.20 = (bf16[1,1,1,4,24,4992]{5,4,3,2,1,0:T(8,128)(2,1)}, bf16[1,1,1,4,24,4992]{5,4,3,2,1,0:T(8,128)(2,1)}, u32[]{:S(2)}, u32[]{:S(2)}) collective-permute-start(bf16[1,1,1,4,24,4992]{5,4,3,2,1,0:T(8,128)(2,1)} %get-tuple-element.243), channel_id=1, source_target_pairs={{0,16},{4,20},{8,24},{12,28},{16,0},{20,4},{24,8},{28,12},{1,17},{... | collective-permute-start | bytes 2875400 | tf_op jit(solution)/shard_map/ppermute | solution.py:526
  356.3 62.6 %collective-permute-start.19 = (bf16[1,1,1,4,24,4992]{5,4,3,2,1,0:T(8,128)(2,1)}, bf16[1,1,1,4,24,4992]{5,4,3,2,1,0:T(8,128)(2,1)}, u32[]{:S(2)}, u32[]{:S(2)}) collective-permute-start(bf16[1,1,1,4,24,4992]{5,4,3,2,1,0:T(8,128)(2,1)} %get-tuple-element.241), channel_id=1, source_target_pairs={{0,8},{4,12},{8,0},{12,4},{16,24},{20,28},{24,16},{28,20},{1,9},{5... | collective-permute-start | bytes 2875400 | tf_op jit(solution)/shard_map/ppermute | solution.py:526
  442.0 22.3 %collective-permute-start.38 = (bf16[1,1,1,1,24,4992]{5,4,3,2,1,0:T(8,128)(2,1)}, bf16[1,1,1,1,24,4992]{5,4,3,2,1,0:T(8,128)(2,1)}, u32[]{:S(2)}, u32[]{:S(2)}) collective-permute-start(bf16[1,1,1,1,24,4992]{5,4,3,2,1,0:T(8,128)(2,1)} %get-tuple-element.262), channel_id=1, source_target_pairs={{0,3},{1,0},{2,1},{3,2},{4,7},{5,4},{6,5},{7,6},{8,11},{9,8},{10,9... | collective-permute-start | bytes 718856 | tf_op jit(solution)/shard_map/ppermute | solution.py:493
  443.3 22.9 %collective-permute-start.37 = (bf16[1,1,1,1,24,4992]{5,4,3,2,1,0:T(8,128)(2,1)}, bf16[1,1,1,1,24,4992]{5,4,3,2,1,0:T(8,128)(2,1)}, u32[]{:S(2)}, u32[]{:S(2)}) collective-permute-start(bf16[1,1,1,1,24,4992]{5,4,3,2,1,0:T(8,128)(2,1)} %get-tuple-element.263), channel_id=1, source_target_pairs={{0,2},{1,3},{2,0},{3,1},{4,6},{5,7},{6,4},{7,5},{8,10},{9,11},{10,... | collective-permute-start | bytes 718856 | tf_op jit(solution)/shard_map/ppermute | solution.py:493
  443.6 22.8 %collective-permute-start.36 = (bf16[1,1,1,1,24,4992]{5,4,3,2,1,0:T(8,128)(2,1)}, bf16[1,1,1,1,24,4992]{5,4,3,2,1,0:T(8,128)(2,1)}, u32[]{:S(2)}, u32[]{:S(2)}) collective-permute-start(bf16[1,1,1,1,24,4992]{5,4,3,2,1,0:T(8,128)(2,1)} %get-tuple-element.261), channel_id=1, source_target_pairs={{0,1},{1,2},{2,3},{3,0},{4,5},{5,6},{6,7},{7,4},{8,9},{9,10},{10,1... | collective-permute-start | bytes 718856 | tf_op jit(solution)/shard_map/ppermute | solution.py:493
  463.7 33.9 %collective-permute-start.29 = (f32[2,2,1,4,24,1920]{5,4,3,2,1,0:T(8,128)}, f32[2,2,1,4,24,1920]{5,4,3,2,1,0:T(8,128)}, u32[]{:S(2)}, u32[]{:S(2)}) collective-permute-start(f32[2,2,1,4,24,1920]{5,4,3,2,1,0:T(8,128)} %constant_dynamic-slice_fusion.1), channel_id=1, source_target_pairs={{0,4},{4,0},{8,12},{12,8},{16,20},{20,16},{24,28},{28,24},{1,5},{5... | collective-permute-start | bytes 8847368 | tf_op jit(solution)/shard_map/ppermute | solution.py:499
  464.3 14.3 %collective-permute-start.48 = (f32[178,128]{1,0:T(8,128)S(1)}, f32[178,128]{1,0:T(8,128)S(1)}, u32[]{:S(2)}, u32[]{:S(2)}) collective-permute-start(f32[178,128]{1,0:T(8,128)S(1)} %add_add_fusion.3), channel_id=1, source_target_pairs={{0,3},{1,0},{2,1},{3,2},{4,7},{5,4},{6,5},{7,6},{8,11},{9,8},{10,9... | collective-permute-start | bytes 273416 | tf_op jit(solution)/shard_map/ppermute | solution.py:493
  466.2 13.3 %collective-permute-start.46 = (f32[178,128]{1,0:T(8,128)S(1)}, f32[178,128]{1,0:T(8,128)S(1)}, u32[]{:S(2)}, u32[]{:S(2)}) collective-permute-start(f32[178,128]{1,0:T(8,128)S(1)} %add_add_fusion.3), channel_id=1, source_target_pairs={{0,1},{1,2},{2,3},{3,0},{4,5},{5,6},{6,7},{7,4},{8,9},{9,10},{10,1... | collective-permute-start | bytes 273416 | tf_op jit(solution)/shard_map/ppermute | solution.py:493
  466.4 13.7 %collective-permute-start.47 = (f32[178,128]{1,0:T(8,128)S(1)}, f32[178,128]{1,0:T(8,128)}, u32[]{:S(2)}, u32[]{:S(2)}) collective-permute-start(f32[178,128]{1,0:T(8,128)S(1)} %add_add_fusion.3), channel_id=1, source_target_pairs={{0,2},{1,3},{2,0},{3,1},{4,6},{5,7},{6,4},{7,5},{8,10},{9,11},{10,... | collective-permute-start | bytes 273416 | tf_op jit(solution)/shard_map/ppermute | solution.py:493
  478.6 14.4 %collective-permute-start.24 = (bf16[1,1,1,4,24,1536]{5,4,3,2,1,0:T(8,128)(2,1)}, bf16[1,1,1,4,24,1536]{5,4,3,2,1,0:T(8,128)(2,1)S(1)}, u32[]{:S(2)}, u32[]{:S(2)}) collective-permute-start(bf16[1,1,1,4,24,1536]{5,4,3,2,1,0:T(8,128)(2,1)} %get-tuple-element.251), channel_id=1, source_target_pairs={{0,16},{4,20},{8,24},{12,28},{16,0},{20,4},{24,8},{28,12},{1,17},{... | collective-permute-start | bytes 884744 | tf_op jit(solution)/shard_map/ppermute | solution.py:526
  479.4 13.6 %collective-permute-start.23 = (bf16[1,1,1,4,24,1536]{5,4,3,2,1,0:T(8,128)(2,1)}, bf16[1,1,1,4,24,1536]{5,4,3,2,1,0:T(8,128)(2,1)}, u32[]{:S(2)}, u32[]{:S(2)}) collective-permute-start(bf16[1,1,1,4,24,1536]{5,4,3,2,1,0:T(8,128)(2,1)} %get-tuple-element.249), channel_id=1, source_target_pairs={{0,8},{4,12},{8,0},{12,4},{16,24},{20,28},{24,16},{28,20},{1,9},{5... | collective-permute-start | bytes 884744 | tf_op jit(solution)/shard_map/ppermute | solution.py:526
  501.7 12.8 %collective-permute-start.32 = (bf16[1,1,1,4,24,1920]{5,4,3,2,1,0:T(8,128)(2,1)}, bf16[1,1,1,4,24,1920]{5,4,3,2,1,0:T(8,128)(2,1)}, u32[]{:S(2)}, u32[]{:S(2)}) collective-permute-start(bf16[1,1,1,4,24,1920]{5,4,3,2,1,0:T(8,128)(2,1)} %get-tuple-element.247), channel_id=1, source_target_pairs={{0,24},{4,28},{8,16},{12,20},{16,8},{20,12},{24,0},{28,4},{1,25},{... | collective-permute-start | bytes 1105928 | tf_op jit(solution)/shard_map/ppermute | solution.py:526
  503.4 17.0 %collective-permute-start.31 = (bf16[1,1,1,4,24,1920]{5,4,3,2,1,0:T(8,128)(2,1)}, bf16[1,1,1,4,24,1920]{5,4,3,2,1,0:T(8,128)(2,1)}, u32[]{:S(2)}, u32[]{:S(2)}) collective-permute-start(bf16[1,1,1,4,24,1920]{5,4,3,2,1,0:T(8,128)(2,1)} %get-tuple-element.248), channel_id=1, source_target_pairs={{0,16},{4,20},{8,24},{12,28},{16,0},{20,4},{24,8},{28,12},{1,17},{... | collective-permute-start | bytes 1105928 | tf_op jit(solution)/shard_map/ppermute | solution.py:526
  504.7 15.8 %collective-permute-start.30 = (bf16[1,1,1,4,24,1920]{5,4,3,2,1,0:T(8,128)(2,1)}, bf16[1,1,1,4,24,1920]{5,4,3,2,1,0:T(8,128)(2,1)}, u32[]{:S(2)}, u32[]{:S(2)}) collective-permute-start(bf16[1,1,1,4,24,1920]{5,4,3,2,1,0:T(8,128)(2,1)} %get-tuple-element.246), channel_id=1, source_target_pairs={{0,8},{4,12},{8,0},{12,4},{16,24},{20,28},{24,16},{28,20},{1,9},{5... | collective-permute-start | bytes 1105928 | tf_op jit(solution)/shard_map/ppermute | solution.py:526
  (106 other events, 1139.5 us)
Sparse Core Ops, SparseCore 0:
  11.5 98.9 all-gather.1

commit v3 on v2

--- a/solution.py
+++ b/solution.py
@@ -2,6 +2,8 @@
 
 import jax
 import jax.numpy as jnp
+import ml_dtypes
+import numpy as np
 from jax import lax
 from jax.experimental import pallas as pl
 from jax.experimental.pallas import tpu as pltpu
@@ -25,6 +27,9 @@
 
 SPAN = 128
 GROUP = 256
+GATE_ROWS = 64
+GATE_BLOCK = 256
+NORM_BLOCK = 256
 GROUPS = INNER // GROUP
 LANES = 128
 LOG2E = 1.4426950408889634
@@ -49,11 +54,19 @@
     return lax.dot_general(a, b, (dims, ((), ())), preferred_element_type=F32)
 
 
-def mm(a, b, dims, passes):
+def mm(a, b, dims, passes, pack=None):
     if passes == 1:
         return raw_dot(a.astype(BF16), b.astype(BF16), dims)
     a_hi, a_lo = halves(a)
     b_hi, b_lo = halves(b)
+    if pack == "k":
+        left = jnp.concatenate([a_hi, a_lo], axis=dims[0][0])
+        right = jnp.concatenate([b_hi, b_hi], axis=dims[1][0])
+        return raw_dot(left, right, dims) + raw_dot(a_hi, b_lo, dims)
+    if pack == "n":
+        both = raw_dot(a_hi, jnp.concatenate([b_hi, b_lo], axis=1 - dims[1][0]), dims)
+        half = both.shape[1] // 2
+        return both[:, :half] + (both[:, half:] + raw_dot(a_lo, b_hi, dims))
     return raw_dot(a_hi, b_hi, dims) + (raw_dot(a_lo, b_hi, dims) + raw_dot(a_hi, b_lo, dims))
 
 
@@ -140,9 +153,27 @@
     return jnp.concatenate([cum_t[head : head + 1, :], cum_t[head + 1 : head + 2, :]], axis=1)
 
 
-def forward_kernel(
-    ends_ref, z_ref, xr_ref, par_ref, gain_ref, hw_ref, spread_ref, gn_ref, ys_ref, st_ref, buf, act, state, yg
-):
+def gate_rows(z_ref, ys_ref, gain_ref, gn_ref, yg):
+    for r in range(ys_ref.shape[0] // GATE_ROWS):
+        rs = slice(GATE_ROWS * r, GATE_ROWS * (r + 1))
+        squares = jnp.zeros((GATE_ROWS, LANES), F32)
+        for c in range(INNER // LANES):
+            cs = slice(LANES * c, LANES * (c + 1))
+            z = z_ref[rs, cs]
+            gated = ys_ref[rs, cs] * (z * sigmoid(z))
+            yg[rs, cs] = gated
+            squares = squares + gated * gated
+        scale = lax.rsqrt(jnp.sum(squares, axis=1, keepdims=True) / INNER + EPSILON)
+        scale = jnp.broadcast_to(scale, (GATE_ROWS, LANES))
+        for c in range(INNER // LANES):
+            cs = slice(LANES * c, LANES * (c + 1))
+            gn_ref[rs, cs] = (yg[rs, cs] * scale * gain_ref[0:1, cs]).astype(BF16)
+
+
+def forward_kernel(gated, ends_ref, xr_ref, par_ref, gain_ref, hw_ref, spread_ref, *refs):
+    if gated:
+        z_ref, gn_ref, *refs = refs
+    ys_ref, st_ref, buf, act, state, *yg = refs
     block = pl.program_id(0)
     base = block * SPAN
 
@@ -174,7 +205,6 @@
     bm_t = bm.T
     steps2, reach2, to_end2 = two_parts(steps), two_parts(reach), two_parts(to_end)
     st_ref[0] = state[...]
-    squares = jnp.zeros((SPAN, LANES), F32)
     for g in range(GROUPS):
         gs = slice(GROUP * g, GROUP * (g + 1))
         spread = spread_ref[:, gs]
@@ -184,33 +214,102 @@
         for q in range(2):
             head = 4 * g + 2 * q
             mix = jnp.exp2(pair_columns(cum, head) - pair_rows(cum_t, head) + bias2) * gram2
-            within.append(mm(mix, lane_split(xd[:, LANES * q : LANES * (q + 1)]), NN, PASS_PAIR))
+            within.append(mm(mix, lane_split(xd[:, LANES * q : LANES * (q + 1)]), NN, PASS_PAIR, "n"))
         reach_g = raw_dot(reach2, spread, NN)
         before = state[:, gs]
-        scan = jnp.concatenate(within, axis=1) + mm(cm, before, NN, PASS_STATE) * reach_g
-        ys_ref[:, gs] = scan
+        scan = jnp.concatenate(within, axis=1) + mm(cm, before, NN, PASS_STATE, "k") * reach_g
+        ys_ref[:, gs] = scan + gain_ref[1:2, gs] * x
         state[:, gs] = before * reach_g[SPAN - 1 : SPAN, :] + mm(
-            bm_t, xd * raw_dot(to_end2, spread, NN), NN, PASS_STATE
+            bm_t, xd * raw_dot(to_end2, spread, NN), NN, PASS_STATE, "k"
         )
-        z = z_ref[:, gs]
-        gated = (scan + gain_ref[1:2, gs] * x) * (z * sigmoid(z))
-        yg[:, gs] = gated
-        gated = gated * gated
-        squares = squares + gated[:, :LANES] + gated[:, LANES:]
-    scale = lax.rsqrt(jnp.sum(squares, axis=1, keepdims=True) / INNER + EPSILON)
-    for g in range(GROUPS):
-        gs = slice(GROUP * g, GROUP * (g + 1))
-        gn_ref[:, gs] = (yg[:, gs] * scale * gain_ref[0:1, gs]).astype(BF16)
+    if gated:
+        gate_rows(z_ref, ys_ref, gain_ref, gn_ref, yg[0])
+
+
+def gate_back_rows(z_ref, ys_ref, dgn_ref, gain_ref, dz_ref, dy_ref, dgain_ref, yg):
+    for r in range(z_ref.shape[0] // GATE_ROWS):
+        rs = slice(GATE_ROWS * r, GATE_ROWS * (r + 1))
+        squares = jnp.zeros((GATE_ROWS, LANES), F32)
+        overlap = jnp.zeros((GATE_ROWS, LANES), F32)
+        for c in range(INNER // LANES):
+            cs = slice(LANES * c, LANES * (c + 1))
+            z = z_ref[rs, cs]
+            gated = ys_ref[rs, cs] * (z * sigmoid(z))
+            yg[rs, cs] = gated
+            overlap = overlap + gated * (dgn_ref[rs, cs] * gain_ref[0:1, cs])
+            squares = squares + gated * gated
+        scale = lax.rsqrt(jnp.sum(squares, axis=1, keepdims=True) / INNER + EPSILON)
+        pull = jnp.sum(overlap, axis=1, keepdims=True) * (scale * scale * scale) / INNER
+        scale = jnp.broadcast_to(scale, (GATE_ROWS, LANES))
+        pull = jnp.broadcast_to(pull, (GATE_ROWS, LANES))
+        for c in range(INNER // LANES):
+            cs = slice(LANES * c, LANES * (c + 1))
+            z = z_ref[rs, cs]
+            gate = sigmoid(z)
+            gated = yg[rs, cs]
+            dgn = dgn_ref[rs, cs] * scale
+            dgain_ref[:, cs] += partial8(dgn * gated)
+            dgated = dgn * gain_ref[0:1, cs] - gated * pull
+            dy_ref[rs, cs] = dgated * (z * gate)
+            dz_ref[rs, cs] = (dgated * ys_ref[rs, cs] * (gate * (1.0 + z * (1.0 - gate)))).astype(BF16)
+
+
+def gate_back_kernel(z_ref, ys_ref, dgn_ref, gain_ref, dz_ref, dy_ref, dgain_ref, yg):
+    @pl.when(pl.program_id(0) == 0)
+    def _():
+        dgain_ref[...] = jnp.zeros_like(dgain_ref)
+
+    gate_back_rows(z_ref, ys_ref, dgn_ref, gain_ref, dz_ref, dy_ref, dgain_ref, yg)
+
+
+def gate_forward(z, ys, gain):
+    tokens = z.shape[0]
+    rows = pl.BlockSpec((GATE_BLOCK, INNER), lambda i: (i, 0))
+    return pl.pallas_call(
+        gate_rows,
+        grid=(tokens // GATE_BLOCK,),
+        in_specs=[rows, rows, whole((8, INNER))],
+        out_specs=rows,
+        out_shape=jax.ShapeDtypeStruct((tokens, INNER), BF16),
+        scratch_shapes=[pltpu.VMEM((GATE_BLOCK, INNER), F32)],
+        compiler_params=pltpu.CompilerParams(vmem_limit_bytes=VMEM_LIMIT),
+        cost_estimate=pl.CostEstimate(flops=20_000_000, bytes_accessed=20_000_000, transcendentals=0),
+        name="gate_forward",
+    )(z, ys, gain)
+
+
+def gate_backward(z, ys, dgn, gain):
+    tokens = z.shape[0]
+    rows = pl.BlockSpec((GATE_BLOCK, INNER), lambda i: (i, 0))
+    return pl.pallas_call(
+        gate_back_kernel,
+        grid=(tokens // GATE_BLOCK,),
+        in_specs=[rows, rows, rows, whole((8, INNER))],
+        out_specs=[rows, rows, whole((8, INNER))],
+        out_shape=[
+            jax.ShapeDtypeStruct((tokens, INNER), BF16),
+            jax.ShapeDtypeStruct((tokens, INNER), F32),
+            jax.ShapeDtypeStruct((8, INNER), F32),
+        ],
+        scratch_shapes=[pltpu.VMEM((GATE_BLOCK, INNER), F32)],
+        compiler_params=pltpu.CompilerParams(vmem_limit_bytes=VMEM_LIMIT),
+        cost_estimate=pl.CostEstimate(flops=60_000_000, bytes_accessed=30_000_000, transcendentals=0),
+        name="gate_backward",
+    )(z, ys, dgn, gain)
 
 
 def backward_kernel(
-    top, ends_ref, z_ref, xr_ref, halo_ref, dgn_ref, ys_ref, st_ref, par_ref, gain_ref, hw_ref, spread_ref, gather_ref,
-    *refs,
+    top, fused, ends_ref, xr_ref, halo_ref, ys_ref, st_ref, par_ref, gain_ref, hw_ref, spread_ref, gather_ref, *refs
 ):
+    if fused:
+        z_ref, dgn_ref, *refs = refs
+        *refs, dz_ref, dgate_ref, dy_ref, yg = refs
+    else:
+        dy_ref, *refs = refs
     (
-        rgrad_in, dcv_in, dz_ref, dxr_ref, dpar_ref, dgain_ref, dhw_ref, rgrad, dcv_out,
-        buf, act, slope, dact, dcv, yg, dgram,
-    ) = refs[-16:]
+        rgrad_in, dcv_in, dxr_ref, dpar_ref, dskip_ref, dhw_ref, rgrad, dcv_out,
+        buf, act, slope, dact, dcv, dgram,
+    ) = refs[-14:]
     step = pl.program_id(0)
     block = top - step
     base = block * SPAN
@@ -220,9 +319,13 @@
         dcv[0:8, :] = dcv_in[...]
         rgrad[...] = rgrad_in[...]
         dpar_ref[...] = jnp.zeros_like(dpar_ref)
-        dgain_ref[...] = jnp.zeros_like(dgain_ref)
+        dskip_ref[...] = jnp.zeros_like(dskip_ref)
         dhw_ref[...] = jnp.zeros_like(dhw_ref)
-
+        if fused:
+            dgate_ref[...] = jnp.zeros_like(dgate_ref)
+
+    if fused:
+        gate_back_rows(z_ref, ys_ref, dgn_ref, gain_ref, dz_ref, dy_ref, dgate_ref, yg)
     place, seg, pre, steps, log_rate, cum, reach, to_end, rows, cols, same = block_terms(
         base, ends_ref, hw_ref, xr_ref[:, CH:XR]
     )
@@ -250,20 +353,6 @@
     cm_t = cm.T
     steps2, reach2, to_end2 = two_parts(steps), two_parts(reach), two_parts(to_end)
 
-    squares = jnp.zeros((SPAN, LANES), F32)
-    overlap = jnp.zeros((SPAN, LANES), F32)
-    for g in range(GROUPS):
-        gs = slice(GROUP * g, GROUP * (g + 1))
-        z = z_ref[:, gs]
-        gated = (ys_ref[:, gs] + gain_ref[1:2, gs] * act[:, gs]) * (z * sigmoid(z))
-        yg[:, gs] = gated
-        shared = gated * (dgn_ref[:, gs] * gain_ref[0:1, gs])
-        gated = gated * gated
-        squares = squares + gated[:, :LANES] + gated[:, LANES:]
-        overlap = overlap + shared[:, :LANES] + shared[:, LANES:]
-    scale = lax.rsqrt(jnp.sum(squares, axis=1, keepdims=True) / INNER + EPSILON)
-    pull = jnp.sum(overlap, axis=1, keepdims=True) * (scale * scale * scale) / INNER
-
     dgram[...] = jnp.zeros_like(dgram)
     dbm = jnp.zeros((SPAN, STATE), F32)
     dcm = jnp.zeros((SPAN, STATE), F32)
@@ -276,19 +365,9 @@
         spread = spread_ref[:, gs]
         gather = gather_ref[gs, :]
         x = act[:, gs]
-        z = z_ref[:, gs]
-        gate = sigmoid(z)
-        soft = z * gate
-        scan = ys_ref[:, gs]
         skip = gain_ref[1:2, gs]
-        y = scan + skip * x
-        gated = yg[:, gs]
-        dgn = dgn_ref[:, gs]
-        dgated = scale * (dgn * gain_ref[0:1, gs]) - gated * pull
-        dgain_ref[0:8, gs] += partial8(dgn * (gated * scale))
-        dy = dgated * soft
-        dz_ref[:, gs] = (dgated * y * (gate * (1.0 + z * (1.0 - gate)))).astype(BF16)
-        dgain_ref[8:16, gs] += partial8(dy * x)
+        dy = dy_ref[:, gs]
+        dskip_ref[:, gs] += partial8(dy * x)
         steps_g = raw_dot(steps2, spread, NN)
         reach_g = raw_dot(reach2, spread, NN)
         to_end_g = raw_dot(to_end2, spread, NN)
@@ -299,15 +378,15 @@
             qs = slice(LANES * q, LANES * (q + 1))
             decay = jnp.exp2(pair_rows(cum_t, head) - pair_columns(cum, head) + bias2)
             dy_two = lane_split(dy[:, qs])
-            dxd_in.append(mm(decay * gram2, dy_two, NN, PASS_PAIR))
+            dxd_in.append(mm(decay * gram2, dy_two, NN, PASS_PAIR, "n"))
             dgram[...] += decay * mm(xd[:, qs], dy_two, NT, PASS_PAIR)
         dxd_in = jnp.concatenate(dxd_in, axis=1)
         later = rgrad[:, gs]
         before = st_ref[0, :, gs]
         dxd_out = mm(bm, later, NN, PASS_STATE) * to_end_g
-        dbm = dbm + mm(xd * to_end_g, later, NT, PASS_STATE)
+        dbm = dbm + mm(xd * to_end_g, later, NT, PASS_STATE, "n")
         dy_reach = dy * reach_g
-        dcm = dcm + mm(dy_reach, before, NT, PASS_STATE)
+        dcm = dcm + mm(dy_reach, before, NT, PASS_STATE, "n")
         fade = reach_g[SPAN - 1 : SPAN, :]
         red_through = red_through + reduce_right(partial8(before * later) * fade, gather, 2)
         rgrad[:, gs] = later * fade + mm(cm_t, dy_reach, NN, PASS_STATE)
@@ -316,7 +395,7 @@
         else:
             dy_seen, xd_seen = dy, xd
         dxd = dxd_in + dxd_out
-        red_rate = red_rate + reduce_right(dy_seen * scan - xd_seen * dxd_in, gather, 2)
+        red_rate = red_rate + reduce_right(dy_seen * (ys_ref[:, gs] - skip * x) - xd_seen * dxd_in, gather, 2)
         red_tail = red_tail + reduce_right(x * dxd_out, gather, PASS_RED)
         red_step = red_step + reduce_right(x * dxd, gather, PASS_RED)
         dact[:, gs] = skip * dy + steps_g * dxd
@@ -336,25 +415,23 @@
 
     for c in range(CH // LANES):
         cs = slice(LANES * c, LANES * (c + 1))
+        now = xr_ref[:, cs]
         dconv = dact[:, cs] * slope[:, cs]
         dcv[0:SPAN, cs] = dconv
         dxbc = par_ref[3:4, cs] * dconv
-        dpar_ref[24:32, cs] += partial8(dconv * buf[8 : 8 + SPAN, cs])
+        dpar_ref[24:32, cs] += partial8(dconv * now)
         dpar_ref[32:40, cs] += partial8(dconv)
         for k in range(1, 4):
-            dxbc = dxbc + par_ref[3 - k : 4 - k, cs] * (fore_masks[k - 1] * dcv[k : k + SPAN, cs])
-            dpar_ref[24 - 8 * k : 32 - 8 * k, cs] += partial8(
-                dconv * (back_masks[k - 1] * buf[8 - k : 8 - k + SPAN, cs])
-            )
+            ahead = fore_masks[k - 1] * dcv[k : k + SPAN, cs]
+            dxbc = dxbc + par_ref[3 - k : 4 - k, cs] * ahead
+            dpar_ref[24 - 8 * k : 32 - 8 * k, cs] += partial8(ahead * now)
         dxr_ref[:, cs] = dxbc.astype(BF16)
     dcv_out[...] = dcv[0:8, :]
 
 
 def spread_matrices():
-    heads = lax.broadcasted_iota(jnp.int32, (LANES, INNER), 0)
-    lanes = lax.broadcasted_iota(jnp.int32, (LANES, INNER), 1) // HEADDIM
-    one = (heads == lanes).astype(BF16)
-    return jnp.concatenate([one, one], axis=0), one.T
+    one = (np.arange(LANES)[:, None] == np.arange(INNER)[None, :] // HEADDIM).astype(ml_dtypes.bfloat16)
+    return jnp.asarray(np.concatenate([one, one], axis=0)), jnp.asarray(one.T)
 
 
 def kernel_params(vector, head):
@@ -374,100 +451,141 @@
 SMEM = pl.BlockSpec(memory_space=pltpu.SMEM)
 
 
-def mixer_forward(ends, z, xr, par, gain, hw, spread):
-    tokens = z.shape[0]
+def mixer_forward(ends, xr, par, gain, hw, spread, z=None):
+    tokens = xr.shape[0]
     blocks = tokens // SPAN
     rows = lambda width: pl.BlockSpec((SPAN, width), lambda i: (i, 0))
+    in_specs = [SMEM, rows(XR), whole((8, CH)), whole((8, INNER)), whole((8, LANES)), whole((256, INNER))]
+    out_specs = [rows(INNER), pl.BlockSpec((1, STATE, INNER), lambda i: (i, 0, 0))]
+    out_shape = [
+        jax.ShapeDtypeStruct((tokens, INNER), F32),
+        jax.ShapeDtypeStruct((blocks, STATE, INNER), F32),
+    ]
+    scratch = [
+        pltpu.VMEM((SPAN + 8, CH), F32),
+        pltpu.VMEM((SPAN, CH), F32),
+        pltpu.VMEM((STATE, INNER), F32),
+    ]
+    more = []
+    if z is not None:
+        more = [z]
+        in_specs.append(rows(INNER))
+        out_specs.insert(0, rows(INNER))
+        out_shape.insert(0, jax.ShapeDtypeStruct((tokens, INNER), BF16))
+        scratch.append(pltpu.VMEM((SPAN, INNER), F32))
     return pl.pallas_call(
-        forward_kernel,
+        partial(forward_kernel, z is not None),
         grid=(blocks,),
-        in_specs=[SMEM, rows(INNER), rows(XR), whole((8, CH)), whole((8, INNER)), whole((8, LANES)), whole((256, INNER))],
-        out_specs=[rows(INNER), rows(INNER), pl.BlockSpec((1, STATE, INNER), lambda i: (i, 0, 0))],
-        out_shape=[
-            jax.ShapeDtypeStruct((tokens, INNER), BF16),
-            jax.ShapeDtypeStruct((tokens, INNER), F32),
-            jax.ShapeDtypeStruct((blocks, STATE, INNER), F32),
-        ],
-        scratch_shapes=[
-            pltpu.VMEM((SPAN + 8, CH), F32),
-            pltpu.VMEM((SPAN, CH), F32),
-            pltpu.VMEM((STATE, INNER), F32),
-            pltpu.VMEM((SPAN, INNER), F32),
-        ],
+        in_specs=in_specs,
+        out_specs=out_specs,
+        out_shape=out_shape,
+        scratch_shapes=scratch,
         compiler_params=pltpu.CompilerParams(vmem_limit_bytes=VMEM_LIMIT),
-        cost_estimate=pl.CostEstimate(flops=20_000_000_000, bytes_accessed=30_000_000, transcendentals=6_000_000),
+        cost_estimate=pl.CostEstimate(flops=30_000_000_000, bytes_accessed=30_000_000, transcendentals=0),
         name="mixer_forward",
-    )(ends, z, xr, par, gain, hw, spread)
-
-
-def mixer_backward(ends, z, xr, dgn, ys, st, par, gain, hw, spread, gather, first, last, earlier=None):
-    tokens = z.shape[0]
+    )(ends, xr, par, gain, hw, spread, *more)
+
+
+def mixer_backward(ends, xr, ys, st, par, gain, hw, spread, gather, grads, first, last, earlier=None):
+    tokens = xr.shape[0]
     top = last - 1
+    fused = len(grads) == 2
     back = lambda width: pl.BlockSpec((SPAN, width), lambda i: (top - i, 0))
     halo = pl.BlockSpec((8, XR), lambda i: (jnp.maximum((top - i) * (SPAN // 8) - 1, 0), 0))
     if earlier is None:
         held, carried = [], [jnp.zeros((STATE, INNER), F32), jnp.zeros((8, CH), F32)]
     else:
-        held, carried = list(earlier[:2]), list(earlier[5:])
+        held, carried = list(earlier[:1]), list(earlier[4:6])
+    in_specs = [
+        SMEM,
+        back(XR),
+        halo,
+        back(INNER),
+        pl.BlockSpec((1, STATE, INNER), lambda i: (top - i, 0, 0)),
+        whole((8, CH)),
+        whole((8, INNER)),
+        whole((8, LANES)),
+        whole((256, INNER)),
+        whole((INNER, LANES)),
+    ]
+    in_specs += [back(INNER)] * len(grads)
+    held_at = len(in_specs)
+    in_specs += [pl.BlockSpec(memory_space=pl.ANY)] * len(held)
+    in_specs += [whole((STATE, INNER)), whole((8, CH))]
+    outs = [
+        (back(XR), (tokens, XR), BF16),
+        (whole((40, CH)), (40, CH), F32),
+        (whole((8, INNER)), (8, INNER), F32),
+        (whole((16, LANES)), (16, LANES), F32),
+        (whole((STATE, INNER)), (STATE, INNER), F32),
+        (whole((8, CH)), (8, CH), F32),
+    ]
+    scratch = [
+        pltpu.VMEM((SPAN + 8, CH), F32),
+        pltpu.VMEM((SPAN, CH), F32),
+        pltpu.VMEM((SPAN, CH), F32),
+        pltpu.VMEM((SPAN, CH), F32),
+        pltpu.VMEM((SPAN + 8, CH), F32),
+        pltpu.VMEM((SPAN, 2 * SPAN), F32),
+    ]
+    if fused:
+        outs += [(back(INNER), (tokens, INNER), BF16), (whole((8, INNER)), (8, INNER), F32)]
+        scratch += [pltpu.VMEM((SPAN, INNER), F32)] * 2
+    kernel = partial(backward_kernel, top, fused)
+    if fused:
+        def kernel(*refs):
+            plain, (dz_ref, dgate_ref), used, last_two = refs[: -10], refs[-10:-8], refs[-8:-2], refs[-2:]
+            backward_kernel(top, fused, *plain, *used, dz_ref, dgate_ref, *last_two)
+
     return pl.pallas_call(
-        partial(backward_kernel, top),
+        kernel,
         grid=(last - first,),
-        in_specs=[
-            SMEM,
-            back(INNER),
-            back(XR),
-            halo,
-            back(INNER),
-            back(INNER),
-            pl.BlockSpec((1, STATE, INNER), lambda i: (top - i, 0, 0)),
-            whole((8, CH)),
-            whole((8, INNER)),
-            whole((8, LANES)),
-            whole((256, INNER)),
-            whole((INNER, LANES)),
-        ]
-        + [pl.BlockSpec(memory_space=pl.ANY)] * len(held)
-        + [whole((STATE, INNER)), whole((8, CH))],
-        out_specs=[
-            back(INNER),
-            back(XR),
-            whole((40, CH)),
-            whole((16, INNER)),
-            whole((16, LANES)),
-            whole((STATE, INNER)),
-            whole((8, CH)),
-        ],
-        out_shape=[
-            jax.ShapeDtypeStruct((tokens, INNER), BF16),
-            jax.ShapeDtypeStruct((tokens, XR), BF16),
-            jax.ShapeDtypeStruct((40, CH), F32),
-            jax.ShapeDtypeStruct((16, INNER), F32),
-            jax.ShapeDtypeStruct((16, LANES), F32),
-            jax.ShapeDtypeStruct((STATE, INNER), F32),
-            jax.ShapeDtypeStruct((8, CH), F32),
-        ],
-        input_output_aliases={12 + k: k for k in range(len(held))},
-        scratch_shapes=[
-            pltpu.VMEM((SPAN + 8, CH), F32),
-            pltpu.VMEM((SPAN, CH), F32),
-            pltpu.VMEM((SPAN, CH), F32),
-            pltpu.VMEM((SPAN, CH), F32),
-            pltpu.VMEM((SPAN + 8, CH), F32),
-            pltpu.VMEM((SPAN, INNER), F32),
-            pltpu.VMEM((SPAN, 2 * SPAN), F32),
-        ],
+        in_specs=in_specs,
+        out_specs=[o[0] for o in outs],
+        out_shape=[jax.ShapeDtypeStruct(o[1], o[2]) for o in outs],
+        input_output_aliases={held_at + k: k for k in range(len(held))},
+        scratch_shapes=scratch,
         compiler_params=pltpu.CompilerParams(vmem_limit_bytes=VMEM_LIMIT),
         cost_estimate=pl.CostEstimate(
-            flops=7_500_000_000 * (last - first), bytes_accessed=6_000_000 * (last - first), transcendentals=0
+            flops=7_000_000_000 * (last - first), bytes_accessed=5_000_000 * (last - first), transcendentals=0
         ),
         name="mixer_backward",
-    )(ends, z, xr, xr, dgn, ys, st, par, gain, hw, spread, gather, *held, *carried)
-
-
-def finish_params(dpar, dgain, dhw):
+    )(ends, xr, xr, ys, st, par, gain, hw, spread, gather, *grads, *held, *carried)
+
+
+def norm_back_kernel(dz_ref, dxr_ref, wz_ref, wx_ref, h_ref, flow_ref, gain_ref, out_ref, dgain_ref):
+    @pl.when(pl.program_id(0) == 0)
+    def _():
+        dgain_ref[...] = jnp.zeros_like(dgain_ref)
+
+    dxn = raw_dot(dz_ref[...], wz_ref[...], NT) + raw_dot(dxr_ref[...], wx_ref[...], NT)
+    h = h_ref[...].astype(F32)
+    scale = lax.rsqrt(jnp.sum(h * h, axis=1, keepdims=True) / D + EPSILON)
+    scaled = dxn * gain_ref[0:1, :]
+    pull = jnp.sum(scaled * h, axis=1, keepdims=True) * (scale * scale * scale) / D
+    out_ref[...] = flow_ref[...] + (scale * scaled - h * pull)
+    dgain_ref[...] += partial8(dxn * (h * scale))
+
+
+def norm_backward(dz, dxr, wz, wx, h, flowing, gain):
+    tokens = dz.shape[0]
+    rows = lambda width: pl.BlockSpec((NORM_BLOCK, width), lambda i: (i, 0))
+    return pl.pallas_call(
+        norm_back_kernel,
+        grid=(tokens // NORM_BLOCK,),
+        in_specs=[rows(INNER), rows(XR), whole((D, INNER)), whole((D, XR)), rows(D), rows(D), whole((8, D))],
+        out_specs=[rows(D), whole((8, D))],
+        out_shape=[jax.ShapeDtypeStruct((tokens, D), F32), jax.ShapeDtypeStruct((8, D), F32)],
+        compiler_params=pltpu.CompilerParams(vmem_limit_bytes=VMEM_LIMIT),
+        cost_estimate=pl.CostEstimate(flops=1_000_000, bytes_accessed=1_000_000, transcendentals=0),
+        name="norm_backward",
+    )(dz, dxr, wz, wx, h, flowing, gain)
+
+
+def finish_params(dgate, dpar, dskip, dhw):
     dtaps = jnp.sum(dpar.reshape(5, 8, CH), axis=1).reshape(5 * CH)
-    dgate = jnp.sum(dgain[0:8], axis=0)
-    dskip = jnp.sum(dgain[8:16].reshape(8, NHEADS, HEADDIM), axis=(0, 2))
+    dgate = jnp.sum(dgate, axis=0)
+    dskip = jnp.sum(dskip.reshape(8, NHEADS, HEADDIM), axis=(0, 2))
     dh = jnp.sum(dhw.reshape(2, 8, LANES), axis=1)[:, :NHEADS]
     return jnp.concatenate([dgate, dtaps]), jnp.concatenate([dh, dskip[None]], axis=0)
 
@@ -528,32 +646,38 @@
     def steps_xy(self):
         return [(dy, dx) for dy in range(self.sizes["y"]) for dx in range(self.sizes["x"]) if dy or dx]
 
-    def scatter_axis(self, value, axis, at, wire=F32):
-        if axis == "xy":
-            ny, nx = self.sizes["y"], self.sizes["x"]
-
-            def block(dy, dx):
-                row = lax.dynamic_index_in_dim(value, (at["y"] + dy) % ny, 0)
-                return lax.dynamic_index_in_dim(row, (at["x"] + dx) % nx, 1)
-
-            total = block(0, 0)
-            for dy, dx in self.steps_xy():
-                total = total + self.shift_xy(block(dy, dx).astype(wire), dy, dx).astype(F32)
-            return total
-        n, dim = self.sizes[axis], self.order.index(axis)
-        total = lax.dynamic_index_in_dim(value, at[axis], dim)
-        for d in range(1, n):
-            part = lax.dynamic_index_in_dim(value, (at[axis] + d) % n, dim)
-            total = total + self.shift(part.astype(wire), axis, d).astype(F32)
+    def xy_sum(self, value, wire=F32):
+        plane = self.sizes["y"] * self.sizes["x"]
+        groups = [[2 * k + c for k in range(plane)] for c in range(2)]
+        value = value.reshape(plane, *value.shape[3:]).astype(wire)
+        got = lax.all_to_all(value, "dp", 0, 0, axis_index_groups=groups)
+        return jnp.sum(got.astype(F32), axis=0)
+
+    def z_sum(self, value, wire=F32):
+        count, at = self.sizes["z"], lax.axis_index("fsdp")
+        total = lax.dynamic_index_in_dim(value, at, 0, keepdims=False)
+        for d in range(1, count):
+            part = lax.dynamic_index_in_dim(value, (at + d) % count, 0, keepdims=False)
+            total = total + self.shift(part.astype(wire), "z", d).astype(F32)
         return total
+
+    def core_send(self, value, at):
+        return self.shift(lax.dynamic_index_in_dim(value, 1 - at["core"], 2), "core", 1)
+
+    def core_sum(self, value, got, at):
+        return lax.dynamic_index_in_dim(value, at["core"], 2) + got
 
     def blocks(self, whole):
         s = self.sizes
         return whole.reshape(s["y"], s["x"], s["core"], s["z"], -1, whole.shape[1])
 
-    def total(self, value):
-        value = value + self.shift(value, "core", 1)
-        value = value + sum(self.shift_xy(value, dy, dx) for dy, dx in self.steps_xy())
+    def total_core(self, value):
+        return value + self.shift(value, "core", 1)
+
+    def total_xy(self, value):
+        return value + sum(self.shift_xy(value, dy, dx) for dy, dx in self.steps_xy())
+
+    def total_z(self, value):
         return value + sum(self.shift(value, "z", d) for d in range(1, self.sizes["z"]))
 
 
@@ -614,7 +738,8 @@
     devices = rest.shape[0] // shard_rows
 
     def out_rows(columns):
-        return columns.reshape(devices, shard_rows, 2, D).swapaxes(1, 2).reshape(INNER, D)
+        columns = columns.reshape(devices, 1, shard_rows, 2 * D)
+        return jnp.concatenate([columns[..., :D], columns[..., D:]], axis=1).reshape(INNER, D)
 
     in_from = 2 * D
     out_from = in_from + INNER + XR
@@ -629,67 +754,79 @@
     stored = []
     for l in range(LAYERS):
         tables = kernel_params(vector_full[l], head_weight[l])
-        normed, norm_pull = jax.vjp(norm_part, stream, vector_full[l, :D])
-        normed = normed.astype(BF16)
+        normed_from = hidden_in if l == 0 else stream
+        normed = norm_part(stream, vector_full[l, :D]).astype(BF16)
         z = jnp.dot(normed, ins[l][0], preferred_element_type=F32)
         xr = jnp.dot(normed, ins[l][1], preferred_element_type=F32)
-        gn, ys, st = mixer_forward(ends, z, xr, *tables, spread)
+        gn, ys, st = mixer_forward(ends, xr, *tables, spread, z)
         stream = stream + jnp.dot(gn, outs[l], preferred_element_type=F32)
-        stored.append((norm_pull, normed, z, xr, gn, ys, st, tables))
+        stored.append((normed_from, normed, z, xr, gn, ys, st, tables))
+    fence = lax.optimization_barrier
+    blocks = token_count // SPAN
+    at = net.coordinates()
+    flowing = cotangent.astype(F32) * valid[:, None]
+    small_parts = [None] * LAYERS
+    arrived = [None] * LAYERS
+    in_sums = []
+
+    def product(a, b):
+        return jnp.einsum("td,tp->dp", a, b, preferred_element_type=F32)
+
+    for l in reversed(range(LAYERS)):
+        normed_from, normed, z, xr, gn, ys, st, tables = stored[l]
+        wire = BF16 if l == 0 else F32
+        gb = flowing.astype(BF16)
+        grad_out = product(gn, gb)
+        gb, grad_out = fence((gb, grad_out))
+        got = net.core_send(net.blocks(grad_out), at)
+        dgn = jnp.einsum("td,ed->te", gb, outs[l], preferred_element_type=F32)
+        dgn, grad_out, got = fence((dgn, grad_out, got))
+        out_sum = side_by_side(net.core_sum(net.blocks(grad_out), got, at))
+        waiting = jnp.concatenate(in_sums + [out_sum], axis=-1).astype(wire)
+        dgn, waiting, arrived = fence((dgn, waiting, arrived))
+        waiting = net.xy_sum(waiting, wire)
+        back = mixer_backward(ends, xr, ys, st, *tables, spread, gather, (z, dgn), 0, blocks)
+        back, waiting = fence((back, waiting))
+        if l > 0:
+            arrived[l] = net.z_sum(waiting, wire)
+        dxr, dz = back[0], back[6]
+        grads = [product(normed, dxr), product(normed, dz)]
+        dz, dxr, grads = fence((dz, dxr, grads))
+        got = [net.core_send(net.blocks(g), at) for g in grads]
+        if l == 0:
+            grads, got, in_late, out_late, vector_late = fence((grads, got, in_weight, out_weight, vector_weight))
+            in_sums = [net.core_sum(net.blocks(g), v, at) for g, v in zip(grads, got)]
+            in_zero = jnp.concatenate(in_sums, axis=-1).astype(BF16)
+            dz, dxr, in_zero, waiting = fence((dz, dxr, in_zero, waiting))
+            in_zero = net.xy_sum(in_zero, BF16)
+            arrived[0] = net.z_sum(waiting, wire)
+        gain = jnp.broadcast_to(vector_full[l, None, :D], (8, D))
+        flowing, dnorm = norm_backward(dz, dxr, *ins[l], normed_from, flowing, gain)
+        if l > 0:
+            flowing, grads, got = fence((flowing, grads, got))
+            in_sums = [net.core_sum(net.blocks(g), v, at) for g, v in zip(grads, got)]
+        dvec, dhead = finish_params(back[7], *back[1:4])
+        small_parts[l] = jnp.concatenate([jnp.sum(dnorm, axis=0), dvec, dhead.reshape(-1)])
+    small = jnp.stack(small_parts)
+    small = jnp.pad(small, ((0, 0), (0, -small.shape[1] % LANES))).reshape(-1, LANES)
     layer_out = stream.astype(BF16)
-    flowing = cotangent.astype(F32) * valid[:, None]
-    arrived = [None] * LAYERS
-    small_parts = [None] * LAYERS
-    travelling = []
-    at = net.coordinates()
-    blocks = token_count // SPAN
-    for l in reversed(range(LAYERS)):
-        norm_pull, normed, z, xr, gn, ys, st, tables = stored[l]
-        gb = flowing.astype(BF16)
-        grad_out = jnp.einsum("te,td->ed", gn, gb, preferred_element_type=F32)
-        gb, grad_out = lax.optimization_barrier((gb, grad_out))
-        out_sum = side_by_side(net.scatter_axis(net.blocks(grad_out), "core", at))
-        travelling = jnp.concatenate(travelling + [out_sum], axis=-1)
-        dgn = jnp.einsum("td,ed->te", gb, outs[l], preferred_element_type=F32)
-        dgn, travelling = lax.optimization_barrier((dgn, travelling))
-        travelling = net.scatter_axis(travelling, "xy", at, BF16)
-        dz, dxr, *sums = mixer_backward(ends, z, xr, dgn, ys, st, *tables, spread, gather, 0, blocks)[:5]
-        dz, dxr, travelling = lax.optimization_barrier((dz, dxr, travelling))
-        arrived[l] = net.scatter_axis(travelling, "z", at, BF16)
-        grad_x = jnp.einsum("td,tp->dp", normed, dxr, preferred_element_type=F32)
-        dz, dxr, grad_x = lax.optimization_barrier((dz, dxr, grad_x))
-        grad_z = jnp.einsum("td,tp->dp", normed, dz, preferred_element_type=F32)
-        dz, dxr, grad_z = lax.optimization_barrier((dz, dxr, grad_z))
-        travelling = [net.scatter_axis(net.blocks(g), "core", at) for g in (grad_x, grad_z)]
-        dxn = jnp.einsum("tp,dp->td", dz, ins[l][0], preferred_element_type=F32) + jnp.einsum(
-            "tp,dp->td", dxr, ins[l][1], preferred_element_type=F32
-        )
-        grad_stream, dnorm = norm_pull(dxn)
-        flowing = flowing + grad_stream
-        dvec, dhead = finish_params(*sums)
-        small_parts[l] = jnp.concatenate([dnorm, dvec, dhead.reshape(-1)])
-    travelling_late = travelling
-    for axis in ("xy", "z"):
-        travelling = [net.scatter_axis(v, axis, at, BF16) for v in travelling]
-    flat = [v.reshape(-1, v.shape[-1]) for v in (arrived[1], arrived[0], *travelling)]
-    in_parts = [
-        jnp.concatenate([flat[3], flat[2]], axis=1)[:, :P_SIZE],
-        jnp.concatenate([flat[1][:, XR : XR + INNER], flat[1][:, :XR]], axis=1)[:, :P_SIZE],
-    ]
-    out_parts = [
-        jnp.concatenate([v[:, -2 * D : -D], v[:, -D:]], axis=0) for v in (flat[1], flat[0])
-    ]
-    late, _ = lax.optimization_barrier(((in_weight, out_weight, vector_weight), travelling_late))
-    weight_squares = [jnp.sum(w * w, axis=tuple(range(1, w.ndim))) for w in late]
-    small = jnp.stack(small_parts)
-    small = net.total(jnp.pad(small, ((0, 0), (0, -small.shape[1] % LANES))).reshape(-1, LANES))
-    small = small.reshape(LAYERS, -1)
+    weight_squares = [jnp.sum(w * w, axis=tuple(range(1, w.ndim))) for w in (in_late, out_late, vector_late)]
+    small = net.total_core(small)
+    small, in_zero, arrived, flowing, layer_out, weight_squares = fence(
+        (small, in_zero, arrived, flowing, layer_out, weight_squares)
+    )
+    in_zero = net.z_sum(in_zero, BF16)
+    small = net.total_xy(small)
+    in_zero, small = fence((in_zero, small))
+    small = net.total_z(small).reshape(LAYERS, -1)
     head_total = small[:, VEC : VEC + 3 * NHEADS].reshape(LAYERS, 3, NHEADS)
     share = VEC // devices
     mine = lax.axis_index("dp") * lax.axis_size("fsdp") + lax.axis_index("fsdp")
     grad_vector = lax.dynamic_slice(small, (0, mine * share), (LAYERS, share))
-    grad_in = jnp.stack(in_parts)
-    grad_out = jnp.stack(out_parts)
+    grad_in = jnp.stack(
+        [jnp.concatenate([v[:, XR : XR + INNER], v[:, : P_SIZE - INNER]], axis=1) for v in (in_zero, arrived[0])]
+    )
+    grad_out = jnp.stack([jnp.concatenate([v[:, -2 * D : -D], v[:, -D:]], axis=0) for v in arrived])
     squares_in = grad_in * grad_in
     squares_out = grad_out * grad_out
     row_in = MOMENT_DECAY * in_row_moment + (1.0 - MOMENT_DECAY) * jnp.mean(squares_in, axis=2)
@@ -717,7 +854,7 @@
         edges.append(edges[-1] + v.shape[1])
     summed = jnp.concatenate(local, axis=1)
     summed = jnp.pad(summed, ((0, 0), (0, -edges[-1] % LANES))).reshape(-1, LANES)
-    summed = net.total(summed).reshape(LAYERS, -1)
+    summed = net.total_z(net.total_xy(net.total_core(summed))).reshape(LAYERS, -1)
     column_in, column_out, scaled_in, scaled_out, totals = [
         summed[:, a:b] for a, b in zip(edges[:-1], edges[1:])
     ]

time: 574 us -> 536 us (0.934)
  matrix products: 86.2 us -> 63.7 us
  local copies, waits for them, and re-layouts: 72.6 us -> 55.3 us
  waiting for transfers between devices: 73.4 us -> 87 us
  other arithmetic: 69.8 us -> 58.7 us
  starting transfers between devices: 65.4 us -> 55.5 us
    ppermute x24 -> x21, waiting for transfers between devices: 21 us -> 56.3 us  [shift(): return lax.ppermute(value, 'fsdp', [(i, (i + by) % n) for i in range(n)])]
    ppermute x18 -> x6, waiting for transfers between devices: 26.2 us -> 3.6 us  [shift_xy(): return lax.ppermute(value, 'dp', pairs)]
    dot_general x10 -> x6, matrix products: 44.6 us -> 22.5 us  [product(): return jnp.einsum('td,tp->dp', a, b, preferred_element_type=F32)]
    add x17 -> x10, other arithmetic: 23.2 us -> 7.74 us  [the longest x3 3.02 us: z_sum(): total = total + self.shift(part.astype(wire), 'z', d).astype(F32)]
    ppermute x18 -> x6, starting transfers between devices: 21.7 us -> 7.04 us  [shift_xy(): return lax.ppermute(value, 'dp', pairs)]
    all_to_all x0 -> x3, starting transfers between devices: none -> 12.7 us  [xy_sum(): got = lax.all_to_all(value, 'dp', 0, 0, axis_index_groups=groups)]
    reshape x6 -> x4, local copies, waits for them, and re-layouts: 11.4 us -> 0.25 us  [the longest x2 0.17 us: on_device(): dhead.reshape(-1)]
    unnamed x174 -> x168, local copies, waits for them, and re-layouts: 30.2 us -> 20 us
  transfers between devices with their start and end apart: 57 -> 45, of which waited for: 18 -> 21; matrix products, arithmetic and copies ran while one was open for 20% -> 16% of each run, Pallas kernels for 27% -> 28%
where the time goes in v3:
time: 536 us; the launch traced here: 526 us
  Pallas kernels  187 us (35%)
  waiting for transfers between devices  87 us (16%)
  matrix products  63.7 us (12%)
  other arithmetic  58.7 us (11%)
  starting transfers between devices  55.5 us (10%)
  local copies, waits for them, and re-layouts  55.3 us (10%)
  between operations  18.4 us (3%)
    pallas_call x2, Pallas kernels, mixer_backward(): pl.pallas_call(kernel, grid=(last - first,), in_specs=in_specs, out_specs...  106 us
    pallas_call x2, Pallas kernels, mixer_forward(): pl.pallas_call(partial(forward_kernel, z is not None), grid=(blocks,), in...  57 us
    ppermute x21, waiting for transfers between devices, shift(): return lax.ppermute(value, 'fsdp', [(i, (i + by) % n) for i in range(n)])  56.3 us
    ppermute x21, starting transfers between devices, shift(): return lax.ppermute(value, 'fsdp', [(i, (i + by) % n) for i in range(n)])  28.6 us
    pallas_call x2, Pallas kernels, norm_backward(): pl.pallas_call(norm_back_kernel, grid=(tokens // NORM_BLOCK,), in_specs=[...  24.5 us
    ppermute x14, waiting for transfers between devices, shift(): return lax.ppermute(value, 'dp', pairs)  23.3 us
    dot_general x6, matrix products, product(): return jnp.einsum('td,tp->dp', a, b, preferred_element_type=F32)  22.5 us
    unnamed x168, local copies, waits for them, and re-layouts  20 us
  transfers between devices with their start and end apart: 45, of which 21 were waited for; matrix products, arithmetic and copies ran while one was open for 16% of the time, Pallas kernels for 28%

profile of v3, /device:TPU:0, one launch (start us, length us, event | category | flops | bytes accessed | tf_op | source)
XLA Modules:
  0.0 526.2 jit_solution(17473455055622054412)
XLA Ops:
  31.7 3.9 collective-permute-done
  38.8 11.6 %collective-permute-done.3 = bf16[1,1,1,4,24,2048]{5,4,3,2,1,0:T(8,128)(2,1)S(1)} collective-permute-done((bf16[1,1,1,4,24,2048]{5,4,3,2,1,0:T(8,128)(2,1)S(1)}, bf16[1,1,1,4,24,2048]{5,4,3,2,1,0:T(8,128)(2,1)S(1)}, u32[]{:S(2)}, u32[]{:S(2)}) %collective-permute-start.3) | collective-permute-done | bytes 393248 | tf_op jit(solution)/shard_map/ppermute | solution.py:617
  56.7 10.5 %collective-permute-done.10 = bf16[2,1,1,4,24,1536]{5,4,3,2,1,0:T(8,128)(2,1)S(1)} collective-permute-done((bf16[2,1,1,4,24,1536]{5,4,3,2,1,0:T(8,128)(2,1)}, bf16[2,1,1,4,24,1536]{5,4,3,2,1,0:T(8,128)(2,1)S(1)}, u32[]{:S(2)}, u32[]{:S(2)}) %collective-permute-start.10) | collective-permute-done | bytes 589856 | tf_op jit(solution)/shard_map/ppermute | solution.py:617
  80.9 7.1 %fusion.54.refs_0_.refs_10_ = f32[1024,1536]{1,0:T(8,128)} fusion(bf16[768,1536]{1,0:T(8,128)(2,1)} %bitcast.191, bf16[1024,768]{1,0:T(8,128)(2,1)S(1)} %copy-done, f32[768]{0:T(1024)S(1)} %get-tuple-element.284, f32[1024]{0:T(1024)S(1)} %add_rsqrt_fusion.1), kind=kOutput, calls=%fused_computation.209 | convolution fusion | flops 2419064832 | bytes 10230784 | tf_op jit(solution)/shard_map/dot_general | solution.py:759
  88.0 5.7 %fusion.48.xr_ref.refs_1_.refs_2_ = f32[1024,1920]{1,0:T(8,128)} fusion(bf16[768,2048]{1,0:T(8,128)(2,1)S(1)} %bitcast.187, bf16[1024,768]{1,0:T(8,128)(2,1)S(1)} %copy-done, f32[768]{0:T(1024)S(1)} %get-tuple-element.284, f32[1024]{0:T(1024)S(1)} %add_rsqrt_fusion.1), kind=kOutput, calls=%fused_computation.205 | convolution fusion | flops 3023044608 | bytes 12394496 | tf_op jit(solution)/shard_map/dot_general | solution.py:760
  93.8 28.4 %mixer_forward.2 = (bf16[1024,1536]{1,0:T(8,128)(2,1)}, f32[1024,1536]{1,0:T(8,128)}, f32[8,128,1536]{2,1,0:T(8,128)}) custom-call(s32[4]{0:T(128)} %pad_add_fusion.ends_ref.refs_0_, f32[1024,1920]{1,0:T(8,128)} %fusion.48.xr_ref.refs_1_.refs_2_, f32[8,1792]{1,0:T(8,128)} %concatenate.107.par_ref.refs_5_, f32[8,1536]{1,0:T(8,128)} %get-tuple-element.379.gain_ref.refs_6_, ...), custom_call_target="tpu_custom_call" | custom-call | flops 30000001024 | bytes 30000000 | tf_op jit(solution)/shard_map/mixer_forward/pallas_call | solution.py:476
  122.2 5.7 %fusion.66 = (bf16[768,1536]{1,0:T(8,128)(2,1)}, bf16[768,1536]{1,0:T(8,128)(2,1)}, bf16[768,1536]{1,0:T(8,128)(2,1)S(1)}) fusion(bf16[768,6528]{1,0:T(8,128)(2,1)} %all-gather.2.cloned.1.call-done), kind=kLoop, calls=%fused_computation.216 | loop fusion | bytes 14155776 | tf_op jit(solution)/shard_map/slice | solution.py:748
  135.1 4.7 fusion.44.refs_0_.refs_10_
  139.7 5.6 %fusion.46.xr_ref.refs_1_.refs_2_ = f32[1024,1920]{1,0:T(8,128)} fusion(bf16[1024,768]{1,0:T(8,128)(2,1)S(1)} %multiply_convert_fusion, bf16[768,6528]{1,0:T(8,128)(2,1)S(1)} %bitcast.190), kind=kOutput, calls=%fused_computation.203 | convolution fusion | flops 3019898880 | bytes 12386304 | tf_op jit(solution)/shard_map/dot_general | solution.py:760
  145.3 28.6 %mixer_forward.3 = (bf16[1024,1536]{1,0:T(8,128)(2,1)}, f32[1024,1536]{1,0:T(8,128)}, f32[8,128,1536]{2,1,0:T(8,128)}) custom-call(s32[4]{0:T(128)} %pad_add_fusion.ends_ref.refs_0_, f32[1024,1920]{1,0:T(8,128)} %fusion.46.xr_ref.refs_1_.refs_2_, f32[8,1792]{1,0:T(8,128)} %concatenate.115.par_ref.refs_5_, f32[8,1536]{1,0:T(8,128)} %get-tuple-element.378.gain_ref.refs_6_, ...), custom_call_target="tpu_custom_call" | custom-call | flops 30000001024 | bytes 30000000 | tf_op jit(solution)/shard_map/mixer_forward/pallas_call | solution.py:476
  173.9 4.6 fusion.75
  183.5 4.6 fusion.76.refs_11_
  197.2 53.0 %mixer_backward.2 = (bf16[1024,1920]{1,0:T(8,128)(2,1)}, f32[40,1792]{1,0:T(8,128)}, f32[8,1536]{1,0:T(8,128)}, f32[16,128]{1,0:T(8,128)}, f32[128,1536]{1,0:T(8...) custom-call(s32[4]{0:T(128)} %pad_add_fusion.ends_ref.refs_0_, ...), custom_call_target="tpu_custom_call" | custom-call | flops 56000000000 | bytes 40000000 | tf_op jit(solution)/shard_map/mixer_backward/pallas_call | solution.py:540
  250.4 5.2 fusion.78
  268.0 12.4 %norm_backward.2 = (f32[1024,768]{1,0:T(8,128)}, f32[8,768]{1,0:T(8,128)}) custom-call(bf16[1024,1536]{1,0:T(8,128)(2,1)} %get-tuple-element.128.dz_ref, bf16[1024,1920]{1,0:T(8,128)(2,1)} %get-tuple-element.129.dxr_ref, bf16[768,1536]{1,0:T(8,128)(2,1)} %get-tuple-element.313.wz_ref, bf16[768,1920]{1,0:T(8,128)(2,1)} %slice.300.wx_ref, ...), custom_call_target="tpu_custom_call" | custom-call | flops 1000000 | bytes 1000000 | tf_op jit(solution)/shard_map/norm_backward/pallas_call | solution.py:573
  293.8 4.9 collective-permute-done.16
  301.3 5.6 %collective-permute-done.17 = f32[24,1536]{1,0:T(8,128)S(1)} collective-permute-done((f32[24,1536]{1,0:T(8,128)S(1)}, f32[24,1536]{1,0:T(8,128)S(1)}, u32[]{:S(2)}, u32[]{:S(2)}) %collective-permute-start.17) | collective-permute-done | bytes 147488 | tf_op jit(solution)/shard_map/ppermute | solution.py:611
  313.7 5.1 fusion.80.refs_11_
  321.2 4.8 all-to-all-start.1
  326.0 52.9 %mixer_backward.3 = (bf16[1024,1920]{1,0:T(8,128)(2,1)}, f32[40,1792]{1,0:T(8,128)}, f32[8,1536]{1,0:T(8,128)}, f32[16,128]{1,0:T(8,128)}, f32[128,1536]{1,0:T(8...) custom-call(s32[4]{0:T(128)} %pad_add_fusion.ends_ref.refs_0_, ...), custom_call_target="tpu_custom_call" | custom-call | flops 56000000000 | bytes 40000000 | tf_op jit(solution)/shard_map/mixer_backward/pallas_call | solution.py:540
  379.0 4.3 convert_reduce_fusion
  399.8 5.7 %add_convert_fusion = bf16[1024,768]{1,0:T(8,128)(2,1)} fusion(f32[1024,768]{1,0:T(8,128)S(1)} %copy-done.8, bf16[1024,1536]{1,0:T(8,128)(2,1)} %get-tuple-element.112, bf16[1536,768]{1,0:T(8,128)(2,1)S(1)} %bitcast.207), kind=kOutput, calls=%fused_computation.10 | convolution fusion | flops 2417491968 | bytes 10223616 | tf_op jit(solution)/shard_map/dot_general | solution.py:762
  414.9 12.1 %norm_backward.3 = (f32[1024,768]{1,0:T(8,128)}, f32[8,768]{1,0:T(8,128)}) custom-call(bf16[1024,1536]{1,0:T(8,128)(2,1)} %get-tuple-element.163.dz_ref, bf16[1024,1920]{1,0:T(8,128)(2,1)} %get-tuple-element.164.dxr_ref, bf16[768,1536]{1,0:T(8,128)(2,1)} %bitcast.192, bf16[768,1920]{1,0:T(8,128)(2,1)} %slice.288.wx_ref, bf16[1024,768]{1,0:T(8,128)(2,1)} %h_ref.1, ...), custom_call_target="tpu_custom_call" | custom-call | flops 1000000 | bytes 1000000 | tf_op jit(solution)/shard_map/norm_backward/pallas_call | solution.py:573
  427.8 4.3 all-to-all-start.2
  434.3 3.8 collective-permute-start.24
  441.1 4.0 collective-permute-done.22
  445.1 4.2 collective-permute-done.24
  449.3 8.3 %collective-permute-done.23 = bf16[24,4992]{1,0:T(8,128)(2,1)} collective-permute-done((bf16[24,4992]{1,0:T(8,128)(2,1)}, bf16[24,4992]{1,0:T(8,128)(2,1)}, u32[]{:S(2)}, u32[]{:S(2)}) %collective-permute-start.23) | collective-permute-done | bytes 239648 | tf_op jit(solution)/shard_map/ppermute | solution.py:611
  459.9 3.8 all-to-all-done.2
  470.5 3.8 collective-permute-start.27
  475.6 3.9 collective-permute-done.25
  479.5 7.0 %collective-permute-done.26 = bf16[24,3456]{1,0:T(8,128)(2,1)S(1)} collective-permute-done((bf16[24,3456]{1,0:T(8,128)(2,1)S(1)}, bf16[24,3456]{1,0:T(8,128)(2,1)S(1)}, u32[]{:S(2)}, u32[]{:S(2)}) %collective-permute-start.26) | collective-permute-done | bytes 165920 | tf_op jit(solution)/shard_map/ppermute | solution.py:611
  (425 shorter events, 177.7 us)
Async XLA Ops:
  7.2 114.9 %all-gather.2.cloned.1.call-start = ((), (), s32[]{:S(2)}) async-start(), calls=%async_computation.3 | async-start | bytes 10340352 | tf_op jit(solution)/shard_map/all_gather | solution.py:732
  10.3 13.5 %collective-permute-start.8 = (bf16[1,1,1,1,24,1536]{5,4,3,2,1,0:T(8,128)(2,1)S(1)}, bf16[1,1,1,1,24,1536]{5,4,3,2,1,0:T(8,128)(2,1)S(1)}, u32[]{:S(2)}, u32[]{:S(2)}) collective-permute-start(bf16[1,1,1,1,24,1536]{5,4,3,2,1,0:T(8,128)(2,1)S(1)} %slice_bitcast_fusion), channel_id=1, source_target_pairs={{0,1},{1,2},{2,3},{3,0},{4,5},{5,6},{6,7},{7,4},{8,9},{9,10},{10,1... | collective-permute-start | bytes 221192 | tf_op jit(solution)/shard_map/ppermute | solution.py:611
  13.4 13.3 %collective-permute-start.7 = (bf16[1,1,1,1,24,1536]{5,4,3,2,1,0:T(8,128)(2,1)S(1)}, bf16[1,1,1,1,24,1536]{5,4,3,2,1,0:T(8,128)(2,1)S(1)}, u32[]{:S(2)}, u32[]{:S(2)}) collective-permute-start(bf16[1,1,1,1,24,1536]{5,4,3,2,1,0:T(8,128)(2,1)S(1)} %slice_bitcast_fusion), channel_id=1, source_target_pairs={{0,2},{1,3},{2,0},{3,1},{4,6},{5,7},{6,4},{7,5},{8,10},{9,11},{10,... | collective-permute-start | bytes 221192 | tf_op jit(solution)/shard_map/ppermute | solution.py:611
  16.0 10.7 %collective-permute-start.6 = (bf16[1,1,1,1,24,1536]{5,4,3,2,1,0:T(8,128)(2,1)S(1)}, bf16[1,1,1,1,24,1536]{5,4,3,2,1,0:T(8,128)(2,1)S(1)}, u32[]{:S(2)}, u32[]{:S(2)}) collective-permute-start(bf16[1,1,1,1,24,1536]{5,4,3,2,1,0:T(8,128)(2,1)S(1)} %slice_bitcast_fusion), channel_id=1, source_target_pairs={{0,3},{1,0},{2,1},{3,2},{4,7},{5,4},{6,5},{7,6},{8,11},{9,8},{10,9... | collective-permute-start | bytes 221192 | tf_op jit(solution)/shard_map/ppermute | solution.py:611
  17.5 10.9 %collective-permute-start.2 = (bf16[1,1,1,1,24,2048]{5,4,3,2,1,0:T(8,128)(2,1)S(1)}, bf16[1,1,1,1,24,2048]{5,4,3,2,1,0:T(8,128)(2,1)S(1)}, u32[]{:S(2)}, u32[]{:S(2)}) collective-permute-start(bf16[1,1,1,1,24,2048]{5,4,3,2,1,0:T(8,128)(2,1)S(1)} %maximum_bitcast_fusion.4), channel_id=1, source_target_pairs={{0,1},{1,2},{2,3},{3,0},{4,5},{5,6},{6,7},{7,4},{8,9},{9,10},{10,1... | collective-permute-start | bytes 294920 | tf_op jit(solution)/shard_map/ppermute | solution.py:611
  18.2 13.5 %collective-permute-start.1 = (bf16[1,1,1,1,24,2048]{5,4,3,2,1,0:T(8,128)(2,1)S(1)}, bf16[1,1,1,1,24,2048]{5,4,3,2,1,0:T(8,128)(2,1)S(1)}, u32[]{:S(2)}, u32[]{:S(2)}) collective-permute-start(bf16[1,1,1,1,24,2048]{5,4,3,2,1,0:T(8,128)(2,1)S(1)} %maximum_bitcast_fusion.4), channel_id=1, source_target_pairs={{0,2},{1,3},{2,0},{3,1},{4,6},{5,7},{6,4},{7,5},{8,10},{9,11},{10,... | collective-permute-start | bytes 294920 | tf_op jit(solution)/shard_map/ppermute | solution.py:611
  23.9 11.7 %collective-permute-start = (bf16[1,1,1,1,24,2048]{5,4,3,2,1,0:T(8,128)(2,1)S(1)}, bf16[1,1,1,1,24,2048]{5,4,3,2,1,0:T(8,128)(2,1)S(1)}, u32[]{:S(2)}, u32[]{:S(2)}) collective-permute-start(bf16[1,1,1,1,24,2048]{5,4,3,2,1,0:T(8,128)(2,1)S(1)} %maximum_bitcast_fusion.4), channel_id=1, source_target_pairs={{0,3},{1,0},{2,1},{3,2},{4,7},{5,4},{6,5},{7,6},{8,11},{9,8},{10,9... | collective-permute-start | bytes 294920 | tf_op jit(solution)/shard_map/ppermute | solution.py:611
  26.8 10.5 %collective-permute-start.9 = (bf16[1,1,1,4,24,1536]{5,4,3,2,1,0:T(8,128)(2,1)S(1)}, bf16[1,1,1,4,24,1536]{5,4,3,2,1,0:T(8,128)(2,1)S(1)}, u32[]{:S(2)}, u32[]{:S(2)}) collective-permute-start(bf16[1,1,1,4,24,1536]{5,4,3,2,1,0:T(8,128)(2,1)S(1)} %pad_maximum_fusion.13), channel_id=1, source_target_pairs={{0,16},{4,20},{8,24},{12,28},{16,0},{20,4},{24,8},{28,12},{1,17},{... | collective-permute-start | bytes 884744 | tf_op jit(solution)/shard_map/ppermute | solution.py:617
  35.8 14.6 %collective-permute-start.3 = (bf16[1,1,1,4,24,2048]{5,4,3,2,1,0:T(8,128)(2,1)S(1)}, bf16[1,1,1,4,24,2048]{5,4,3,2,1,0:T(8,128)(2,1)S(1)}, u32[]{:S(2)}, u32[]{:S(2)}) collective-permute-start(bf16[1,1,1,4,24,2048]{5,4,3,2,1,0:T(8,128)(2,1)S(1)} %pad_maximum_fusion.12), channel_id=1, source_target_pairs={{0,8},{4,12},{8,0},{12,4},{16,24},{20,28},{24,16},{28,20},{1,9},{5... | collective-permute-start | bytes 1179656 | tf_op jit(solution)/shard_map/ppermute | solution.py:617
  38.3 29.0 %collective-permute-start.10 = (bf16[2,1,1,4,24,1536]{5,4,3,2,1,0:T(8,128)(2,1)}, bf16[2,1,1,4,24,1536]{5,4,3,2,1,0:T(8,128)(2,1)S(1)}, u32[]{:S(2)}, u32[]{:S(2)}) collective-permute-start(bf16[2,1,1,4,24,1536]{5,4,3,2,1,0:T(8,128)(2,1)} %pad_maximum_fusion.11), channel_id=1, source_target_pairs={{0,8},{4,12},{8,0},{12,4},{16,24},{20,28},{24,16},{28,20},{1,9},{5... | collective-permute-start | bytes 1769480 | tf_op jit(solution)/shard_map/ppermute | solution.py:617
  51.4 16.2 %collective-permute-start.4 = (bf16[1,2,1,4,24,2048]{5,4,3,2,1,0:T(8,128)(2,1)}, bf16[1,2,1,4,24,2048]{5,4,3,2,1,0:T(8,128)(2,1)}, u32[]{:S(2)}, u32[]{:S(2)}) collective-permute-start(bf16[1,2,1,4,24,2048]{5,4,3,2,1,0:T(8,128)(2,1)} %pad_maximum_fusion.9), channel_id=1, source_target_pairs={{0,16},{4,20},{8,24},{12,28},{16,0},{20,4},{24,8},{28,12},{1,17},{... | collective-permute-start | bytes 2359304 | tf_op jit(solution)/shard_map/ppermute | solution.py:617
  191.9 58.3 %all-to-all-start = ((f32[4,4,24,1536]{3,2,1,0:T(8,128)}), f32[4,4,24,1536]{3,2,1,0:T(8,128)S(1)}, u32[]{:S(2)}, u32[]{:S(2)}) async-start(f32[4,4,24,1536]{3,2,1,0:T(8,128)} %bitcast.195), calls=%async_computation | async-start | bytes 4718592 | tf_op jit(solution)/shard_map/all_to_all | solution.py:653
  261.6 18.9 %collective-permute-start.13 = (f32[2,2,1,4,24,1920]{5,4,3,2,1,0:T(8,128)S(1)}, f32[2,2,1,4,24,1920]{5,4,3,2,1,0:T(8,128)}, u32[]{:S(2)}, u32[]{:S(2)}) collective-permute-start(f32[2,2,1,4,24,1920]{5,4,3,2,1,0:T(8,128)S(1)} %constant_dynamic-slice_fusion.5), channel_id=1, source_target_pairs={{0,4},{4,0},{8,12},{12,8},{16,20},{20,16},{24,28},{28,24},{1,5},{5... | collective-permute-start | bytes 8847368 | tf_op jit(solution)/shard_map/ppermute | solution.py:617
  263.5 16.9 %collective-permute-start.14 = (f32[2,2,1,4,24,1536]{5,4,3,2,1,0:T(8,128)}, f32[2,2,1,4,24,1536]{5,4,3,2,1,0:T(8,128)}, u32[]{:S(2)}, u32[]{:S(2)}) collective-permute-start(f32[2,2,1,4,24,1536]{5,4,3,2,1,0:T(8,128)} %constant_dynamic-slice_fusion.4), channel_id=1, source_target_pairs={{0,4},{4,0},{8,12},{12,8},{16,20},{20,16},{24,28},{28,24},{1,5},{5... | collective-permute-start | bytes 7077896 | tf_op jit(solution)/shard_map/ppermute | solution.py:617
  289.0 29.8 %collective-permute-start.15 = (f32[2,2,1,4,48,768]{5,4,3,2,1,0:T(8,128)}, f32[2,2,1,4,48,768]{5,4,3,2,1,0:T(8,128)S(1)}, u32[]{:S(2)}, u32[]{:S(2)}) collective-permute-start(f32[2,2,1,4,48,768]{5,4,3,2,1,0:T(8,128)} %constant_dynamic-slice_fusion.3), channel_id=1, source_target_pairs={{0,4},{4,0},{8,12},{12,8},{16,20},{20,16},{24,28},{28,24},{1,5},{5... | collective-permute-start | bytes 7077896 | tf_op jit(solution)/shard_map/ppermute | solution.py:617
  290.0 8.7 %collective-permute-start.16 = (f32[24,1536]{1,0:T(8,128)}, f32[24,1536]{1,0:T(8,128)S(1)}, u32[]{:S(2)}, u32[]{:S(2)}) collective-permute-start(f32[24,1536]{1,0:T(8,128)} %get-tuple-element.342), channel_id=1, source_target_pairs={{0,1},{1,2},{2,3},{3,0},{4,5},{5,6},{6,7},{7,4},{8,9},{9,10},{10,1... | collective-permute-start | bytes 442376 | tf_op jit(solution)/shard_map/ppermute | solution.py:611
  291.9 9.5 %collective-permute-start.18 = (f32[24,1536]{1,0:T(8,128)}, f32[24,1536]{1,0:T(8,128)S(1)}, u32[]{:S(2)}, u32[]{:S(2)}) collective-permute-start(f32[24,1536]{1,0:T(8,128)} %get-tuple-element.343), channel_id=1, source_target_pairs={{0,3},{1,0},{2,1},{3,2},{4,7},{5,4},{6,5},{7,6},{8,11},{9,8},{10,9... | collective-permute-start | bytes 442376 | tf_op jit(solution)/shard_map/ppermute | solution.py:611
  293.8 13.2 %collective-permute-start.17 = (f32[24,1536]{1,0:T(8,128)S(1)}, f32[24,1536]{1,0:T(8,128)S(1)}, u32[]{:S(2)}, u32[]{:S(2)}) collective-permute-start(f32[24,1536]{1,0:T(8,128)S(1)} %get-tuple-element.344), channel_id=1, source_target_pairs={{0,2},{1,3},{2,0},{3,1},{4,6},{5,7},{6,4},{7,5},{8,10},{9,11},{10,... | collective-permute-start | bytes 442376 | tf_op jit(solution)/shard_map/ppermute | solution.py:611
  321.2 57.8 %all-to-all-start.1 = ((bf16[4,4,24,4992]{3,2,1,0:T(8,128)(2,1)}), bf16[4,4,24,4992]{3,2,1,0:T(8,128)(2,1)}, u32[]{:S(2)}, u32[]{:S(2)}) async-start(bf16[4,4,24,4992]{3,2,1,0:T(8,128)(2,1)} %bitcast.185), calls=%async_computation.1 | async-start | bytes 7667712 | tf_op jit(solution)/shard_map/all_to_all | solution.py:653
  393.2 13.3 %collective-permute-start.19 = (f32[2,2,1,4,24,1920]{5,4,3,2,1,0:T(8,128)}, f32[2,2,1,4,24,1920]{5,4,3,2,1,0:T(8,128)}, u32[]{:S(2)}, u32[]{:S(2)}) collective-permute-start(f32[2,2,1,4,24,1920]{5,4,3,2,1,0:T(8,128)} %constant_dynamic-slice_fusion.2), channel_id=1, source_target_pairs={{0,4},{4,0},{8,12},{12,8},{16,20},{20,16},{24,28},{28,24},{1,5},{5... | collective-permute-start | bytes 8847368 | tf_op jit(solution)/shard_map/ppermute | solution.py:617
  394.9 11.6 %collective-permute-start.20 = (f32[2,2,1,4,24,1536]{5,4,3,2,1,0:T(8,128)}, f32[2,2,1,4,24,1536]{5,4,3,2,1,0:T(8,128)}, u32[]{:S(2)}, u32[]{:S(2)}) collective-permute-start(f32[2,2,1,4,24,1536]{5,4,3,2,1,0:T(8,128)} %constant_dynamic-slice_fusion.1), channel_id=1, source_target_pairs={{0,4},{4,0},{8,12},{12,8},{16,20},{20,16},{24,28},{28,24},{1,5},{5... | collective-permute-start | bytes 7077896 | tf_op jit(solution)/shard_map/ppermute | solution.py:617
  427.8 35.9 %all-to-all-start.2 = ((bf16[4,4,24,3456]{3,2,1,0:T(8,128)(2,1)}), bf16[4,4,24,3456]{3,2,1,0:T(8,128)(2,1)S(1)}, u32[]{:S(2)}, u32[]{:S(2)}) async-start(bf16[4,4,24,3456]{3,2,1,0:T(8,128)(2,1)} %bitcast.56), calls=%async_computation.2 | async-start | bytes 5308416 | tf_op jit(solution)/shard_map/all_to_all | solution.py:653
  434.3 10.8 %collective-permute-start.22 = (bf16[24,4992]{1,0:T(8,128)(2,1)}, bf16[24,4992]{1,0:T(8,128)(2,1)}, u32[]{:S(2)}, u32[]{:S(2)}) collective-permute-start(bf16[24,4992]{1,0:T(8,128)(2,1)} %get-tuple-element.326), channel_id=1, source_target_pairs={{0,1},{1,2},{2,3},{3,0},{4,5},{5,6},{6,7},{7,4},{8,9},{9,10},{10,1... | collective-permute-start | bytes 718856 | tf_op jit(solution)/shard_map/ppermute | solution.py:611
  434.3 15.1 %collective-permute-start.24 = (bf16[24,4992]{1,0:T(8,128)(2,1)}, bf16[24,4992]{1,0:T(8,128)(2,1)}, u32[]{:S(2)}, u32[]{:S(2)}) collective-permute-start(bf16[24,4992]{1,0:T(8,128)(2,1)} %get-tuple-element.327), channel_id=1, source_target_pairs={{0,3},{1,0},{2,1},{3,2},{4,7},{5,4},{6,5},{7,6},{8,11},{9,8},{10,9... | collective-permute-start | bytes 718856 | tf_op jit(solution)/shard_map/ppermute | solution.py:611
  438.1 19.5 %collective-permute-start.23 = (bf16[24,4992]{1,0:T(8,128)(2,1)}, bf16[24,4992]{1,0:T(8,128)(2,1)}, u32[]{:S(2)}, u32[]{:S(2)}) collective-permute-start(bf16[24,4992]{1,0:T(8,128)(2,1)} %get-tuple-element.328), channel_id=1, source_target_pairs={{0,2},{1,3},{2,0},{3,1},{4,6},{5,7},{6,4},{7,5},{8,10},{9,11},{10,... | collective-permute-start | bytes 718856 | tf_op jit(solution)/shard_map/ppermute | solution.py:611
  465.2 9.2 %collective-permute-start.30 = (f32[178,128]{1,0:T(8,128)}, f32[178,128]{1,0:T(8,128)}, u32[]{:S(2)}, u32[]{:S(2)}) collective-permute-start(f32[178,128]{1,0:T(8,128)} %add.278), channel_id=1, source_target_pairs={{0,24},{4,28},{8,16},{12,20},{16,8},{20,12},{24,0},{28,4},{1,25},{... | collective-permute-start | bytes 273416 | tf_op jit(solution)/shard_map/ppermute | solution.py:644
  466.6 7.9 %collective-permute-start.29 = (f32[178,128]{1,0:T(8,128)}, f32[178,128]{1,0:T(8,128)}, u32[]{:S(2)}, u32[]{:S(2)}) collective-permute-start(f32[178,128]{1,0:T(8,128)} %add.278), channel_id=1, source_target_pairs={{0,16},{4,20},{8,24},{12,28},{16,0},{20,4},{24,8},{28,12},{1,17},{... | collective-permute-start | bytes 273416 | tf_op jit(solution)/shard_map/ppermute | solution.py:644
  470.4 9.0 %collective-permute-start.25 = (bf16[24,3456]{1,0:T(8,128)(2,1)S(1)}, bf16[24,3456]{1,0:T(8,128)(2,1)S(1)}, u32[]{:S(2)}, u32[]{:S(2)}) collective-permute-start(bf16[24,3456]{1,0:T(8,128)(2,1)S(1)} %get-tuple-element.333), channel_id=1, source_target_pairs={{0,1},{1,2},{2,3},{3,0},{4,5},{5,6},{6,7},{7,4},{8,9},{9,10},{10,1... | collective-permute-start | bytes 497672 | tf_op jit(solution)/shard_map/ppermute | solution.py:611
  470.5 9.0 %collective-permute-start.27 = (bf16[24,3456]{1,0:T(8,128)(2,1)S(1)}, bf16[24,3456]{1,0:T(8,128)(2,1)S(1)}, u32[]{:S(2)}, u32[]{:S(2)}) collective-permute-start(bf16[24,3456]{1,0:T(8,128)(2,1)S(1)} %get-tuple-element.334), channel_id=1, source_target_pairs={{0,3},{1,0},{2,1},{3,2},{4,7},{5,4},{6,5},{7,6},{8,11},{9,8},{10,9... | collective-permute-start | bytes 497672 | tf_op jit(solution)/shard_map/ppermute | solution.py:611
  474.4 12.1 %collective-permute-start.26 = (bf16[24,3456]{1,0:T(8,128)(2,1)S(1)}, bf16[24,3456]{1,0:T(8,128)(2,1)S(1)}, u32[]{:S(2)}, u32[]{:S(2)}) collective-permute-start(bf16[24,3456]{1,0:T(8,128)(2,1)S(1)} %get-tuple-element.335), channel_id=1, source_target_pairs={{0,2},{1,3},{2,0},{3,1},{4,6},{5,7},{6,4},{7,5},{8,10},{9,11},{10,... | collective-permute-start | bytes 497672 | tf_op jit(solution)/shard_map/ppermute | solution.py:611
  487.3 8.3 %collective-permute-start.32 = (f32[178,128]{1,0:T(8,128)S(1)}, f32[178,128]{1,0:T(8,128)}, u32[]{:S(2)}, u32[]{:S(2)}) collective-permute-start(f32[178,128]{1,0:T(8,128)S(1)} %add_add_fusion.1), channel_id=1, source_target_pairs={{0,2},{1,3},{2,0},{3,1},{4,6},{5,7},{6,4},{7,5},{8,10},{9,11},{10,... | collective-permute-start | bytes 273416 | tf_op jit(solution)/shard_map/ppermute | solution.py:611
  487.3 8.3 %collective-permute-start.31 = (f32[178,128]{1,0:T(8,128)S(1)}, f32[178,128]{1,0:T(8,128)}, u32[]{:S(2)}, u32[]{:S(2)}) collective-permute-start(f32[178,128]{1,0:T(8,128)S(1)} %add_add_fusion.1), channel_id=1, source_target_pairs={{0,1},{1,2},{2,3},{3,0},{4,5},{5,6},{6,7},{7,4},{8,9},{9,10},{10,1... | collective-permute-start | bytes 273416 | tf_op jit(solution)/shard_map/ppermute | solution.py:611
  (95 other events, 913.4 us)
Sparse Core Ops, SparseCore 0:
  11.5 98.7 all-gather.1

commit v4 on v3

--- a/solution.py
+++ b/solution.py
@@ -553,7 +553,7 @@
     )(ends, xr, xr, ys, st, par, gain, hw, spread, gather, *grads, *held, *carried)
 
 
-def norm_back_kernel(dz_ref, dxr_ref, wz_ref, wx_ref, h_ref, flow_ref, gain_ref, out_ref, dgain_ref):
+def norm_back_kernel(dz_ref, dxr_ref, wz_ref, wx_ref, h_ref, flow_ref, gain_ref, out_ref, dgain_ref, *low_ref):
     @pl.when(pl.program_id(0) == 0)
     def _():
         dgain_ref[...] = jnp.zeros_like(dgain_ref)
@@ -563,19 +563,31 @@
     scale = lax.rsqrt(jnp.sum(h * h, axis=1, keepdims=True) / D + EPSILON)
     scaled = dxn * gain_ref[0:1, :]
     pull = jnp.sum(scaled * h, axis=1, keepdims=True) * (scale * scale * scale) / D
-    out_ref[...] = flow_ref[...] + (scale * scaled - h * pull)
+    total = flow_ref[...] + (scale * scaled - h * pull)
+    out_ref[...] = total
+    if low_ref:
+        low_ref[0][...] = total.astype(BF16)
     dgain_ref[...] += partial8(dxn * (h * scale))
 
 
-def norm_backward(dz, dxr, wz, wx, h, flowing, gain):
+def norm_backward(dz, dxr, wz, wx, z_at, low, h, flowing, gain):
     tokens = dz.shape[0]
     rows = lambda width: pl.BlockSpec((NORM_BLOCK, width), lambda i: (i, 0))
     return pl.pallas_call(
         norm_back_kernel,
         grid=(tokens // NORM_BLOCK,),
-        in_specs=[rows(INNER), rows(XR), whole((D, INNER)), whole((D, XR)), rows(D), rows(D), whole((8, D))],
-        out_specs=[rows(D), whole((8, D))],
-        out_shape=[jax.ShapeDtypeStruct((tokens, D), F32), jax.ShapeDtypeStruct((8, D), F32)],
+        in_specs=[
+            rows(INNER),
+            rows(XR),
+            pl.BlockSpec((D, INNER), lambda i: (0, z_at)),
+            whole((D, XR)),
+            rows(D),
+            rows(D),
+            whole((8, D)),
+        ],
+        out_specs=[rows(D), whole((8, D))] + [rows(D)] * low,
+        out_shape=[jax.ShapeDtypeStruct((tokens, D), F32), jax.ShapeDtypeStruct((8, D), F32)]
+        + [jax.ShapeDtypeStruct((tokens, D), BF16)] * low,
         compiler_params=pltpu.CompilerParams(vmem_limit_bytes=VMEM_LIMIT),
         cost_estimate=pl.CostEstimate(flops=1_000_000, bytes_accessed=1_000_000, transcendentals=0),
         name="norm_backward",
@@ -653,13 +665,13 @@
         got = lax.all_to_all(value, "dp", 0, 0, axis_index_groups=groups)
         return jnp.sum(got.astype(F32), axis=0)
 
+    def z_sends(self, value, wire=F32):
+        count, at = self.sizes["z"], lax.axis_index("fsdp")
+        parts = [lax.dynamic_index_in_dim(value, (at + d) % count, 0, keepdims=False) for d in range(count)]
+        return parts[:1] + [self.shift(parts[d].astype(wire), "z", d) for d in range(1, count)]
+
     def z_sum(self, value, wire=F32):
-        count, at = self.sizes["z"], lax.axis_index("fsdp")
-        total = lax.dynamic_index_in_dim(value, at, 0, keepdims=False)
-        for d in range(1, count):
-            part = lax.dynamic_index_in_dim(value, (at + d) % count, 0, keepdims=False)
-            total = total + self.shift(part.astype(wire), "z", d).astype(F32)
-        return total
+        return sum(v.astype(F32) for v in self.z_sends(value, wire))
 
     def core_send(self, value, at):
         return self.shift(lax.dynamic_index_in_dim(value, 1 - at["core"], 2), "core", 1)
@@ -729,25 +741,19 @@
     vec_low = jnp.pad(vec_low, (0, shard_rows * LANES - vec_low.shape[0])).reshape(shard_rows, LANES)
     first = net.gather(jnp.concatenate([in_low[0, :, INNER:], vec_low], axis=1), ("z", "x", "y", "core"))
     first_z = net.gather(in_low[0, :, :INNER], ("z", "y", "x", "core"))
-    rest = lax.all_gather(
-        jnp.concatenate([out_low[0, 0], out_low[0, 1], in_low[1], out_low[1, 0], out_low[1, 1]], axis=1),
-        AXES,
-        axis=0,
-        tiled=True,
-    )
+    gap = jnp.zeros((shard_rows, 2 * INNER - XR - D), BF16)
+    rest = [in_low[1, :, INNER:], out_low[0, 0], gap, in_low[1, :, :INNER], out_low[0, 1], out_low[1, 0], out_low[1, 1]]
+    rest = lax.all_gather(jnp.concatenate(rest, axis=1), AXES, axis=0, tiled=True)
     devices = rest.shape[0] // shard_rows
 
-    def out_rows(columns):
-        columns = columns.reshape(devices, 1, shard_rows, 2 * D)
-        return jnp.concatenate([columns[..., :D], columns[..., D:]], axis=1).reshape(INNER, D)
-
-    in_from = 2 * D
-    out_from = in_from + INNER + XR
-    ins = [
-        (first_z, first[:, :XR]),
-        (rest[:, in_from : in_from + INNER], rest[:, in_from + INNER : out_from]),
-    ]
-    outs = [out_rows(rest[:, :in_from]), out_rows(rest[:, out_from:])]
+    def out_rows(*starts):
+        halves_of = [rest[:, k : k + D].reshape(devices, 1, shard_rows, D) for k in starts]
+        return jnp.concatenate(halves_of, axis=1).reshape(INNER, D)
+
+    after = 3 * INNER
+    ins = [(first_z, first[:, :XR]), (rest[:, 2 * INNER : after], rest[:, :XR])]
+    read_from = [(first_z, first, 0), (rest, rest, 2)]
+    outs = [out_rows(XR, after), out_rows(after + D, after + 2 * D)]
     vector_full = first[:, XR:].reshape(devices, -1)[:, : LAYERS * VEC // devices]
     vector_full = vector_full.reshape(devices, LAYERS, -1).swapaxes(0, 1).reshape(LAYERS, VEC).astype(F32)
     stream = hidden_in.astype(F32)
@@ -766,8 +772,8 @@
     at = net.coordinates()
     flowing = cotangent.astype(F32) * valid[:, None]
     small_parts = [None] * LAYERS
-    arrived = [None] * LAYERS
     in_sums = []
+    low = []
 
     def product(a, b):
         return jnp.einsum("td,tp->dp", a, b, preferred_element_type=F32)
@@ -775,7 +781,7 @@
     for l in reversed(range(LAYERS)):
         normed_from, normed, z, xr, gn, ys, st, tables = stored[l]
         wire = BF16 if l == 0 else F32
-        gb = flowing.astype(BF16)
+        gb = low[0] if low else flowing.astype(BF16)
         grad_out = product(gn, gb)
         gb, grad_out = fence((gb, grad_out))
         got = net.core_send(net.blocks(grad_out), at)
@@ -783,12 +789,12 @@
         dgn, grad_out, got = fence((dgn, grad_out, got))
         out_sum = side_by_side(net.core_sum(net.blocks(grad_out), got, at))
         waiting = jnp.concatenate(in_sums + [out_sum], axis=-1).astype(wire)
-        dgn, waiting, arrived = fence((dgn, waiting, arrived))
+        dgn, waiting = fence((dgn, waiting))
         waiting = net.xy_sum(waiting, wire)
         back = mixer_backward(ends, xr, ys, st, *tables, spread, gather, (z, dgn), 0, blocks)
         back, waiting = fence((back, waiting))
         if l > 0:
-            arrived[l] = net.z_sum(waiting, wire)
+            out_one = waiting
         dxr, dz = back[0], back[6]
         grads = [product(normed, dxr), product(normed, dz)]
         dz, dxr, grads = fence((dz, dxr, grads))
@@ -797,11 +803,14 @@
             grads, got, in_late, out_late, vector_late = fence((grads, got, in_weight, out_weight, vector_weight))
             in_sums = [net.core_sum(net.blocks(g), v, at) for g, v in zip(grads, got)]
             in_zero = jnp.concatenate(in_sums, axis=-1).astype(BF16)
+            waiting = jnp.concatenate([waiting, out_one], axis=-1).astype(BF16)
             dz, dxr, in_zero, waiting = fence((dz, dxr, in_zero, waiting))
             in_zero = net.xy_sum(in_zero, BF16)
-            arrived[0] = net.z_sum(waiting, wire)
+            arrived = net.z_sends(waiting, BF16)
+            dz, dxr, arrived[1] = fence((dz, dxr, arrived[1]))
+            arrived = sum(v.astype(F32) for v in arrived)
         gain = jnp.broadcast_to(vector_full[l, None, :D], (8, D))
-        flowing, dnorm = norm_backward(dz, dxr, *ins[l], normed_from, flowing, gain)
+        flowing, dnorm, *low = norm_backward(dz, dxr, *read_from[l], l > 0, normed_from, flowing, gain)
         if l > 0:
             flowing, grads, got = fence((flowing, grads, got))
             in_sums = [net.core_sum(net.blocks(g), v, at) for g, v in zip(grads, got)]
@@ -824,9 +833,15 @@
     mine = lax.axis_index("dp") * lax.axis_size("fsdp") + lax.axis_index("fsdp")
     grad_vector = lax.dynamic_slice(small, (0, mine * share), (LAYERS, share))
     grad_in = jnp.stack(
-        [jnp.concatenate([v[:, XR : XR + INNER], v[:, : P_SIZE - INNER]], axis=1) for v in (in_zero, arrived[0])]
+        [jnp.concatenate([v[:, XR : XR + INNER], v[:, : P_SIZE - INNER]], axis=1) for v in (in_zero, arrived)]
     )
-    grad_out = jnp.stack([jnp.concatenate([v[:, -2 * D : -D], v[:, -D:]], axis=0) for v in arrived])
+    out_from = XR + INNER
+    grad_out = jnp.stack(
+        [
+            jnp.concatenate([arrived[:, k : k + D], arrived[:, k + D : k + 2 * D]], axis=0)
+            for k in (out_from, out_from + 2 * D)
+        ]
+    )
     squares_in = grad_in * grad_in
     squares_out = grad_out * grad_out
     row_in = MOMENT_DECAY * in_row_moment + (1.0 - MOMENT_DECAY) * jnp.mean(squares_in, axis=2)

time: 536 us -> 492 us (0.918)
  waiting for transfers between devices: 87 us -> 68.2 us
  local copies, waits for them, and re-layouts: 55.3 us -> 37.8 us
  other arithmetic: 58.7 us -> 48.7 us
  matrix products: 63.7 us -> 73 us
    ppermute x21 -> x18, waiting for transfers between devices: 56.3 us -> 28 us  [shift(): return lax.ppermute(value, 'fsdp', [(i, (i + by) % n) for i in range(n)])]
    slice x6 -> x2, local copies, waits for them, and re-layouts: 12.5 us -> 3.84 us  [the longest x1 3.82 us: out_rows(): rest[:, k:k + D].reshape(devices, 1, shard_rows, D)]
    dot_general x6, matrix products: 22.5 us -> 29.7 us  [product(): return jnp.einsum('td,tp->dp', a, b, preferred_element_type=F32)]
    all_to_all x3, waiting for transfers between devices: 3.85 us -> 9.85 us  [xy_sum(): got = lax.all_to_all(value, 'dp', 0, 0, axis_index_groups=groups)]
    unnamed x168 -> x152, local copies, waits for them, and re-layouts: 20 us -> 14.8 us
    another operation x7 -> x6, other arithmetic: 11.3 us -> 6.92 us
    ppermute x21 -> x18, starting transfers between devices: 28.6 us -> 26.1 us  [shift(): return lax.ppermute(value, 'fsdp', [(i, (i + by) % n) for i in range(n)])]
  transfers between devices with their start and end apart: 45 -> 42, of which waited for: 21 -> 16; matrix products, arithmetic and copies ran while one was open for 16% -> 14% of each run, Pallas kernels for 28% -> 30%
where the time goes in v4:
time: 492 us; the launch traced here: 487 us
  Pallas kernels  188 us (38%)
  matrix products  73 us (15%)
  waiting for transfers between devices  68.2 us (14%)
  starting transfers between devices  53.4 us (11%)
  other arithmetic  48.7 us (10%)
  local copies, waits for them, and re-layouts  37.8 us (8%)
  between operations  18.3 us (4%)
    pallas_call x2, Pallas kernels, mixer_backward(): pl.pallas_call(kernel, grid=(last - first,), in_specs=in_specs, out_specs...  106 us
    pallas_call x2, Pallas kernels, mixer_forward(): pl.pallas_call(partial(forward_kernel, z is not None), grid=(blocks,), in...  57.2 us
    dot_general x6, matrix products, product(): return jnp.einsum('td,tp->dp', a, b, preferred_element_type=F32)  29.7 us
    ppermute x18, waiting for transfers between devices, shift(): return lax.ppermute(value, 'fsdp', [(i, (i + by) % n) for i in range(n)])  28 us
    ppermute x14, waiting for transfers between devices, shift(): return lax.ppermute(value, 'dp', pairs)  26.5 us
    ppermute x18, starting transfers between devices, shift(): return lax.ppermute(value, 'fsdp', [(i, (i + by) % n) for i in range(n)])  26.1 us
    pallas_call x2, Pallas kernels, norm_backward(): pl.pallas_call(norm_back_kernel, grid=(tokens // NORM_BLOCK,), in_specs=[...  25.1 us
    unnamed x152, local copies, waits for them, and re-layouts  14.8 us
  transfers between devices with their start and end apart: 42, of which 16 were waited for; matrix products, arithmetic and copies ran while one was open for 14% of the time, Pallas kernels for 30%

profile of v4, /device:TPU:0, one launch (start us, length us, event | category | flops | bytes accessed | tf_op | source)
XLA Modules:
  0.0 487.2 jit_solution(18340453888237490054)
XLA Ops:
  28.4 4.0 collective-permute-done.1
  32.4 3.5 collective-permute-done
  39.1 11.4 %collective-permute-done.3 = bf16[1,1,1,4,24,2048]{5,4,3,2,1,0:T(8,128)(2,1)S(1)} collective-permute-done((bf16[1,1,1,4,24,2048]{5,4,3,2,1,0:T(8,128)(2,1)S(1)}, bf16[1,1,1,4,24,2048]{5,4,3,2,1,0:T(8,128)(2,1)S(1)}, u32[]{:S(2)}, u32[]{:S(2)}) %collective-permute-start.3) | collective-permute-done | bytes 393248 | tf_op jit(solution)/shard_map/ppermute | solution.py:629
  56.3 11.6 %collective-permute-done.10 = bf16[2,1,1,4,24,1536]{5,4,3,2,1,0:T(8,128)(2,1)S(1)} collective-permute-done((bf16[2,1,1,4,24,1536]{5,4,3,2,1,0:T(8,128)(2,1)}, bf16[2,1,1,4,24,1536]{5,4,3,2,1,0:T(8,128)(2,1)S(1)}, u32[]{:S(2)}, u32[]{:S(2)}) %collective-permute-start.10) | collective-permute-done | bytes 589856 | tf_op jit(solution)/shard_map/ppermute | solution.py:629
  80.8 6.6 %fusion.50.refs_0_.refs_10_ = f32[1024,1536]{1,0:T(8,128)} fusion(bf16[768,1536]{1,0:T(8,128)(2,1)} %bitcast.184, bf16[1024,768]{1,0:T(8,128)(2,1)S(1)} %copy-done, f32[768]{0:T(1024)S(1)} %get-tuple-element.288, f32[1024]{0:T(1024)S(1)} %add_rsqrt_fusion.1), kind=kOutput, calls=%fused_computation.204 | convolution fusion | flops 2419064832 | bytes 10230784 | tf_op jit(solution)/shard_map/dot_general | solution.py:765
  87.5 5.7 %fusion.5.xr_ref.refs_1_.refs_2_ = f32[1024,1920]{1,0:T(8,128)} fusion(bf16[768,2048]{1,0:T(8,128)(2,1)S(1)} %bitcast.183, bf16[1024,768]{1,0:T(8,128)(2,1)S(1)} %copy-done, f32[768]{0:T(1024)S(1)} %get-tuple-element.288, f32[1024]{0:T(1024)S(1)} %add_rsqrt_fusion.1), kind=kOutput, calls=%fused_computation.16 | convolution fusion | flops 3023044608 | bytes 12394496 | tf_op jit(solution)/shard_map/dot_general | solution.py:766
  93.2 28.4 %mixer_forward.2 = (bf16[1024,1536]{1,0:T(8,128)(2,1)}, f32[1024,1536]{1,0:T(8,128)}, f32[8,128,1536]{2,1,0:T(8,128)}) custom-call(s32[4]{0:T(128)} %pad_add_fusion.ends_ref.refs_0_, f32[1024,1920]{1,0:T(8,128)} %fusion.5.xr_ref.refs_1_.refs_2_, f32[8,1792]{1,0:T(8,128)} %concatenate.111.par_ref.refs_5_, f32[8,1536]{1,0:T(8,128)} %get-tuple-element.377.gain_ref.refs_6_, ...), custom_call_target="tpu_custom_call" | custom-call | flops 30000001024 | bytes 30000000 | tf_op jit(solution)/shard_map/mixer_forward/pallas_call | solution.py:476
  121.6 3.8 fusion.62
  131.5 4.5 fusion.7.refs_0_.refs_10_
  136.0 5.5 %fusion.3.xr_ref.refs_1_.refs_2_ = f32[1024,1920]{1,0:T(8,128)} fusion(bf16[1024,768]{1,0:T(8,128)(2,1)S(1)} %multiply_convert_fusion, bf16[768,6912]{1,0:T(8,128)(2,1)S(1)} %bitcast.173), kind=kOutput, calls=%fused_computation.14 | convolution fusion | flops 3019898880 | bytes 12386304 | tf_op jit(solution)/shard_map/dot_general | solution.py:766
  141.5 28.8 %mixer_forward.3 = (bf16[1024,1536]{1,0:T(8,128)(2,1)}, f32[1024,1536]{1,0:T(8,128)}, f32[8,128,1536]{2,1,0:T(8,128)}) custom-call(s32[4]{0:T(128)} %pad_add_fusion.ends_ref.refs_0_, f32[1024,1920]{1,0:T(8,128)} %fusion.3.xr_ref.refs_1_.refs_2_, f32[8,1792]{1,0:T(8,128)} %concatenate.119.par_ref.refs_5_, f32[8,1536]{1,0:T(8,128)} %get-tuple-element.376.gain_ref.refs_6_, ...), custom_call_target="tpu_custom_call" | custom-call | flops 30000001024 | bytes 30000000 | tf_op jit(solution)/shard_map/mixer_forward/pallas_call | solution.py:476
  170.3 4.6 fusion.68
  178.1 6.9 %fusion.69.refs_11_ = f32[1024,1536]{1,0:T(8,128)} fusion(bf16[1024,768]{1,0:T(8,128)(2,1)} %get-tuple-element.115, bf16[1536,768]{1,0:T(8,128)(2,1)S(1)} %bitcast.199), kind=kOutput, calls=%fused_computation.218 | convolution fusion | flops 2415919104 | bytes 10223616 | tf_op jit(solution)/shard_map/td,ed->te/dot_general | solution.py:788
  188.9 4.0 all-to-all-start
  194.6 52.8 %mixer_backward.2 = (bf16[1024,1920]{1,0:T(8,128)(2,1)}, f32[40,1792]{1,0:T(8,128)}, f32[8,1536]{1,0:T(8,128)}, f32[16,128]{1,0:T(8,128)}, f32[128,1536]{1,0:T(8...) custom-call(s32[4]{0:T(128)} %pad_add_fusion.ends_ref.refs_0_, ...), custom_call_target="tpu_custom_call" | custom-call | flops 56000000000 | bytes 40000000 | tf_op jit(solution)/shard_map/mixer_backward/pallas_call | solution.py:540
  248.3 7.3 %fusion.71 = f32[768,1536]{1,0:T(8,128)} fusion(bf16[1024,768]{1,0:T(8,128)(2,1)} %copy-done.10, bf16[1024,1536]{1,0:T(8,128)(2,1)} %get-tuple-element.130.dz_ref), kind=kOutput, calls=%fused_computation.220 | convolution fusion | flops 2415919104 | bytes 9437184 | tf_op jit(solution)/shard_map/td,tp->dp/dot_general | solution.py:779
  255.6 5.3 %fusion.70 = f32[768,1920]{1,0:T(8,128)} fusion(bf16[1024,768]{1,0:T(8,128)(2,1)S(1)} %copy-done.11, bf16[1024,1920]{1,0:T(8,128)(2,1)S(1)} %copy-done.18), kind=kOutput, calls=%fused_computation.219 | convolution fusion | flops 3019898880 | bytes 11403264 | tf_op jit(solution)/shard_map/td,tp->dp/dot_general | solution.py:779
  261.5 13.0 %norm_backward.2 = (f32[1024,768]{1,0:T(8,128)}, f32[8,768]{1,0:T(8,128)}, bf16[1024,768]{1,0:T(8,128)(2,1)}) custom-call(bf16[1024,1536]{1,0:T(8,128)(2,1)} %get-tuple-element.130.dz_ref, bf16[1024,1920]{1,0:T(8,128)(2,1)} %get-tuple-element.131.dxr_ref, bf16[768,6912]{1,0:T(8,128)(2,1)} %all-gather.2.cloned.1.call-done.wz_ref.wx_ref, ...), custom_call_target="tpu_custom_call" | custom-call | flops 1000000 | bytes 1000000 | tf_op jit(solution)/shard_map/norm_backward/pallas_call | solution.py:576
  274.5 4.2 fusion.72
  283.9 4.6 fusion.73.refs_11_
  293.8 4.8 all-to-all-start.1
  298.6 52.8 %mixer_backward.3 = (bf16[1024,1920]{1,0:T(8,128)(2,1)}, f32[40,1792]{1,0:T(8,128)}, f32[8,1536]{1,0:T(8,128)}, f32[16,128]{1,0:T(8,128)}, f32[128,1536]{1,0:T(8...) custom-call(s32[4]{0:T(128)} %pad_add_fusion.ends_ref.refs_0_, ...), custom_call_target="tpu_custom_call" | custom-call | flops 56000000000 | bytes 40000000 | tf_op jit(solution)/shard_map/mixer_backward/pallas_call | solution.py:540
  355.0 4.7 fusion.46
  359.7 3.6 fusion.48
  371.1 6.5 %add_convert_fusion = bf16[1024,768]{1,0:T(8,128)(2,1)} fusion(f32[1024,768]{1,0:T(8,128)S(1)} %copy-done.8, bf16[1024,1536]{1,0:T(8,128)(2,1)} %get-tuple-element.114, bf16[1536,768]{1,0:T(8,128)(2,1)} %bitcast.200), kind=kOutput, calls=%fused_computation.10 | convolution fusion | flops 2417491968 | bytes 10223616 | tf_op jit(solution)/shard_map/dot_general | solution.py:768
  390.8 4.2 all-to-all-start.2
  400.6 12.1 %norm_backward.3 = (f32[1024,768]{1,0:T(8,128)}, f32[8,768]{1,0:T(8,128)}) custom-call(bf16[1024,1536]{1,0:T(8,128)(2,1)} %get-tuple-element.168.dz_ref, bf16[1024,1920]{1,0:T(8,128)(2,1)} %get-tuple-element.169.dxr_ref, bf16[768,1536]{1,0:T(8,128)(2,1)} %bitcast.185, bf16[768,2048]{1,0:T(8,128)(2,1)} %bitcast.182, bf16[1024,768]{1,0:T(8,128)(2,1)} %h_ref.1, ...), custom_call_target="tpu_custom_call" | custom-call | flops 1000000 | bytes 1000000 | tf_op jit(solution)/shard_map/norm_backward/pallas_call | solution.py:576
  416.1 9.8 %all-to-all-done.2 = bf16[4,4,24,3456]{3,2,1,0:T(8,128)(2,1)S(1)} async-done(((bf16[4,4,24,3456]{3,2,1,0:T(8,128)(2,1)}), bf16[4,4,24,3456]{3,2,1,0:T(8,128)(2,1)S(1)}, u32[]{:S(2)}, u32[]{:S(2)}) %all-to-all-start.2) | async-done | bytes 2654240 | tf_op jit(solution)/shard_map/all_to_all | solution.py:665
  432.0 3.5 collective-permute-start.24
  436.8 4.0 collective-permute-done.22
  440.8 6.3 %collective-permute-done.23 = bf16[24,3456]{1,0:T(8,128)(2,1)S(1)} collective-permute-done((bf16[24,3456]{1,0:T(8,128)(2,1)S(1)}, bf16[24,3456]{1,0:T(8,128)(2,1)S(1)}, u32[]{:S(2)}, u32[]{:S(2)}) %collective-permute-start.23) | collective-permute-done | bytes 165920 | tf_op jit(solution)/shard_map/ppermute | solution.py:623
  452.1 4.5 collective-permute-done.29
  (395 shorter events, 135.3 us)
Async XLA Ops:
  7.2 114.4 %all-gather.2.cloned.1.call-start = ((), (), s32[]{:S(2)}) async-start(), calls=%async_computation.3 | async-start | bytes 10948608 | tf_op jit(solution)/shard_map/all_gather | solution.py:746
  10.4 13.5 %collective-permute-start.8 = (bf16[1,1,1,1,24,1536]{5,4,3,2,1,0:T(8,128)(2,1)S(1)}, bf16[1,1,1,1,24,1536]{5,4,3,2,1,0:T(8,128)(2,1)S(1)}, u32[]{:S(2)}, u32[]{:S(2)}) collective-permute-start(bf16[1,1,1,1,24,1536]{5,4,3,2,1,0:T(8,128)(2,1)S(1)} %slice_bitcast_fusion.1), channel_id=1, source_target_pairs={{0,1},{1,2},{2,3},{3,0},{4,5},{5,6},{6,7},{7,4},{8,9},{9,10},{10,1... | collective-permute-start | bytes 221192 | tf_op jit(solution)/shard_map/ppermute | solution.py:623
  13.5 13.3 %collective-permute-start.7 = (bf16[1,1,1,1,24,1536]{5,4,3,2,1,0:T(8,128)(2,1)S(1)}, bf16[1,1,1,1,24,1536]{5,4,3,2,1,0:T(8,128)(2,1)S(1)}, u32[]{:S(2)}, u32[]{:S(2)}) collective-permute-start(bf16[1,1,1,1,24,1536]{5,4,3,2,1,0:T(8,128)(2,1)S(1)} %slice_bitcast_fusion.1), channel_id=1, source_target_pairs={{0,2},{1,3},{2,0},{3,1},{4,6},{5,7},{6,4},{7,5},{8,10},{9,11},{10,... | collective-permute-start | bytes 221192 | tf_op jit(solution)/shard_map/ppermute | solution.py:623
  16.0 10.7 %collective-permute-start.6 = (bf16[1,1,1,1,24,1536]{5,4,3,2,1,0:T(8,128)(2,1)S(1)}, bf16[1,1,1,1,24,1536]{5,4,3,2,1,0:T(8,128)(2,1)S(1)}, u32[]{:S(2)}, u32[]{:S(2)}) collective-permute-start(bf16[1,1,1,1,24,1536]{5,4,3,2,1,0:T(8,128)(2,1)S(1)} %slice_bitcast_fusion.1), channel_id=1, source_target_pairs={{0,3},{1,0},{2,1},{3,2},{4,7},{5,4},{6,5},{7,6},{8,11},{9,8},{10,9... | collective-permute-start | bytes 221192 | tf_op jit(solution)/shard_map/ppermute | solution.py:623
  17.5 10.9 %collective-permute-start.2 = (bf16[1,1,1,1,24,2048]{5,4,3,2,1,0:T(8,128)(2,1)S(1)}, bf16[1,1,1,1,24,2048]{5,4,3,2,1,0:T(8,128)(2,1)S(1)}, u32[]{:S(2)}, u32[]{:S(2)}) collective-permute-start(bf16[1,1,1,1,24,2048]{5,4,3,2,1,0:T(8,128)(2,1)S(1)} %maximum_bitcast_fusion.4), channel_id=1, source_target_pairs={{0,1},{1,2},{2,3},{3,0},{4,5},{5,6},{6,7},{7,4},{8,9},{9,10},{10,1... | collective-permute-start | bytes 294920 | tf_op jit(solution)/shard_map/ppermute | solution.py:623
  18.3 14.1 %collective-permute-start.1 = (bf16[1,1,1,1,24,2048]{5,4,3,2,1,0:T(8,128)(2,1)S(1)}, bf16[1,1,1,1,24,2048]{5,4,3,2,1,0:T(8,128)(2,1)S(1)}, u32[]{:S(2)}, u32[]{:S(2)}) collective-permute-start(bf16[1,1,1,1,24,2048]{5,4,3,2,1,0:T(8,128)(2,1)S(1)} %maximum_bitcast_fusion.4), channel_id=1, source_target_pairs={{0,2},{1,3},{2,0},{3,1},{4,6},{5,7},{6,4},{7,5},{8,10},{9,11},{10,... | collective-permute-start | bytes 294920 | tf_op jit(solution)/shard_map/ppermute | solution.py:623
  23.9 12.0 %collective-permute-start = (bf16[1,1,1,1,24,2048]{5,4,3,2,1,0:T(8,128)(2,1)S(1)}, bf16[1,1,1,1,24,2048]{5,4,3,2,1,0:T(8,128)(2,1)S(1)}, u32[]{:S(2)}, u32[]{:S(2)}) collective-permute-start(bf16[1,1,1,1,24,2048]{5,4,3,2,1,0:T(8,128)(2,1)S(1)} %maximum_bitcast_fusion.4), channel_id=1, source_target_pairs={{0,3},{1,0},{2,1},{3,2},{4,7},{5,4},{6,5},{7,6},{8,11},{9,8},{10,9... | collective-permute-start | bytes 294920 | tf_op jit(solution)/shard_map/ppermute | solution.py:623
  26.8 10.7 %collective-permute-start.9 = (bf16[1,1,1,4,24,1536]{5,4,3,2,1,0:T(8,128)(2,1)S(1)}, bf16[1,1,1,4,24,1536]{5,4,3,2,1,0:T(8,128)(2,1)S(1)}, u32[]{:S(2)}, u32[]{:S(2)}) collective-permute-start(bf16[1,1,1,4,24,1536]{5,4,3,2,1,0:T(8,128)(2,1)S(1)} %pad_maximum_fusion.14), channel_id=1, source_target_pairs={{0,16},{4,20},{8,24},{12,28},{16,0},{20,4},{24,8},{28,12},{1,17},{... | collective-permute-start | bytes 884744 | tf_op jit(solution)/shard_map/ppermute | solution.py:629
  36.1 14.4 %collective-permute-start.3 = (bf16[1,1,1,4,24,2048]{5,4,3,2,1,0:T(8,128)(2,1)S(1)}, bf16[1,1,1,4,24,2048]{5,4,3,2,1,0:T(8,128)(2,1)S(1)}, u32[]{:S(2)}, u32[]{:S(2)}) collective-permute-start(bf16[1,1,1,4,24,2048]{5,4,3,2,1,0:T(8,128)(2,1)S(1)} %pad_maximum_fusion.13), channel_id=1, source_target_pairs={{0,8},{4,12},{8,0},{12,4},{16,24},{20,28},{24,16},{28,20},{1,9},{5... | collective-permute-start | bytes 1179656 | tf_op jit(solution)/shard_map/ppermute | solution.py:629
  38.5 29.4 %collective-permute-start.10 = (bf16[2,1,1,4,24,1536]{5,4,3,2,1,0:T(8,128)(2,1)}, bf16[2,1,1,4,24,1536]{5,4,3,2,1,0:T(8,128)(2,1)S(1)}, u32[]{:S(2)}, u32[]{:S(2)}) collective-permute-start(bf16[2,1,1,4,24,1536]{5,4,3,2,1,0:T(8,128)(2,1)} %pad_maximum_fusion.12), channel_id=1, source_target_pairs={{0,8},{4,12},{8,0},{12,4},{16,24},{20,28},{24,16},{28,20},{1,9},{5... | collective-permute-start | bytes 1769480 | tf_op jit(solution)/shard_map/ppermute | solution.py:629
  51.5 16.7 %collective-permute-start.4 = (bf16[1,2,1,4,24,2048]{5,4,3,2,1,0:T(8,128)(2,1)}, bf16[1,2,1,4,24,2048]{5,4,3,2,1,0:T(8,128)(2,1)}, u32[]{:S(2)}, u32[]{:S(2)}) collective-permute-start(bf16[1,2,1,4,24,2048]{5,4,3,2,1,0:T(8,128)(2,1)} %pad_maximum_fusion.10), channel_id=1, source_target_pairs={{0,16},{4,20},{8,24},{12,28},{16,0},{20,4},{24,8},{28,12},{1,17},{... | collective-permute-start | bytes 2359304 | tf_op jit(solution)/shard_map/ppermute | solution.py:629
  177.8 7.2 %collective-permute-start.12 = (f32[2,2,1,4,48,768]{5,4,3,2,1,0:T(8,128)}, f32[2,2,1,4,48,768]{5,4,3,2,1,0:T(8,128)}, u32[]{:S(2)}, u32[]{:S(2)}) collective-permute-start(f32[2,2,1,4,48,768]{5,4,3,2,1,0:T(8,128)} %constant_dynamic-slice_fusion.6), channel_id=1, source_target_pairs={{0,4},{4,0},{8,12},{12,8},{16,20},{20,16},{24,28},{28,24},{1,5},{5... | collective-permute-start | bytes 7077896 | tf_op jit(solution)/shard_map/ppermute | solution.py:629
  188.9 58.5 %all-to-all-start = ((f32[4,4,24,1536]{3,2,1,0:T(8,128)}), f32[4,4,24,1536]{3,2,1,0:T(8,128)S(1)}, u32[]{:S(2)}, u32[]{:S(2)}) async-start(f32[4,4,24,1536]{3,2,1,0:T(8,128)} %bitcast.186), calls=%async_computation | async-start | bytes 4718592 | tf_op jit(solution)/shard_map/all_to_all | solution.py:665
  278.9 12.3 %collective-permute-start.14 = (f32[2,2,1,4,24,1920]{5,4,3,2,1,0:T(8,128)S(1)}, f32[2,2,1,4,24,1920]{5,4,3,2,1,0:T(8,128)S(1)}, u32[]{:S(2)}, u32[]{:S(2)}) collective-permute-start(f32[2,2,1,4,24,1920]{5,4,3,2,1,0:T(8,128)S(1)} %constant_dynamic-slice_fusion.4), channel_id=1, source_target_pairs={{0,4},{4,0},{8,12},{12,8},{16,20},{20,16},{24,28},{28,24},{1,5},{5... | collective-permute-start | bytes 8847368 | tf_op jit(solution)/shard_map/ppermute | solution.py:629
  279.7 8.8 %collective-permute-start.13 = (f32[2,2,1,4,48,768]{5,4,3,2,1,0:T(8,128)S(1)}, f32[2,2,1,4,48,768]{5,4,3,2,1,0:T(8,128)S(1)}, u32[]{:S(2)}, u32[]{:S(2)}) collective-permute-start(f32[2,2,1,4,48,768]{5,4,3,2,1,0:T(8,128)S(1)} %constant_dynamic-slice_fusion.5), channel_id=1, source_target_pairs={{0,4},{4,0},{8,12},{12,8},{16,20},{20,16},{24,28},{28,24},{1,5},{5... | collective-permute-start | bytes 7077896 | tf_op jit(solution)/shard_map/ppermute | solution.py:629
  282.0 9.2 %collective-permute-start.15 = (f32[2,2,1,4,24,1536]{5,4,3,2,1,0:T(8,128)S(1)}, f32[2,2,1,4,24,1536]{5,4,3,2,1,0:T(8,128)S(1)}, u32[]{:S(2)}, u32[]{:S(2)}) collective-permute-start(f32[2,2,1,4,24,1536]{5,4,3,2,1,0:T(8,128)S(1)} %constant_dynamic-slice_fusion.3), channel_id=1, source_target_pairs={{0,4},{4,0},{8,12},{12,8},{16,20},{20,16},{24,28},{28,24},{1,5},{5... | collective-permute-start | bytes 7077896 | tf_op jit(solution)/shard_map/ppermute | solution.py:629
  293.8 57.6 %all-to-all-start.1 = ((bf16[4,4,24,4992]{3,2,1,0:T(8,128)(2,1)}), bf16[4,4,24,4992]{3,2,1,0:T(8,128)(2,1)}, u32[]{:S(2)}, u32[]{:S(2)}) async-start(bf16[4,4,24,4992]{3,2,1,0:T(8,128)(2,1)} %bitcast.180), calls=%async_computation.1 | async-start | bytes 7667712 | tf_op jit(solution)/shard_map/all_to_all | solution.py:665
  366.8 11.9 %collective-permute-start.16 = (f32[2,2,1,4,24,1920]{5,4,3,2,1,0:T(8,128)}, f32[2,2,1,4,24,1920]{5,4,3,2,1,0:T(8,128)}, u32[]{:S(2)}, u32[]{:S(2)}) collective-permute-start(f32[2,2,1,4,24,1920]{5,4,3,2,1,0:T(8,128)} %constant_dynamic-slice_fusion.2), channel_id=1, source_target_pairs={{0,4},{4,0},{8,12},{12,8},{16,20},{20,16},{24,28},{28,24},{1,5},{5... | collective-permute-start | bytes 8847368 | tf_op jit(solution)/shard_map/ppermute | solution.py:629
  370.9 7.9 %collective-permute-start.17 = (f32[2,2,1,4,24,1536]{5,4,3,2,1,0:T(8,128)}, f32[2,2,1,4,24,1536]{5,4,3,2,1,0:T(8,128)}, u32[]{:S(2)}, u32[]{:S(2)}) collective-permute-start(f32[2,2,1,4,24,1536]{5,4,3,2,1,0:T(8,128)} %constant_dynamic-slice_fusion.1), channel_id=1, source_target_pairs={{0,4},{4,0},{8,12},{12,8},{16,20},{20,16},{24,28},{28,24},{1,5},{5... | collective-permute-start | bytes 7077896 | tf_op jit(solution)/shard_map/ppermute | solution.py:629
  387.6 12.4 %collective-permute-start.18 = (bf16[24,6528]{1,0:T(8,128)(2,1)}, bf16[24,6528]{1,0:T(8,128)(2,1)}, u32[]{:S(2)}, u32[]{:S(2)}) collective-permute-start(bf16[24,6528]{1,0:T(8,128)(2,1)} %get-tuple-element.336), channel_id=1, source_target_pairs={{0,1},{1,2},{2,3},{3,0},{4,5},{5,6},{6,7},{7,4},{8,9},{9,10},{10,1... | collective-permute-start | bytes 940040 | tf_op jit(solution)/shard_map/ppermute | solution.py:623
  390.8 35.2 %all-to-all-start.2 = ((bf16[4,4,24,3456]{3,2,1,0:T(8,128)(2,1)}), bf16[4,4,24,3456]{3,2,1,0:T(8,128)(2,1)S(1)}, u32[]{:S(2)}, u32[]{:S(2)}) async-start(bf16[4,4,24,3456]{3,2,1,0:T(8,128)(2,1)} %bitcast.56), calls=%async_computation.2 | async-start | bytes 5308416 | tf_op jit(solution)/shard_map/all_to_all | solution.py:665
  395.0 18.8 %collective-permute-start.20 = (bf16[24,6528]{1,0:T(8,128)(2,1)}, bf16[24,6528]{1,0:T(8,128)(2,1)}, u32[]{:S(2)}, u32[]{:S(2)}) collective-permute-start(bf16[24,6528]{1,0:T(8,128)(2,1)} %get-tuple-element.334), channel_id=1, source_target_pairs={{0,2},{1,3},{2,0},{3,1},{4,6},{5,7},{6,4},{7,5},{8,10},{9,11},{10,... | collective-permute-start | bytes 940040 | tf_op jit(solution)/shard_map/ppermute | solution.py:623
  395.0 18.9 %collective-permute-start.21 = (bf16[24,6528]{1,0:T(8,128)(2,1)}, bf16[24,6528]{1,0:T(8,128)(2,1)}, u32[]{:S(2)}, u32[]{:S(2)}) collective-permute-start(bf16[24,6528]{1,0:T(8,128)(2,1)} %get-tuple-element.335), channel_id=1, source_target_pairs={{0,3},{1,0},{2,1},{3,2},{4,7},{5,4},{6,5},{7,6},{8,11},{9,8},{10,9... | collective-permute-start | bytes 940040 | tf_op jit(solution)/shard_map/ppermute | solution.py:623
  427.4 8.3 %collective-permute-start.27 = (f32[178,128]{1,0:T(8,128)S(1)}, f32[178,128]{1,0:T(8,128)}, u32[]{:S(2)}, u32[]{:S(2)}) collective-permute-start(f32[178,128]{1,0:T(8,128)S(1)} %add.252), channel_id=1, source_target_pairs={{0,24},{4,28},{8,16},{12,20},{16,8},{20,12},{24,0},{28,4},{1,25},{... | collective-permute-start | bytes 273416 | tf_op jit(solution)/shard_map/ppermute | solution.py:656
  428.8 6.9 %collective-permute-start.26 = (f32[178,128]{1,0:T(8,128)S(1)}, f32[178,128]{1,0:T(8,128)}, u32[]{:S(2)}, u32[]{:S(2)}) collective-permute-start(f32[178,128]{1,0:T(8,128)S(1)} %add.252), channel_id=1, source_target_pairs={{0,16},{4,20},{8,24},{12,28},{16,0},{20,4},{24,8},{28,12},{1,17},{... | collective-permute-start | bytes 273416 | tf_op jit(solution)/shard_map/ppermute | solution.py:656
  431.7 9.1 %collective-permute-start.22 = (bf16[24,3456]{1,0:T(8,128)(2,1)S(1)}, bf16[24,3456]{1,0:T(8,128)(2,1)S(1)}, u32[]{:S(2)}, u32[]{:S(2)}) collective-permute-start(bf16[24,3456]{1,0:T(8,128)(2,1)S(1)} %get-tuple-element.331), channel_id=1, source_target_pairs={{0,1},{1,2},{2,3},{3,0},{4,5},{5,6},{6,7},{7,4},{8,9},{9,10},{10,1... | collective-permute-start | bytes 497672 | tf_op jit(solution)/shard_map/ppermute | solution.py:623
  432.0 8.8 %collective-permute-start.24 = (bf16[24,3456]{1,0:T(8,128)(2,1)S(1)}, bf16[24,3456]{1,0:T(8,128)(2,1)S(1)}, u32[]{:S(2)}, u32[]{:S(2)}) collective-permute-start(bf16[24,3456]{1,0:T(8,128)(2,1)S(1)} %get-tuple-element.332), channel_id=1, source_target_pairs={{0,3},{1,0},{2,1},{3,2},{4,7},{5,4},{6,5},{7,6},{8,11},{9,8},{10,9... | collective-permute-start | bytes 497672 | tf_op jit(solution)/shard_map/ppermute | solution.py:623
  435.7 11.5 %collective-permute-start.23 = (bf16[24,3456]{1,0:T(8,128)(2,1)S(1)}, bf16[24,3456]{1,0:T(8,128)(2,1)S(1)}, u32[]{:S(2)}, u32[]{:S(2)}) collective-permute-start(bf16[24,3456]{1,0:T(8,128)(2,1)S(1)} %get-tuple-element.333), channel_id=1, source_target_pairs={{0,2},{1,3},{2,0},{3,1},{4,6},{5,7},{6,4},{7,5},{8,10},{9,11},{10,... | collective-permute-start | bytes 497672 | tf_op jit(solution)/shard_map/ppermute | solution.py:623
  448.5 8.1 %collective-permute-start.29 = (f32[178,128]{1,0:T(8,128)S(1)}, f32[178,128]{1,0:T(8,128)}, u32[]{:S(2)}, u32[]{:S(2)}) collective-permute-start(f32[178,128]{1,0:T(8,128)S(1)} %add_add_fusion.1), channel_id=1, source_target_pairs={{0,2},{1,3},{2,0},{3,1},{4,6},{5,7},{6,4},{7,5},{8,10},{9,11},{10,... | collective-permute-start | bytes 273416 | tf_op jit(solution)/shard_map/ppermute | solution.py:623
  448.5 8.1 %collective-permute-start.28 = (f32[178,128]{1,0:T(8,128)S(1)}, f32[178,128]{1,0:T(8,128)}, u32[]{:S(2)}, u32[]{:S(2)}) collective-permute-start(f32[178,128]{1,0:T(8,128)S(1)} %add_add_fusion.1), channel_id=1, source_target_pairs={{0,1},{1,2},{2,3},{3,0},{4,5},{5,6},{6,7},{7,4},{8,9},{9,10},{10,1... | collective-permute-start | bytes 273416 | tf_op jit(solution)/shard_map/ppermute | solution.py:623
  468.5 7.1 %collective-permute-start.36 = (f32[130,128]{1,0:T(8,128)S(1)}, f32[130,128]{1,0:T(8,128)S(1)}, u32[]{:S(2)}, u32[]{:S(2)}) collective-permute-start(f32[130,128]{1,0:T(8,128)S(1)} %add_add_fusion.3), channel_id=1, source_target_pairs={{0,2},{1,3},{2,0},{3,1},{4,6},{5,7},{6,4},{7,5},{8,10},{9,11},{10,... | collective-permute-start | bytes 199688 | tf_op jit(solution)/shard_map/ppermute | solution.py:623
  468.7 6.9 %collective-permute-start.35 = (f32[130,128]{1,0:T(8,128)S(1)}, f32[130,128]{1,0:T(8,128)S(1)}, u32[]{:S(2)}, u32[]{:S(2)}) collective-permute-start(f32[130,128]{1,0:T(8,128)S(1)} %add_add_fusion.3), channel_id=1, source_target_pairs={{0,1},{1,2},{2,3},{3,0},{4,5},{5,6},{6,7},{7,4},{8,9},{9,10},{10,1... | collective-permute-start | bytes 199688 | tf_op jit(solution)/shard_map/ppermute | solution.py:623
  (83 other events, 757.2 us)
Sparse Core Ops, SparseCore 0:
  11.4 102.1 all-gather.1

commit v5 on v4

--- a/solution.py
+++ b/solution.py
@@ -29,7 +29,7 @@
 GROUP = 256
 GATE_ROWS = 64
 GATE_BLOCK = 256
-NORM_BLOCK = 256
+NORM_BLOCK = 512
 GROUPS = INNER // GROUP
 LANES = 128
 LOG2E = 1.4426950408889634
@@ -307,17 +307,17 @@
     else:
         dy_ref, *refs = refs
     (
-        rgrad_in, dcv_in, dxr_ref, dpar_ref, dskip_ref, dhw_ref, rgrad, dcv_out,
+        dxr_ref, dpar_ref, dskip_ref, dhw_ref, rgrad, dcv_out,
         buf, act, slope, dact, dcv, dgram,
-    ) = refs[-14:]
+    ) = refs[-12:]
     step = pl.program_id(0)
     block = top - step
     base = block * SPAN
 
     @pl.when(step == 0)
     def _():
-        dcv[0:8, :] = dcv_in[...]
-        rgrad[...] = rgrad_in[...]
+        dcv[0:8, :] = jnp.zeros((8, CH), F32)
+        rgrad[...] = jnp.zeros_like(rgrad)
         dpar_ref[...] = jnp.zeros_like(dpar_ref)
         dskip_ref[...] = jnp.zeros_like(dskip_ref)
         dhw_ref[...] = jnp.zeros_like(dhw_ref)
@@ -486,16 +486,12 @@
     )(ends, xr, par, gain, hw, spread, *more)
 
 
-def mixer_backward(ends, xr, ys, st, par, gain, hw, spread, gather, grads, first, last, earlier=None):
+def mixer_backward(ends, xr, ys, st, par, gain, hw, spread, gather, grads, first, last):
     tokens = xr.shape[0]
     top = last - 1
     fused = len(grads) == 2
     back = lambda width: pl.BlockSpec((SPAN, width), lambda i: (top - i, 0))
     halo = pl.BlockSpec((8, XR), lambda i: (jnp.maximum((top - i) * (SPAN // 8) - 1, 0), 0))
-    if earlier is None:
-        held, carried = [], [jnp.zeros((STATE, INNER), F32), jnp.zeros((8, CH), F32)]
-    else:
-        held, carried = list(earlier[:1]), list(earlier[4:6])
     in_specs = [
         SMEM,
         back(XR),
@@ -509,9 +505,6 @@
         whole((INNER, LANES)),
     ]
     in_specs += [back(INNER)] * len(grads)
-    held_at = len(in_specs)
-    in_specs += [pl.BlockSpec(memory_space=pl.ANY)] * len(held)
-    in_specs += [whole((STATE, INNER)), whole((8, CH))]
     outs = [
         (back(XR), (tokens, XR), BF16),
         (whole((40, CH)), (40, CH), F32),
@@ -543,14 +536,13 @@
         in_specs=in_specs,
         out_specs=[o[0] for o in outs],
         out_shape=[jax.ShapeDtypeStruct(o[1], o[2]) for o in outs],
-        input_output_aliases={held_at + k: k for k in range(len(held))},
         scratch_shapes=scratch,
         compiler_params=pltpu.CompilerParams(vmem_limit_bytes=VMEM_LIMIT),
         cost_estimate=pl.CostEstimate(
             flops=7_000_000_000 * (last - first), bytes_accessed=5_000_000 * (last - first), transcendentals=0
         ),
         name="mixer_backward",
-    )(ends, xr, xr, ys, st, par, gain, hw, spread, gather, *grads, *held, *carried)
+    )(ends, xr, xr, ys, st, par, gain, hw, spread, gather, *grads)
 
 
 def norm_back_kernel(dz_ref, dxr_ref, wz_ref, wx_ref, h_ref, flow_ref, gain_ref, out_ref, dgain_ref, *low_ref):

time: 492 us -> 492 us (level)
  transfers between devices with their start and end apart: 42 -> 42, of which waited for: 16 -> 16; matrix products, arithmetic and copies ran while one was open for 14% -> 13% of each run, Pallas kernels for 30% -> 30%
where the time goes in v5:
time: 492 us; the launch traced here: 487 us
  Pallas kernels  189 us (38%)
  matrix products  73 us (15%)
  waiting for transfers between devices  67.1 us (14%)
  starting transfers between devices  54.4 us (11%)
  other arithmetic  48.7 us (10%)
  local copies, waits for them, and re-layouts  35.9 us (7%)
  between operations  18.6 us (4%)
    pallas_call x2, Pallas kernels, mixer_backward(): pl.pallas_call(kernel, grid=(last - first,), in_specs=in_specs, out_specs...  105 us
    pallas_call x2, Pallas kernels, mixer_forward(): pl.pallas_call(partial(forward_kernel, z is not None), grid=(blocks,), in...  57.3 us
    dot_general x6, matrix products, product(): return jnp.einsum('td,tp->dp', a, b, preferred_element_type=F32)  29.7 us
    ppermute x18, waiting for transfers between devices, shift(): return lax.ppermute(value, 'fsdp', [(i, (i + by) % n) for i in range(n)])  27.6 us
    ppermute x18, starting transfers between devices, shift(): return lax.ppermute(value, 'fsdp', [(i, (i + by) % n) for i in range(n)])  26.7 us
    pallas_call x2, Pallas kernels, norm_backward(): pl.pallas_call(norm_back_kernel, grid=(tokens // NORM_BLOCK,), in_specs=[...  26.5 us
    ppermute x14, waiting for transfers between devices, shift(): return lax.ppermute(value, 'dp', pairs)  26.4 us
    unnamed x152, local copies, waits for them, and re-layouts  14.6 us
  transfers between devices with their start and end apart: 42, of which 16 were waited for; matrix products, arithmetic and copies ran while one was open for 13% of the time, Pallas kernels for 30%

profile of v5, /device:TPU:0, one launch (start us, length us, event | category | flops | bytes accessed | tf_op | source)
XLA Modules:
  0.0 486.5 jit_solution(8374095925050750538)
XLA Ops:
  28.4 3.9 collective-permute-done.1
  32.3 3.7 collective-permute-done
  39.1 11.3 %collective-permute-done.3 = bf16[1,1,1,4,24,2048]{5,4,3,2,1,0:T(8,128)(2,1)S(1)} collective-permute-done((bf16[1,1,1,4,24,2048]{5,4,3,2,1,0:T(8,128)(2,1)S(1)}, bf16[1,1,1,4,24,2048]{5,4,3,2,1,0:T(8,128)(2,1)S(1)}, u32[]{:S(2)}, u32[]{:S(2)}) %collective-permute-start.3) | collective-permute-done | bytes 393248 | tf_op jit(solution)/shard_map/ppermute | solution.py:621
  56.3 11.6 %collective-permute-done.10 = bf16[2,1,1,4,24,1536]{5,4,3,2,1,0:T(8,128)(2,1)S(1)} collective-permute-done((bf16[2,1,1,4,24,1536]{5,4,3,2,1,0:T(8,128)(2,1)}, bf16[2,1,1,4,24,1536]{5,4,3,2,1,0:T(8,128)(2,1)S(1)}, u32[]{:S(2)}, u32[]{:S(2)}) %collective-permute-start.10) | collective-permute-done | bytes 589856 | tf_op jit(solution)/shard_map/ppermute | solution.py:621
  80.7 6.6 %fusion.50.refs_0_.refs_10_ = f32[1024,1536]{1,0:T(8,128)} fusion(bf16[768,1536]{1,0:T(8,128)(2,1)} %bitcast.184, bf16[1024,768]{1,0:T(8,128)(2,1)S(1)} %copy-done, f32[768]{0:T(1024)S(1)} %get-tuple-element.288, f32[1024]{0:T(1024)S(1)} %add_rsqrt_fusion.1), kind=kOutput, calls=%fused_computation.204 | convolution fusion | flops 2419064832 | bytes 10230784 | tf_op jit(solution)/shard_map/dot_general | solution.py:757
  87.4 5.7 %fusion.5.xr_ref.refs_1_.refs_2_ = f32[1024,1920]{1,0:T(8,128)} fusion(bf16[768,2048]{1,0:T(8,128)(2,1)S(1)} %bitcast.183, bf16[1024,768]{1,0:T(8,128)(2,1)S(1)} %copy-done, f32[768]{0:T(1024)S(1)} %get-tuple-element.288, f32[1024]{0:T(1024)S(1)} %add_rsqrt_fusion.1), kind=kOutput, calls=%fused_computation.16 | convolution fusion | flops 3023044608 | bytes 12394496 | tf_op jit(solution)/shard_map/dot_general | solution.py:758
  93.1 28.4 %mixer_forward.2 = (bf16[1024,1536]{1,0:T(8,128)(2,1)}, f32[1024,1536]{1,0:T(8,128)}, f32[8,128,1536]{2,1,0:T(8,128)}) custom-call(s32[4]{0:T(128)} %pad_add_fusion.ends_ref.refs_0_, f32[1024,1920]{1,0:T(8,128)} %fusion.5.xr_ref.refs_1_.refs_2_, f32[8,1792]{1,0:T(8,128)} %concatenate.111.par_ref.refs_5_, f32[8,1536]{1,0:T(8,128)} %get-tuple-element.377.gain_ref.refs_6_, ...), custom_call_target="tpu_custom_call" | custom-call | flops 30000001024 | bytes 30000000 | tf_op jit(solution)/shard_map/mixer_forward/pallas_call | solution.py:476
  121.5 3.8 fusion.62
  131.4 4.5 fusion.7.refs_0_.refs_10_
  135.9 5.5 %fusion.3.xr_ref.refs_1_.refs_2_ = f32[1024,1920]{1,0:T(8,128)} fusion(bf16[1024,768]{1,0:T(8,128)(2,1)S(1)} %multiply_convert_fusion, bf16[768,6912]{1,0:T(8,128)(2,1)S(1)} %bitcast.173), kind=kOutput, calls=%fused_computation.14 | convolution fusion | flops 3019898880 | bytes 12386304 | tf_op jit(solution)/shard_map/dot_general | solution.py:758
  141.4 28.9 %mixer_forward.3 = (bf16[1024,1536]{1,0:T(8,128)(2,1)}, f32[1024,1536]{1,0:T(8,128)}, f32[8,128,1536]{2,1,0:T(8,128)}) custom-call(s32[4]{0:T(128)} %pad_add_fusion.ends_ref.refs_0_, f32[1024,1920]{1,0:T(8,128)} %fusion.3.xr_ref.refs_1_.refs_2_, f32[8,1792]{1,0:T(8,128)} %concatenate.119.par_ref.refs_5_, f32[8,1536]{1,0:T(8,128)} %get-tuple-element.376.gain_ref.refs_6_, ...), custom_call_target="tpu_custom_call" | custom-call | flops 30000001024 | bytes 30000000 | tf_op jit(solution)/shard_map/mixer_forward/pallas_call | solution.py:476
  170.3 4.6 fusion.68
  178.1 6.9 %fusion.69.refs_11_ = f32[1024,1536]{1,0:T(8,128)} fusion(bf16[1024,768]{1,0:T(8,128)(2,1)} %get-tuple-element.115, bf16[1536,768]{1,0:T(8,128)(2,1)S(1)} %bitcast.199), kind=kOutput, calls=%fused_computation.218 | convolution fusion | flops 2415919104 | bytes 10223616 | tf_op jit(solution)/shard_map/td,ed->te/dot_general | solution.py:780
  188.9 4.1 all-to-all-start
  193.0 52.6 %mixer_backward.2 = (bf16[1024,1920]{1,0:T(8,128)(2,1)}, f32[40,1792]{1,0:T(8,128)}, f32[8,1536]{1,0:T(8,128)}, f32[16,128]{1,0:T(8,128)}, f32[128,1536]{1,0:T(8...) custom-call(s32[4]{0:T(128)} %pad_add_fusion.ends_ref.refs_0_, ...), custom_call_target="tpu_custom_call" | custom-call | flops 56000000000 | bytes 40000000 | tf_op jit(solution)/shard_map/mixer_backward/pallas_call | solution.py:533
  246.5 7.3 %fusion.71 = f32[768,1536]{1,0:T(8,128)} fusion(bf16[1024,768]{1,0:T(8,128)(2,1)} %copy-done.10, bf16[1024,1536]{1,0:T(8,128)(2,1)} %get-tuple-element.130.dz_ref), kind=kOutput, calls=%fused_computation.220 | convolution fusion | flops 2415919104 | bytes 9437184 | tf_op jit(solution)/shard_map/td,tp->dp/dot_general | solution.py:771
  253.8 5.3 %fusion.70 = f32[768,1920]{1,0:T(8,128)} fusion(bf16[1024,768]{1,0:T(8,128)(2,1)S(1)} %copy-done.11, bf16[1024,1920]{1,0:T(8,128)(2,1)S(1)} %copy-done.18), kind=kOutput, calls=%fused_computation.219 | convolution fusion | flops 3019898880 | bytes 11403264 | tf_op jit(solution)/shard_map/td,tp->dp/dot_general | solution.py:771
  259.7 13.7 %norm_backward.2 = (f32[1024,768]{1,0:T(8,128)}, f32[8,768]{1,0:T(8,128)}, bf16[1024,768]{1,0:T(8,128)(2,1)}) custom-call(bf16[1024,1536]{1,0:T(8,128)(2,1)} %get-tuple-element.130.dz_ref, bf16[1024,1920]{1,0:T(8,128)(2,1)} %get-tuple-element.131.dxr_ref, bf16[768,6912]{1,0:T(8,128)(2,1)} %all-gather.2.cloned.1.call-done.wz_ref.wx_ref, ...), custom_call_target="tpu_custom_call" | custom-call | flops 1000000 | bytes 1000000 | tf_op jit(solution)/shard_map/norm_backward/pallas_call | solution.py:568
  273.4 4.2 fusion.72
  282.8 4.6 fusion.73.refs_11_
  292.7 5.0 %all-to-all-start.1 = ((bf16[4,4,24,4992]{3,2,1,0:T(8,128)(2,1)}), bf16[4,4,24,4992]{3,2,1,0:T(8,128)(2,1)}, u32[]{:S(2)}, u32[]{:S(2)}) async-start(bf16[4,4,24,4992]{3,2,1,0:T(8,128)(2,1)} %bitcast.180), calls=%async_computation.1 | async-start | bytes 7667712 | tf_op jit(solution)/shard_map/all_to_all | solution.py:657
  297.7 52.6 %mixer_backward.3 = (bf16[1024,1920]{1,0:T(8,128)(2,1)}, f32[40,1792]{1,0:T(8,128)}, f32[8,1536]{1,0:T(8,128)}, f32[16,128]{1,0:T(8,128)}, f32[128,1536]{1,0:T(8...) custom-call(s32[4]{0:T(128)} %pad_add_fusion.ends_ref.refs_0_, ...), custom_call_target="tpu_custom_call" | custom-call | flops 56000000000 | bytes 40000000 | tf_op jit(solution)/shard_map/mixer_backward/pallas_call | solution.py:533
  353.8 4.7 fusion.46
  358.5 3.6 fusion.48
  369.9 6.5 %add_convert_fusion = bf16[1024,768]{1,0:T(8,128)(2,1)} fusion(f32[1024,768]{1,0:T(8,128)S(1)} %copy-done.8, bf16[1024,1536]{1,0:T(8,128)(2,1)} %get-tuple-element.114, bf16[1536,768]{1,0:T(8,128)(2,1)} %bitcast.200), kind=kOutput, calls=%fused_computation.10 | convolution fusion | flops 2417491968 | bytes 10223616 | tf_op jit(solution)/shard_map/dot_general | solution.py:760
  389.8 4.2 all-to-all-start.2
  399.5 12.8 %norm_backward.3 = (f32[1024,768]{1,0:T(8,128)}, f32[8,768]{1,0:T(8,128)}) custom-call(bf16[1024,1536]{1,0:T(8,128)(2,1)} %get-tuple-element.168.dz_ref, bf16[1024,1920]{1,0:T(8,128)(2,1)} %get-tuple-element.169.dxr_ref, bf16[768,1536]{1,0:T(8,128)(2,1)} %bitcast.185, bf16[768,2048]{1,0:T(8,128)(2,1)} %bitcast.182, bf16[1024,768]{1,0:T(8,128)(2,1)} %h_ref.1, ...), custom_call_target="tpu_custom_call" | custom-call | flops 1000000 | bytes 1000000 | tf_op jit(solution)/shard_map/norm_backward/pallas_call | solution.py:568
  415.6 9.3 %all-to-all-done.2 = bf16[4,4,24,3456]{3,2,1,0:T(8,128)(2,1)S(1)} async-done(((bf16[4,4,24,3456]{3,2,1,0:T(8,128)(2,1)}), bf16[4,4,24,3456]{3,2,1,0:T(8,128)(2,1)S(1)}, u32[]{:S(2)}, u32[]{:S(2)}) %all-to-all-start.2) | async-done | bytes 2654240 | tf_op jit(solution)/shard_map/all_to_all | solution.py:657
  431.0 3.8 collective-permute-start.24
  436.1 3.7 collective-permute-done.22
  439.8 6.2 %collective-permute-done.23 = bf16[24,3456]{1,0:T(8,128)(2,1)S(1)} collective-permute-done((bf16[24,3456]{1,0:T(8,128)(2,1)S(1)}, bf16[24,3456]{1,0:T(8,128)(2,1)S(1)}, u32[]{:S(2)}, u32[]{:S(2)}) %collective-permute-start.23) | collective-permute-done | bytes 165920 | tf_op jit(solution)/shard_map/ppermute | solution.py:615
  451.2 4.3 collective-permute-done.29
  (393 shorter events, 134.0 us)
Async XLA Ops:
  7.2 114.3 %all-gather.2.cloned.1.call-start = ((), (), s32[]{:S(2)}) async-start(), calls=%async_computation.3 | async-start | bytes 10948608 | tf_op jit(solution)/shard_map/all_gather | solution.py:738
  10.4 13.5 %collective-permute-start.8 = (bf16[1,1,1,1,24,1536]{5,4,3,2,1,0:T(8,128)(2,1)S(1)}, bf16[1,1,1,1,24,1536]{5,4,3,2,1,0:T(8,128)(2,1)S(1)}, u32[]{:S(2)}, u32[]{:S(2)}) collective-permute-start(bf16[1,1,1,1,24,1536]{5,4,3,2,1,0:T(8,128)(2,1)S(1)} %slice_bitcast_fusion.1), channel_id=1, source_target_pairs={{0,1},{1,2},{2,3},{3,0},{4,5},{5,6},{6,7},{7,4},{8,9},{9,10},{10,1... | collective-permute-start | bytes 221192 | tf_op jit(solution)/shard_map/ppermute | solution.py:615
  13.5 13.2 %collective-permute-start.7 = (bf16[1,1,1,1,24,1536]{5,4,3,2,1,0:T(8,128)(2,1)S(1)}, bf16[1,1,1,1,24,1536]{5,4,3,2,1,0:T(8,128)(2,1)S(1)}, u32[]{:S(2)}, u32[]{:S(2)}) collective-permute-start(bf16[1,1,1,1,24,1536]{5,4,3,2,1,0:T(8,128)(2,1)S(1)} %slice_bitcast_fusion.1), channel_id=1, source_target_pairs={{0,2},{1,3},{2,0},{3,1},{4,6},{5,7},{6,4},{7,5},{8,10},{9,11},{10,... | collective-permute-start | bytes 221192 | tf_op jit(solution)/shard_map/ppermute | solution.py:615
  16.0 10.7 %collective-permute-start.6 = (bf16[1,1,1,1,24,1536]{5,4,3,2,1,0:T(8,128)(2,1)S(1)}, bf16[1,1,1,1,24,1536]{5,4,3,2,1,0:T(8,128)(2,1)S(1)}, u32[]{:S(2)}, u32[]{:S(2)}) collective-permute-start(bf16[1,1,1,1,24,1536]{5,4,3,2,1,0:T(8,128)(2,1)S(1)} %slice_bitcast_fusion.1), channel_id=1, source_target_pairs={{0,3},{1,0},{2,1},{3,2},{4,7},{5,4},{6,5},{7,6},{8,11},{9,8},{10,9... | collective-permute-start | bytes 221192 | tf_op jit(solution)/shard_map/ppermute | solution.py:615
  17.5 10.9 %collective-permute-start.2 = (bf16[1,1,1,1,24,2048]{5,4,3,2,1,0:T(8,128)(2,1)S(1)}, bf16[1,1,1,1,24,2048]{5,4,3,2,1,0:T(8,128)(2,1)S(1)}, u32[]{:S(2)}, u32[]{:S(2)}) collective-permute-start(bf16[1,1,1,1,24,2048]{5,4,3,2,1,0:T(8,128)(2,1)S(1)} %maximum_bitcast_fusion.4), channel_id=1, source_target_pairs={{0,1},{1,2},{2,3},{3,0},{4,5},{5,6},{6,7},{7,4},{8,9},{9,10},{10,1... | collective-permute-start | bytes 294920 | tf_op jit(solution)/shard_map/ppermute | solution.py:615
  18.3 14.0 %collective-permute-start.1 = (bf16[1,1,1,1,24,2048]{5,4,3,2,1,0:T(8,128)(2,1)S(1)}, bf16[1,1,1,1,24,2048]{5,4,3,2,1,0:T(8,128)(2,1)S(1)}, u32[]{:S(2)}, u32[]{:S(2)}) collective-permute-start(bf16[1,1,1,1,24,2048]{5,4,3,2,1,0:T(8,128)(2,1)S(1)} %maximum_bitcast_fusion.4), channel_id=1, source_target_pairs={{0,2},{1,3},{2,0},{3,1},{4,6},{5,7},{6,4},{7,5},{8,10},{9,11},{10,... | collective-permute-start | bytes 294920 | tf_op jit(solution)/shard_map/ppermute | solution.py:615
  23.9 12.0 %collective-permute-start = (bf16[1,1,1,1,24,2048]{5,4,3,2,1,0:T(8,128)(2,1)S(1)}, bf16[1,1,1,1,24,2048]{5,4,3,2,1,0:T(8,128)(2,1)S(1)}, u32[]{:S(2)}, u32[]{:S(2)}) collective-permute-start(bf16[1,1,1,1,24,2048]{5,4,3,2,1,0:T(8,128)(2,1)S(1)} %maximum_bitcast_fusion.4), channel_id=1, source_target_pairs={{0,3},{1,0},{2,1},{3,2},{4,7},{5,4},{6,5},{7,6},{8,11},{9,8},{10,9... | collective-permute-start | bytes 294920 | tf_op jit(solution)/shard_map/ppermute | solution.py:615
  26.8 10.8 %collective-permute-start.9 = (bf16[1,1,1,4,24,1536]{5,4,3,2,1,0:T(8,128)(2,1)S(1)}, bf16[1,1,1,4,24,1536]{5,4,3,2,1,0:T(8,128)(2,1)S(1)}, u32[]{:S(2)}, u32[]{:S(2)}) collective-permute-start(bf16[1,1,1,4,24,1536]{5,4,3,2,1,0:T(8,128)(2,1)S(1)} %pad_maximum_fusion.14), channel_id=1, source_target_pairs={{0,16},{4,20},{8,24},{12,28},{16,0},{20,4},{24,8},{28,12},{1,17},{... | collective-permute-start | bytes 884744 | tf_op jit(solution)/shard_map/ppermute | solution.py:621
  36.1 14.4 %collective-permute-start.3 = (bf16[1,1,1,4,24,2048]{5,4,3,2,1,0:T(8,128)(2,1)S(1)}, bf16[1,1,1,4,24,2048]{5,4,3,2,1,0:T(8,128)(2,1)S(1)}, u32[]{:S(2)}, u32[]{:S(2)}) collective-permute-start(bf16[1,1,1,4,24,2048]{5,4,3,2,1,0:T(8,128)(2,1)S(1)} %pad_maximum_fusion.13), channel_id=1, source_target_pairs={{0,8},{4,12},{8,0},{12,4},{16,24},{20,28},{24,16},{28,20},{1,9},{5... | collective-permute-start | bytes 1179656 | tf_op jit(solution)/shard_map/ppermute | solution.py:621
  38.5 29.3 %collective-permute-start.10 = (bf16[2,1,1,4,24,1536]{5,4,3,2,1,0:T(8,128)(2,1)}, bf16[2,1,1,4,24,1536]{5,4,3,2,1,0:T(8,128)(2,1)S(1)}, u32[]{:S(2)}, u32[]{:S(2)}) collective-permute-start(bf16[2,1,1,4,24,1536]{5,4,3,2,1,0:T(8,128)(2,1)} %pad_maximum_fusion.12), channel_id=1, source_target_pairs={{0,8},{4,12},{8,0},{12,4},{16,24},{20,28},{24,16},{28,20},{1,9},{5... | collective-permute-start | bytes 1769480 | tf_op jit(solution)/shard_map/ppermute | solution.py:621
  51.5 16.6 %collective-permute-start.4 = (bf16[1,2,1,4,24,2048]{5,4,3,2,1,0:T(8,128)(2,1)}, bf16[1,2,1,4,24,2048]{5,4,3,2,1,0:T(8,128)(2,1)}, u32[]{:S(2)}, u32[]{:S(2)}) collective-permute-start(bf16[1,2,1,4,24,2048]{5,4,3,2,1,0:T(8,128)(2,1)} %pad_maximum_fusion.10), channel_id=1, source_target_pairs={{0,16},{4,20},{8,24},{12,28},{16,0},{20,4},{24,8},{28,12},{1,17},{... | collective-permute-start | bytes 2359304 | tf_op jit(solution)/shard_map/ppermute | solution.py:621
  177.7 7.3 %collective-permute-start.12 = (f32[2,2,1,4,48,768]{5,4,3,2,1,0:T(8,128)}, f32[2,2,1,4,48,768]{5,4,3,2,1,0:T(8,128)}, u32[]{:S(2)}, u32[]{:S(2)}) collective-permute-start(f32[2,2,1,4,48,768]{5,4,3,2,1,0:T(8,128)} %constant_dynamic-slice_fusion.6), channel_id=1, source_target_pairs={{0,4},{4,0},{8,12},{12,8},{16,20},{20,16},{24,28},{28,24},{1,5},{5... | collective-permute-start | bytes 7077896 | tf_op jit(solution)/shard_map/ppermute | solution.py:621
  188.9 56.7 %all-to-all-start = ((f32[4,4,24,1536]{3,2,1,0:T(8,128)}), f32[4,4,24,1536]{3,2,1,0:T(8,128)S(1)}, u32[]{:S(2)}, u32[]{:S(2)}) async-start(f32[4,4,24,1536]{3,2,1,0:T(8,128)} %bitcast.186), calls=%async_computation | async-start | bytes 4718592 | tf_op jit(solution)/shard_map/all_to_all | solution.py:657
  277.8 12.2 %collective-permute-start.14 = (f32[2,2,1,4,24,1920]{5,4,3,2,1,0:T(8,128)S(1)}, f32[2,2,1,4,24,1920]{5,4,3,2,1,0:T(8,128)S(1)}, u32[]{:S(2)}, u32[]{:S(2)}) collective-permute-start(f32[2,2,1,4,24,1920]{5,4,3,2,1,0:T(8,128)S(1)} %constant_dynamic-slice_fusion.4), channel_id=1, source_target_pairs={{0,4},{4,0},{8,12},{12,8},{16,20},{20,16},{24,28},{28,24},{1,5},{5... | collective-permute-start | bytes 8847368 | tf_op jit(solution)/shard_map/ppermute | solution.py:621
  278.5 8.8 %collective-permute-start.13 = (f32[2,2,1,4,48,768]{5,4,3,2,1,0:T(8,128)S(1)}, f32[2,2,1,4,48,768]{5,4,3,2,1,0:T(8,128)S(1)}, u32[]{:S(2)}, u32[]{:S(2)}) collective-permute-start(f32[2,2,1,4,48,768]{5,4,3,2,1,0:T(8,128)S(1)} %constant_dynamic-slice_fusion.5), channel_id=1, source_target_pairs={{0,4},{4,0},{8,12},{12,8},{16,20},{20,16},{24,28},{28,24},{1,5},{5... | collective-permute-start | bytes 7077896 | tf_op jit(solution)/shard_map/ppermute | solution.py:621
  280.9 9.2 %collective-permute-start.15 = (f32[2,2,1,4,24,1536]{5,4,3,2,1,0:T(8,128)S(1)}, f32[2,2,1,4,24,1536]{5,4,3,2,1,0:T(8,128)S(1)}, u32[]{:S(2)}, u32[]{:S(2)}) collective-permute-start(f32[2,2,1,4,24,1536]{5,4,3,2,1,0:T(8,128)S(1)} %constant_dynamic-slice_fusion.3), channel_id=1, source_target_pairs={{0,4},{4,0},{8,12},{12,8},{16,20},{20,16},{24,28},{28,24},{1,5},{5... | collective-permute-start | bytes 7077896 | tf_op jit(solution)/shard_map/ppermute | solution.py:621
  292.7 57.6 %all-to-all-start.1 = ((bf16[4,4,24,4992]{3,2,1,0:T(8,128)(2,1)}), bf16[4,4,24,4992]{3,2,1,0:T(8,128)(2,1)}, u32[]{:S(2)}, u32[]{:S(2)}) async-start(bf16[4,4,24,4992]{3,2,1,0:T(8,128)(2,1)} %bitcast.180), calls=%async_computation.1 | async-start | bytes 7667712 | tf_op jit(solution)/shard_map/all_to_all | solution.py:657
  365.7 12.0 %collective-permute-start.16 = (f32[2,2,1,4,24,1920]{5,4,3,2,1,0:T(8,128)}, f32[2,2,1,4,24,1920]{5,4,3,2,1,0:T(8,128)}, u32[]{:S(2)}, u32[]{:S(2)}) collective-permute-start(f32[2,2,1,4,24,1920]{5,4,3,2,1,0:T(8,128)} %constant_dynamic-slice_fusion.2), channel_id=1, source_target_pairs={{0,4},{4,0},{8,12},{12,8},{16,20},{20,16},{24,28},{28,24},{1,5},{5... | collective-permute-start | bytes 8847368 | tf_op jit(solution)/shard_map/ppermute | solution.py:621
  369.7 7.9 %collective-permute-start.17 = (f32[2,2,1,4,24,1536]{5,4,3,2,1,0:T(8,128)}, f32[2,2,1,4,24,1536]{5,4,3,2,1,0:T(8,128)}, u32[]{:S(2)}, u32[]{:S(2)}) collective-permute-start(f32[2,2,1,4,24,1536]{5,4,3,2,1,0:T(8,128)} %constant_dynamic-slice_fusion.1), channel_id=1, source_target_pairs={{0,4},{4,0},{8,12},{12,8},{16,20},{20,16},{24,28},{28,24},{1,5},{5... | collective-permute-start | bytes 7077896 | tf_op jit(solution)/shard_map/ppermute | solution.py:621
  386.4 12.4 %collective-permute-start.18 = (bf16[24,6528]{1,0:T(8,128)(2,1)}, bf16[24,6528]{1,0:T(8,128)(2,1)}, u32[]{:S(2)}, u32[]{:S(2)}) collective-permute-start(bf16[24,6528]{1,0:T(8,128)(2,1)} %get-tuple-element.336), channel_id=1, source_target_pairs={{0,1},{1,2},{2,3},{3,0},{4,5},{5,6},{6,7},{7,4},{8,9},{9,10},{10,1... | collective-permute-start | bytes 940040 | tf_op jit(solution)/shard_map/ppermute | solution.py:615
  389.8 35.2 %all-to-all-start.2 = ((bf16[4,4,24,3456]{3,2,1,0:T(8,128)(2,1)}), bf16[4,4,24,3456]{3,2,1,0:T(8,128)(2,1)S(1)}, u32[]{:S(2)}, u32[]{:S(2)}) async-start(bf16[4,4,24,3456]{3,2,1,0:T(8,128)(2,1)} %bitcast.56), calls=%async_computation.2 | async-start | bytes 5308416 | tf_op jit(solution)/shard_map/all_to_all | solution.py:657
  394.0 19.4 %collective-permute-start.20 = (bf16[24,6528]{1,0:T(8,128)(2,1)}, bf16[24,6528]{1,0:T(8,128)(2,1)}, u32[]{:S(2)}, u32[]{:S(2)}) collective-permute-start(bf16[24,6528]{1,0:T(8,128)(2,1)} %get-tuple-element.334), channel_id=1, source_target_pairs={{0,2},{1,3},{2,0},{3,1},{4,6},{5,7},{6,4},{7,5},{8,10},{9,11},{10,... | collective-permute-start | bytes 940040 | tf_op jit(solution)/shard_map/ppermute | solution.py:615
  394.0 19.4 %collective-permute-start.21 = (bf16[24,6528]{1,0:T(8,128)(2,1)}, bf16[24,6528]{1,0:T(8,128)(2,1)}, u32[]{:S(2)}, u32[]{:S(2)}) collective-permute-start(bf16[24,6528]{1,0:T(8,128)(2,1)} %get-tuple-element.335), channel_id=1, source_target_pairs={{0,3},{1,0},{2,1},{3,2},{4,7},{5,4},{6,5},{7,6},{8,11},{9,8},{10,9... | collective-permute-start | bytes 940040 | tf_op jit(solution)/shard_map/ppermute | solution.py:615
  426.4 8.5 %collective-permute-start.27 = (f32[178,128]{1,0:T(8,128)S(1)}, f32[178,128]{1,0:T(8,128)}, u32[]{:S(2)}, u32[]{:S(2)}) collective-permute-start(f32[178,128]{1,0:T(8,128)S(1)} %add.252), channel_id=1, source_target_pairs={{0,24},{4,28},{8,16},{12,20},{16,8},{20,12},{24,0},{28,4},{1,25},{... | collective-permute-start | bytes 273416 | tf_op jit(solution)/shard_map/ppermute | solution.py:648
  427.9 7.2 %collective-permute-start.26 = (f32[178,128]{1,0:T(8,128)S(1)}, f32[178,128]{1,0:T(8,128)}, u32[]{:S(2)}, u32[]{:S(2)}) collective-permute-start(f32[178,128]{1,0:T(8,128)S(1)} %add.252), channel_id=1, source_target_pairs={{0,16},{4,20},{8,24},{12,28},{16,0},{20,4},{24,8},{28,12},{1,17},{... | collective-permute-start | bytes 273416 | tf_op jit(solution)/shard_map/ppermute | solution.py:648
  430.7 9.1 %collective-permute-start.22 = (bf16[24,3456]{1,0:T(8,128)(2,1)S(1)}, bf16[24,3456]{1,0:T(8,128)(2,1)S(1)}, u32[]{:S(2)}, u32[]{:S(2)}) collective-permute-start(bf16[24,3456]{1,0:T(8,128)(2,1)S(1)} %get-tuple-element.331), channel_id=1, source_target_pairs={{0,1},{1,2},{2,3},{3,0},{4,5},{5,6},{6,7},{7,4},{8,9},{9,10},{10,1... | collective-permute-start | bytes 497672 | tf_op jit(solution)/shard_map/ppermute | solution.py:615
  431.0 8.8 %collective-permute-start.24 = (bf16[24,3456]{1,0:T(8,128)(2,1)S(1)}, bf16[24,3456]{1,0:T(8,128)(2,1)S(1)}, u32[]{:S(2)}, u32[]{:S(2)}) collective-permute-start(bf16[24,3456]{1,0:T(8,128)(2,1)S(1)} %get-tuple-element.332), channel_id=1, source_target_pairs={{0,3},{1,0},{2,1},{3,2},{4,7},{5,4},{6,5},{7,6},{8,11},{9,8},{10,9... | collective-permute-start | bytes 497672 | tf_op jit(solution)/shard_map/ppermute | solution.py:615
  435.0 11.1 %collective-permute-start.23 = (bf16[24,3456]{1,0:T(8,128)(2,1)S(1)}, bf16[24,3456]{1,0:T(8,128)(2,1)S(1)}, u32[]{:S(2)}, u32[]{:S(2)}) collective-permute-start(bf16[24,3456]{1,0:T(8,128)(2,1)S(1)} %get-tuple-element.333), channel_id=1, source_target_pairs={{0,2},{1,3},{2,0},{3,1},{4,6},{5,7},{6,4},{7,5},{8,10},{9,11},{10,... | collective-permute-start | bytes 497672 | tf_op jit(solution)/shard_map/ppermute | solution.py:615
  447.5 8.0 %collective-permute-start.29 = (f32[178,128]{1,0:T(8,128)S(1)}, f32[178,128]{1,0:T(8,128)}, u32[]{:S(2)}, u32[]{:S(2)}) collective-permute-start(f32[178,128]{1,0:T(8,128)S(1)} %add_add_fusion.1), channel_id=1, source_target_pairs={{0,2},{1,3},{2,0},{3,1},{4,6},{5,7},{6,4},{7,5},{8,10},{9,11},{10,... | collective-permute-start | bytes 273416 | tf_op jit(solution)/shard_map/ppermute | solution.py:615
  447.5 8.0 %collective-permute-start.28 = (f32[178,128]{1,0:T(8,128)S(1)}, f32[178,128]{1,0:T(8,128)}, u32[]{:S(2)}, u32[]{:S(2)}) collective-permute-start(f32[178,128]{1,0:T(8,128)S(1)} %add_add_fusion.1), channel_id=1, source_target_pairs={{0,1},{1,2},{2,3},{3,0},{4,5},{5,6},{6,7},{7,4},{8,9},{9,10},{10,1... | collective-permute-start | bytes 273416 | tf_op jit(solution)/shard_map/ppermute | solution.py:615
  467.2 7.4 %collective-permute-start.36 = (f32[130,128]{1,0:T(8,128)S(1)}, f32[130,128]{1,0:T(8,128)S(1)}, u32[]{:S(2)}, u32[]{:S(2)}) collective-permute-start(f32[130,128]{1,0:T(8,128)S(1)} %add_add_fusion.3), channel_id=1, source_target_pairs={{0,2},{1,3},{2,0},{3,1},{4,6},{5,7},{6,4},{7,5},{8,10},{9,11},{10,... | collective-permute-start | bytes 199688 | tf_op jit(solution)/shard_map/ppermute | solution.py:615
  467.9 6.8 %collective-permute-start.35 = (f32[130,128]{1,0:T(8,128)S(1)}, f32[130,128]{1,0:T(8,128)S(1)}, u32[]{:S(2)}, u32[]{:S(2)}) collective-permute-start(f32[130,128]{1,0:T(8,128)S(1)} %add_add_fusion.3), channel_id=1, source_target_pairs={{0,1},{1,2},{2,3},{3,0},{4,5},{5,6},{6,7},{7,4},{8,9},{9,10},{10,1... | collective-permute-start | bytes 199688 | tf_op jit(solution)/shard_map/ppermute | solution.py:615
  (83 other events, 760.5 us)
Sparse Core Ops, SparseCore 0:
  11.4 102.1 all-gather.1
